TPU v7x, 32 devices: a whole 2x2x4 slice. The times are simulated.
32 devices in a mesh: section: 2 (over y), tensor: 4 (over z), dp: 4 (over x, core).
Axes of the slice: x: 2, y: 2, z: 4, core: 2. Of those that a mesh axis runs over, the one named last changes fastest.
Arguments:
- tokens: bfloat16 [2, 4096, 1280], P(None, 'dp'), may hold values from -6 to 6
- cotangent: bfloat16 [2, 4096, 1280], P(None, 'dp'), may hold values from -6 to 6
- seg_ids: int32 [2, 4096], P(None, 'dp'), may hold values from 0 to 448, as said below
- observed: int32 [2, 4096], P(None, 'dp'), may hold values from 0 to 1, as said below
- query_key_value_weight: bfloat16 [2, 3, 1280, 1280], P('section', None, None, 'tensor'), may hold values from -0.15625 to 0.15625
- w_out: bfloat16 [2, 1280, 1280], P('section', 'tensor'), may hold values from -0.625 to 0.625
- w_in: bfloat16 [2, 1280, 5120], P('section', None, 'tensor'), may hold values from -0.15625 to 0.15625
- w_down: bfloat16 [2, 5120, 1280], P('section', 'tensor'), may hold values from -0.125 to 0.125
- norm_gains: float32 [2, 2, 1280], P('section'), may hold values from 0.25 to 1.75
Outputs:
- layer_acts: bfloat16 [2, 2, 4096, 1280], P('section', None, 'dp')
- grad_acts: bfloat16 [2, 2, 4096, 1280], P('section', None, 'dp')
- w_qkv_grad: float32 [2, 3, 1280, 1280], P('section', None, 'dp', 'tensor')
- w_out_grad: float32 [2, 1280, 1280], P('section', 'tensor', 'dp')
- w_in_grad: float32 [2, 1280, 5120], P('section', 'dp', 'tensor')
- w_down_grad: float32 [2, 5120, 1280], P('section', 'tensor', 'dp')
- norm_gains_grad: float32 [2, 2, 1280], P('section', None, 'dp')
Inputs may be any that keep to these rules, and one draw needn't show every extreme that they name: `seg_ids`: within each aligned block of 512 positions the series numbers start at 0, rise by one at each new series and never fall; a series holds 1 to 64 positions, and the first series of every block holds exactly 64. `observed`: in every series the unobserved patches come first.
All inputs are finite; a program needn't handle non-finite values.
Results may differ from a plain program's by a relative error of at most 0.025.
Values may be sent and summed in bfloat16 or wider, within the bound.
A program may use at most 256 MiB of HBM per device.

v0:
```python
import math

import jax
import jax.numpy as jnp
from jax import lax
from jax.sharding import PartitionSpec as P

HEAD_SIZE = 80
ROW_POSITIONS = 512


EPS = 1e-06
BIG = 1000000000.0


def shifted(block, axis, distance):
    devices = range(lax.axis_size(axis))
    route = [(i - distance, i) for i in devices if i - distance in devices]
    return lax.ppermute(block, axis, route)


def matrix_product(left, right):
    return jnp.dot(left, right, preferred_element_type=jnp.float32)


def inner_rows(left, right):
    return lax.dot_general(
        left, right, (((0,), (0,)), ((), ())), preferred_element_type=jnp.float32
    )


def outer_cols(left, right):
    return lax.dot_general(
        left, right, (((1,), (1,)), ((), ())), preferred_element_type=jnp.float32
    )


def rope_tables():
    half_size = HEAD_SIZE // 2
    frequencies = 10000.0 ** (-jnp.arange(half_size, dtype=jnp.float32) / half_size)
    rotary_angles = jnp.arange(ROW_POSITIONS, dtype=jnp.float32)[:, None] * frequencies[None, :]
    return (jnp.cos(rotary_angles)[:, None, :], jnp.sin(rotary_angles)[:, None, :])


def rotate(values, cosine, sine):
    half_size = HEAD_SIZE // 2
    first_half = values[..., :half_size]
    second_half = values[..., half_size:]
    return jnp.concatenate(
        [first_half * cosine - second_half * sine, first_half * sine + second_half * cosine],
        axis=-1,
    )


def unrotate(grads, cosine, sine):
    half_size = HEAD_SIZE // 2
    first_half = grads[..., :half_size]
    second_half = grads[..., half_size:]
    return jnp.concatenate(
        [first_half * cosine + second_half * sine, second_half * cosine - first_half * sine],
        axis=-1,
    )


def masked_scores(query, key_rows, series_values, visited_count):
    scores = jnp.einsum(
        "qhd,khd->hqk", query, key_rows, preferred_element_type=jnp.float32
    ) / math.sqrt(HEAD_SIZE)
    target_slots = jnp.arange(ROW_POSITIONS, dtype=jnp.int32)
    allowed = (
        (series_values[:, None] == series_values[None, :])
        & (target_slots[None, :] <= target_slots[:, None])
        & ((visited_count[None, :] == 1) | (target_slots[None, :] == target_slots[:, None]))
    )
    return (jnp.where(allowed[None], scores, -BIG), allowed)


def attend_row(inputs):
    query, key_rows, value_rows, series_values, visited_count = inputs
    scores, allowed = masked_scores(query, key_rows, series_values, visited_count)
    highest = jnp.max(scores, axis=-1, keepdims=True)
    weights = jnp.exp(scores - highest)
    denom = jnp.sum(weights, axis=-1, keepdims=True)
    probs = (weights / denom).astype(jnp.bfloat16)
    mixed = jnp.einsum("hqk,khd->qhd", probs, value_rows, preferred_element_type=jnp.float32)
    return (mixed, (highest + jnp.log(denom))[..., 0])


def attend_row_back(inputs):
    query, key_rows, value_rows, series_values, visited_count, grad_mixed, logsum = inputs
    scores, allowed = masked_scores(query, key_rows, series_values, visited_count)
    probs = jnp.where(allowed[None], jnp.exp(scores - logsum[..., None]), 0.0)
    rounded = probs.astype(jnp.bfloat16)
    grad_values = jnp.einsum(
        "hqk,qhd->khd", rounded, grad_mixed, preferred_element_type=jnp.float32
    )
    grad_probs = jnp.einsum(
        "qhd,khd->hqk", grad_mixed, value_rows, preferred_element_type=jnp.float32
    )
    offset_sum = jnp.sum(probs * grad_probs, axis=-1, keepdims=True)
    grad_scores = (probs * (grad_probs - offset_sum)).astype(jnp.bfloat16)
    factor = 1.0 / math.sqrt(HEAD_SIZE)
    grad_query = (
        jnp.einsum("hqk,khd->qhd", grad_scores, key_rows, preferred_element_type=jnp.float32)
        * factor
    )
    grad_keys = (
        jnp.einsum("hqk,qhd->khd", grad_scores, query, preferred_element_type=jnp.float32) * factor
    )
    return (grad_query, grad_keys, grad_values.astype(jnp.bfloat16))


def partial_total(term):
    return lax.psum(term.astype(jnp.bfloat16), "tensor").astype(jnp.float32)


def partial_back(term):
    return lax.psum(term.astype(jnp.bfloat16), "tensor").astype(jnp.float32)


def layer_forward(layer_in, params, series_values, visited_count, tables):
    query_key_value_weight, w_out, w_in, w_down, norm_gains = params
    cosine, sine = tables
    overall_rows = layer_in.shape[0]
    count_of_rows = overall_rows // ROW_POSITIONS
    model_width = w_out.shape[0]
    split_into_heads = (count_of_rows, ROW_POSITIONS, model_width // HEAD_SIZE, HEAD_SIZE)
    scale_first = lax.rsqrt(jnp.mean(layer_in * layer_in, axis=-1, keepdims=True) + EPS)
    normed = (layer_in * scale_first * norm_gains[0]).astype(jnp.bfloat16)
    query = rotate(
        matrix_product(normed, query_key_value_weight[0]).reshape(split_into_heads), cosine, sine
    ).astype(jnp.bfloat16)
    key_rows = rotate(
        matrix_product(normed, query_key_value_weight[1]).reshape(split_into_heads), cosine, sine
    ).astype(jnp.bfloat16)
    value_rows = (
        matrix_product(normed, query_key_value_weight[2])
        .astype(jnp.bfloat16)
        .reshape(split_into_heads)
    )
    rows_per_series = series_values.reshape(count_of_rows, ROW_POSITIONS)
    visited_rows = visited_count.reshape(count_of_rows, ROW_POSITIONS)
    mixed, logsum = lax.map(
        attend_row, (query, key_rows, value_rows, rows_per_series, visited_rows)
    )
    mixed = mixed.reshape(overall_rows, model_width).astype(jnp.bfloat16)
    middle = layer_in + partial_total(matrix_product(mixed, w_out))
    scale_second = lax.rsqrt(jnp.mean(middle * middle, axis=-1, keepdims=True) + EPS)
    normed_second = (middle * scale_second * norm_gains[1]).astype(jnp.bfloat16)
    before = matrix_product(normed_second, w_in)
    activated = (before * lax.logistic(before)).astype(jnp.bfloat16)
    result = middle + partial_total(matrix_product(activated, w_down))
    kept = (
        layer_in,
        scale_first,
        normed,
        query,
        key_rows,
        value_rows,
        mixed,
        logsum,
        middle,
        scale_second,
        normed_second,
        before,
        activated,
        rows_per_series,
        visited_rows,
    )
    return (result, kept)


def layer_backward(grad_output, kept, params, tables):
    query_key_value_weight, w_out, w_in, w_down, norm_gains = params
    cosine, sine = tables
    (
        layer_in,
        scale_first,
        normed,
        query,
        key_rows,
        value_rows,
        mixed,
        logsum,
        middle,
        scale_second,
        normed_second,
        before,
        activated,
        rows_per_series,
        visited_rows,
    ) = kept
    overall_rows = layer_in.shape[0]
    model_width = w_out.shape[0]
    grad_low = grad_output.astype(jnp.bfloat16)
    grad_down = inner_rows(activated, grad_low)
    grad_hidden = outer_cols(grad_low, w_down)
    sigmoid_term = lax.logistic(before)
    grad_before = (grad_hidden * sigmoid_term * (1.0 + before * (1.0 - sigmoid_term))).astype(
        jnp.bfloat16
    )
    grad_inproj = inner_rows(normed_second, grad_before)
    grad_normed_second = partial_back(outer_cols(grad_before, w_in))
    scaled_second = norm_gains[1] * grad_normed_second
    gain_second = jnp.sum(grad_normed_second * middle * scale_second, axis=0)
    cube_second = scale_second * scale_second * scale_second
    grad_middle = (
        grad_output
        + scale_second * scaled_second
        - middle * cube_second * jnp.mean(middle * scaled_second, axis=-1, keepdims=True)
    )
    grad_attn = grad_middle.astype(jnp.bfloat16)
    grad_outproj = inner_rows(mixed, grad_attn)
    grad_mixed = outer_cols(grad_attn, w_out).astype(jnp.bfloat16).reshape(query.shape)
    grad_query, grad_keys, grad_values = lax.map(
        attend_row_back,
        (query, key_rows, value_rows, rows_per_series, visited_rows, grad_mixed, logsum),
    )
    grad_qpre = (
        unrotate(grad_query, cosine, sine).astype(jnp.bfloat16).reshape(overall_rows, model_width)
    )
    grad_kpre = (
        unrotate(grad_keys, cosine, sine).astype(jnp.bfloat16).reshape(overall_rows, model_width)
    )
    grad_values = grad_values.reshape(overall_rows, model_width)
    grad_qkv = jnp.stack(
        [
            inner_rows(normed, grad_qpre),
            inner_rows(normed, grad_kpre),
            inner_rows(normed, grad_values),
        ]
    )
    grad_normed = partial_back(
        outer_cols(grad_qpre, query_key_value_weight[0])
        + outer_cols(grad_kpre, query_key_value_weight[1])
        + outer_cols(grad_values, query_key_value_weight[2])
    )
    scaled_first = norm_gains[0] * grad_normed
    gain_first = jnp.sum(grad_normed * layer_in * scale_first, axis=0)
    cube_first = scale_first * scale_first * scale_first
    grad_input = (
        grad_middle
        + scale_first * scaled_first
        - layer_in * cube_first * jnp.mean(layer_in * scaled_first, axis=-1, keepdims=True)
    )
    return (
        grad_input,
        (grad_qkv, grad_outproj, grad_inproj, grad_down, jnp.stack([gain_first, gain_second])),
    )


def on_device(
    tokens, cotangent, seg_ids, observed, query_key_value_weight, w_out, w_in, w_down, norm_gains
):
    params = (query_key_value_weight[0], w_out[0], w_in[0], w_down[0], norm_gains[0])
    tables = rope_tables()
    is_first = lax.axis_index("section") == 0
    micro_count = tokens.shape[0]
    blank = jnp.zeros_like(tokens[0])
    arriving = blank
    kept_ticks = []
    out_ticks = []
    for moment in range(micro_count + 1):
        own_index = min(moment, micro_count - 1)
        prior_index = max(moment - 1, 0)
        fresh = tokens[moment] if moment < micro_count else blank
        layer_input = jnp.where(is_first, fresh, arriving).astype(jnp.float32)
        series_values = jnp.where(is_first, seg_ids[own_index], seg_ids[prior_index])
        visited_count = jnp.where(is_first, observed[own_index], observed[prior_index])
        result, kept = layer_forward(layer_input, params, series_values, visited_count, tables)
        result = result.astype(jnp.bfloat16)
        kept_ticks.append(kept)
        out_ticks.append(result)
        if moment < micro_count:
            arriving = shifted(result, "section", 1)
    layer_acts = jnp.stack(
        [
            jnp.where(is_first, out_ticks[row_index], out_ticks[row_index + 1])
            for row_index in range(micro_count)
        ]
    )[None]
    upstream = blank
    grad_ticks = []
    summed = None
    for moment in range(micro_count + 1):
        later = cotangent[micro_count - 1 - moment] if moment < micro_count else blank
        grad_output = jnp.where(is_first, upstream, later).astype(jnp.float32)
        grad_input, grads = layer_backward(
            grad_output, kept_ticks[micro_count - moment], params, tables
        )
        grad_input = grad_input.astype(jnp.bfloat16)
        grad_ticks.append(grad_input)
        summed = (
            grads if summed is None else tuple((left + right for left, right in zip(summed, grads)))
        )
        if moment < micro_count:
            upstream = shifted(grad_input, "section", -1)
    summed = (
        lax.psum_scatter(
            summed[0].astype(jnp.bfloat16), "dp", scatter_dimension=1, tiled=True
        ).astype(jnp.float32),
        lax.psum_scatter(
            summed[1].astype(jnp.bfloat16), "dp", scatter_dimension=1, tiled=True
        ).astype(jnp.float32),
        lax.psum_scatter(
            summed[2].astype(jnp.bfloat16), "dp", scatter_dimension=0, tiled=True
        ).astype(jnp.float32),
        lax.psum_scatter(
            summed[3].astype(jnp.bfloat16), "dp", scatter_dimension=1, tiled=True
        ).astype(jnp.float32),
        lax.psum_scatter(
            summed[4].astype(jnp.bfloat16), "dp", scatter_dimension=1, tiled=True
        ).astype(jnp.float32),
    )
    grad_acts = jnp.stack(
        [
            jnp.where(
                is_first,
                grad_ticks[micro_count - row_index],
                grad_ticks[micro_count - 1 - row_index],
            )
            for row_index in range(micro_count)
        ]
    )[None]
    return (
        layer_acts,
        grad_acts,
        summed[0][None],
        summed[1][None],
        summed[2][None],
        summed[3][None],
        summed[4][None],
    )


def solution(mesh):
    return jax.shard_map(
        on_device,
        mesh=mesh,
        in_specs=(
            P(None, "dp", None),
            P(None, "dp", None),
            P(None, "dp"),
            P(None, "dp"),
            P("section", None, None, "tensor"),
            P("section", "tensor", None),
            P("section", None, "tensor"),
            P("section", "tensor", None),
            P("section", None, None),
        ),
        out_specs=(
            P("section", None, "dp", None),
            P("section", None, "dp", None),
            P("section", None, "dp", "tensor"),
            P("section", "tensor", "dp"),
            P("section", "dp", "tensor"),
            P("section", "tensor", "dp"),
            P("section", None, "dp"),
        ),
        check_vma=False,
    )
```

profile of v0, /device:TPU:0, one launch (start us, length us, event | category | flops | bytes accessed | tf_op | source)
XLA Modules:
  0.0 2018.6 jit_solution(13520599456594698902)
XLA Ops:
  34.7 11.7 while.78
  54.0 106.4 %all-reduce.13.cloned.1.call-done = bf16[1024,1280]{1,0:T(8,128)(2,1)} async-done(((bf16[1024,1280]{1,0:T(8,128)(2,1)}), bf16[1024,1280]{1,0:T(8,128)(2,1)}) %all-reduce.13.cloned.1.call-update) | async-done | bytes 2621456 | tf_op jit(solution)/shard_map/psum | solution.py:114
  164.8 5.9 fusion.247
  178.7 103.2 %all-reduce.15.cloned.1.call-done = bf16[1024,1280]{1,0:T(8,128)(2,1)} async-done(((bf16[1024,1280]{1,0:T(8,128)(2,1)}), bf16[1024,1280]{1,0:T(8,128)(2,1)}) %all-reduce.15.cloned.1.call-update) | async-done | bytes 2621456 | tf_op jit(solution)/shard_map/psum | solution.py:114
  294.9 52.7 %collective-permute-done = bf16[1024,1280]{1,0:T(8,128)(2,1)} collective-permute-done((bf16[1024,1280]{1,0:T(8,128)(2,1)}, bf16[1024,1280]{1,0:T(8,128)(2,1)}, u32[]{:S(2)}, u32[]{:S(2)}) %collective-permute-start) | collective-permute-done | bytes 2621472 | tf_op jit(solution)/shard_map/ppermute | solution.py:19
  368.5 11.7 while.79
  387.4 105.0 %all-reduce.17.cloned.1.call-done = bf16[1024,1280]{1,0:T(8,128)(2,1)} async-done(((bf16[1024,1280]{1,0:T(8,128)(2,1)}), bf16[1024,1280]{1,0:T(8,128)(2,1)}) %all-reduce.17.cloned.1.call-update) | async-done | bytes 2621456 | tf_op jit(solution)/shard_map/psum | solution.py:114
  508.4 103.2 %all-reduce.19.cloned.1.call-done = bf16[1024,1280]{1,0:T(8,128)(2,1)} async-done(((bf16[1024,1280]{1,0:T(8,128)(2,1)}), bf16[1024,1280]{1,0:T(8,128)(2,1)}) %all-reduce.19.cloned.1.call-update) | async-done | bytes 2621456 | tf_op jit(solution)/shard_map/psum | solution.py:114
  611.7 7.7 select_bitcast_fusion.1
  623.9 54.5 %collective-permute-done.1 = bf16[1024,1280]{1,0:T(8,128)(2,1)} collective-permute-done((bf16[1024,1280]{1,0:T(8,128)(2,1)}, bf16[1024,1280]{1,0:T(8,128)(2,1)}, u32[]{:S(2)}, u32[]{:S(2)}) %collective-permute-start.1) | collective-permute-done | bytes 2621472 | tf_op jit(solution)/shard_map/ppermute | solution.py:19
  696.7 11.8 while.80
  715.7 107.7 %all-reduce.21.cloned.1.call-done = bf16[1024,1280]{1,0:T(8,128)(2,1)} async-done(((bf16[1024,1280]{1,0:T(8,128)(2,1)}), bf16[1024,1280]{1,0:T(8,128)(2,1)}) %all-reduce.21.cloned.1.call-update) | async-done | bytes 2621456 | tf_op jit(solution)/shard_map/psum | solution.py:114
  830.5 8.1 multiply_convert_fusion.5
  845.2 105.7 %all-reduce.23.cloned.1.call-done = bf16[1024,1280]{1,0:T(8,128)(2,1)} async-done(((bf16[1024,1280]{1,0:T(8,128)(2,1)}), bf16[1024,1280]{1,0:T(8,128)(2,1)}) %all-reduce.23.cloned.1.call-update) | async-done | bytes 2621456 | tf_op jit(solution)/shard_map/psum | solution.py:118
  972.6 19.3 while.81
  1002.8 103.8 %all-reduce.25.cloned.1.call-done = bf16[1024,1280]{1,0:T(8,128)(2,1)} async-done(((bf16[1024,1280]{1,0:T(8,128)(2,1)}), bf16[1024,1280]{1,0:T(8,128)(2,1)}) %all-reduce.25.cloned.1.call-update) | async-done | bytes 2621456 | tf_op jit(solution)/shard_map/psum | solution.py:118
  1116.2 59.7 %collective-permute-done.2 = bf16[1024,1280]{1,0:T(8,128)(2,1)S(1)} collective-permute-done((bf16[1024,1280]{1,0:T(8,128)(2,1)S(1)}, bf16[1024,1280]{1,0:T(8,128)(2,1)S(1)}, u32[]{:S(2)}, u32[]{:S(2)}) %collective-permute-start.2) | collective-permute-done | bytes 2621472 | tf_op jit(solution)/shard_map/ppermute | solution.py:19
  1187.6 102.5 %all-reduce.27.cloned.1.call-done = bf16[1024,1280]{1,0:T(8,128)(2,1)} async-done(((bf16[1024,1280]{1,0:T(8,128)(2,1)}), bf16[1024,1280]{1,0:T(8,128)(2,1)}) %all-reduce.27.cloned.1.call-update) | async-done | bytes 2621456 | tf_op jit(solution)/shard_map/psum | solution.py:118
  1311.9 19.2 while.82
  1341.9 103.2 %all-reduce.29.cloned.1.call-done = bf16[1024,1280]{1,0:T(8,128)(2,1)} async-done(((bf16[1024,1280]{1,0:T(8,128)(2,1)}), bf16[1024,1280]{1,0:T(8,128)(2,1)}) %all-reduce.29.cloned.1.call-update) | async-done | bytes 2621456 | tf_op jit(solution)/shard_map/psum | solution.py:118
  1458.3 59.2 %collective-permute-done.3 = bf16[1024,1280]{1,0:T(8,128)(2,1)S(1)} collective-permute-done((bf16[1024,1280]{1,0:T(8,128)(2,1)S(1)}, bf16[1024,1280]{1,0:T(8,128)(2,1)S(1)}, u32[]{:S(2)}, u32[]{:S(2)}) %collective-permute-start.3) | collective-permute-done | bytes 2621472 | tf_op jit(solution)/shard_map/ppermute | solution.py:19
  1529.0 9.8 fusion.255
  1543.5 88.0 %all-reduce.31.cloned.1.call-done = bf16[1024,1280]{1,0:T(8,128)(2,1)} async-done(((bf16[1024,1280]{1,0:T(8,128)(2,1)}), bf16[1024,1280]{1,0:T(8,128)(2,1)}) %all-reduce.31.cloned.1.call-update) | async-done | bytes 2621456 | tf_op jit(solution)/shard_map/psum | solution.py:118
  1649.3 9.7 convolution_add_fusion.1
  1659.0 8.1 fusion.172
  1667.8 6.4 fusion.322
  1713.0 19.3 while.83
  1743.6 7.6 copy.121
  1751.3 8.3 reshape.966
  1759.7 9.3 convolution_convert_fusion.3
  1783.6 10.1 reduce-scatter.16.cloned.1.call-done
  1805.8 180.1 %all-reduce.33.cloned.1.call-done = (bf16[1024,1280]{1,0:T(8,128)(2,1)}, bf16[1024,1280]{1,0:T(8,128)(2,1)}) async-done(((bf16[1024,1280]{1,0:T(8,128)(2,1)}, bf16[1024,1280]{1,0:T(8,128)(2,1)}), (bf16[1024,1280]{1,0:T(8,128)(2,1)}, bf16[1024,1280]{1,0:T(8,128)(2,1)})) %all-reduce.33.cloned.1.call-update) | async-done | bytes 5242896 | tf_op jit(solution)/shard_map/psum | solution.py:114
  (786 shorter events, 475.0 us)
Async XLA Ops:
  7.2 157.6 %copy-start = (bf16[1,1280,1280]{2,1,0:T(8,128)(2,1)S(1)}, bf16[1,1280,1280]{2,1,0:T(8,128)(2,1)}, u32[]{:S(2)}) copy-start(bf16[1,1280,1280]{2,1,0:T(8,128)(2,1)} %param.27) | copy-start | bytes 9830404
  7.2 153.2 %all-reduce.13.cloned.1.call-start = ((), (), s32[]{:S(2)}) async-start(), calls=%async_computation.5 | async-start | bytes 5242880 | tf_op jit(solution)/shard_map/psum | solution.py:114
  11.7 668.1 %copy-start.119 = (f32[1280]{0:T(1024)}, f32[1280]{0:T(1024)S(1)}, u32[]{:S(2)}) copy-start(f32[1280]{0:T(1024)S(1)} %get-tuple-element.533) | copy-start | bytes 15364
  12.0 1321.1 %copy-start.82 = (f32[512,40]{0,1:T(8,128)}, f32[512,40]{0,1:T(8,128)S(1)}, u32[]{:S(2)}) copy-start(f32[512,40]{0,1:T(8,128)S(1)} %get-tuple-element.725) | copy-start | bytes 245764
  12.0 1321.1 %copy-start.84 = (f32[512,40]{0,1:T(8,128)}, f32[512,40]{0,1:T(8,128)S(1)}, u32[]{:S(2)}) copy-start(f32[512,40]{0,1:T(8,128)S(1)} %get-tuple-element.726) | copy-start | bytes 245764
  46.5 248.4 %copy-start.129 = (s32[2,512]{1,0:T(2,128)}, s32[2,512]{1,0:T(2,128)S(1)}, u32[]{:S(2)}) copy-start(s32[2,512]{1,0:T(2,128)S(1)} %get-tuple-element.1375) | copy-start | bytes 12292
  46.5 248.4 %copy-start.127 = (s32[2,512]{1,0:T(2,128)}, s32[2,512]{1,0:T(2,128)S(1)}, u32[]{:S(2)}) copy-start(s32[2,512]{1,0:T(2,128)S(1)} %get-tuple-element.1374) | copy-start | bytes 12292
  53.4 228.5 %all-reduce.15.cloned.1.call-start = ((), (), s32[]{:S(2)}) async-start(), calls=%async_computation.6 | async-start | bytes 5242880 | tf_op jit(solution)/shard_map/psum | solution.py:114
  178.6 313.8 %all-reduce.17.cloned.1.call-start = ((), (), s32[]{:S(2)}) async-start(), calls=%async_computation.7 | async-start | bytes 5242880 | tf_op jit(solution)/shard_map/psum | solution.py:114
  287.8 59.8 %collective-permute-start = (bf16[1024,1280]{1,0:T(8,128)(2,1)}, bf16[1024,1280]{1,0:T(8,128)(2,1)}, u32[]{:S(2)}, u32[]{:S(2)}) collective-permute-start(bf16[1024,1280]{1,0:T(8,128)(2,1)} %add_convert_fusion.5), channel_id=1, source_target_pairs={{0,16},{1,17},{2,18},{3,19},{4,20},{5,21},{6,22},{7,23},{8,24},{9,... | collective-permute-start | bytes 7864328 | tf_op jit(solution)/shard_map/ppermute | solution.py:19
  387.2 224.5 %all-reduce.19.cloned.1.call-start = ((), (), s32[]{:S(2)}) async-start(), calls=%async_computation.8 | async-start | bytes 5242880 | tf_op jit(solution)/shard_map/psum | solution.py:114
  508.4 315.0 %all-reduce.21.cloned.1.call-start = ((), (), s32[]{:S(2)}) async-start(), calls=%async_computation.9 | async-start | bytes 5242880 | tf_op jit(solution)/shard_map/psum | solution.py:114
  619.4 59.0 %collective-permute-start.1 = (bf16[1024,1280]{1,0:T(8,128)(2,1)}, bf16[1024,1280]{1,0:T(8,128)(2,1)}, u32[]{:S(2)}, u32[]{:S(2)}) collective-permute-start(bf16[1024,1280]{1,0:T(8,128)(2,1)} %get-tuple-element.657), channel_id=1, source_target_pairs={{0,16},{1,17},{2,18},{3,19},{4,20},{5,21},{6,22},{7,23},{8,24},{9,... | collective-permute-start | bytes 7864328 | tf_op jit(solution)/shard_map/ppermute | solution.py:19
  715.5 235.5 %all-reduce.23.cloned.1.call-start = ((), (), s32[]{:S(2)}) async-start(), calls=%async_computation.10 | async-start | bytes 5242880 | tf_op jit(solution)/shard_map/psum | solution.py:118
  826.4 129.8 %copy-start.150 = (f32[1024]{0:T(1024)}, f32[1024]{0:T(1024)S(1)}, u32[]{:S(2)}) copy-start(f32[1024]{0:T(1024)S(1)} %get-tuple-element.724) | copy-start | bytes 12292
  845.0 261.6 %all-reduce.25.cloned.1.call-start = ((), (), s32[]{:S(2)}) async-start(), calls=%async_computation.11 | async-start | bytes 5242880 | tf_op jit(solution)/shard_map/psum | solution.py:118
  1002.7 287.3 %all-reduce.27.cloned.1.call-start = ((), (), s32[]{:S(2)}) async-start(), calls=%async_computation.12 | async-start | bytes 5242880 | tf_op jit(solution)/shard_map/psum | solution.py:118
  1114.6 61.2 %collective-permute-start.2 = (bf16[1024,1280]{1,0:T(8,128)(2,1)S(1)}, bf16[1024,1280]{1,0:T(8,128)(2,1)S(1)}, u32[]{:S(2)}, u32[]{:S(2)}) collective-permute-start(bf16[1024,1280]{1,0:T(8,128)(2,1)S(1)} %fusion.201), channel_id=1, source_target_pairs={{16,0},{17,1},{18,2},{19,3},{20,4},{21,5},{22,6},{23,7},{24,8},{25... | collective-permute-start | bytes 7864328 | tf_op jit(solution)/shard_map/ppermute | solution.py:19
  1187.5 257.6 %all-reduce.29.cloned.1.call-start = ((), (), s32[]{:S(2)}) async-start(), calls=%async_computation.13 | async-start | bytes 5242880 | tf_op jit(solution)/shard_map/psum | solution.py:118
  1187.6 108.3 %copy-start.159 = (f32[1024]{0:T(1024)S(1)}, f32[1024]{0:T(1024)}, u32[]{:S(2)}) copy-start(f32[1024]{0:T(1024)} %get-tuple-element.719) | copy-start | bytes 12292
  1341.8 108.4 %copy-start.158 = (f32[1024]{0:T(1024)S(1)}, f32[1024]{0:T(1024)}, u32[]{:S(2)}) copy-start(f32[1024]{0:T(1024)} %get-tuple-element.717) | copy-start | bytes 12292
  1341.9 289.6 %all-reduce.31.cloned.1.call-start = ((), (), s32[]{:S(2)}) async-start(), calls=%async_computation.14 | async-start | bytes 5242880 | tf_op jit(solution)/shard_map/psum | solution.py:118
  1457.0 60.4 %collective-permute-start.3 = (bf16[1024,1280]{1,0:T(8,128)(2,1)S(1)}, bf16[1024,1280]{1,0:T(8,128)(2,1)S(1)}, u32[]{:S(2)}, u32[]{:S(2)}) collective-permute-start(bf16[1024,1280]{1,0:T(8,128)(2,1)S(1)} %get-tuple-element.655), channel_id=1, source_target_pairs={{16,0},{17,1},{18,2},{19,3},{20,4},{21,5},{22,6},{23,7},{24,8},{25... | collective-permute-start | bytes 7864328 | tf_op jit(solution)/shard_map/ppermute | solution.py:19
  1529.0 247.9 %reduce-scatter.18.cloned.1.call-start = ((), (), s32[]{:S(2)}) async-start(), calls=%async_computation.18 | async-start | bytes 1228800
  1649.1 129.7 %reduce-scatter.14.cloned.1.call-start = ((), (), s32[]{:S(2)}) async-start(), calls=%async_computation.16 | async-start | bytes 4096000 | tf_op jit(solution)/shard_map/reduce_scatter | solution.py:308
  1667.2 114.1 %reduce-scatter.12.cloned.1.call-start = ((), (), s32[]{:S(2)}) async-start(), calls=%async_computation.15 | async-start | bytes 4096000 | tf_op jit(solution)/shard_map/reduce_scatter | solution.py:305
  1699.5 94.2 %reduce-scatter.16.cloned.1.call-start = ((), (), s32[]{:S(2)}) async-start(), calls=%async_computation.17 | async-start | bytes 3276800
  1759.6 226.3 %all-reduce.33.cloned.1.call-start = ((), (), s32[]{:S(2)}) async-start(), calls=%async_computation.20 | async-start | bytes 10485760 | tf_op jit(solution)/shard_map/psum | solution.py:114
  1775.5 234.8 %reduce-scatter.20.cloned.1.call-start = ((), (), s32[]{:S(2)}) async-start(), calls=%async_computation.19 | async-start | bytes 409600
  1797.2 188.7 %copy-start.121 = (f32[1280]{0:T(1024)S(1)}, f32[1280]{0:T(1024)}, u32[]{:S(2)}) copy-start(f32[1280]{0:T(1024)} %copy-done.119) | copy-start | bytes 15364
  1797.2 188.7 %copy-start.144 = (f32[1024]{0:T(1024)S(1)}, f32[1024]{0:T(1024)}, u32[]{:S(2)}) copy-start(f32[1024]{0:T(1024)} %copy-done.143) | copy-start | bytes 12292
  1805.8 183.9 %copy-start.157 = (f32[1,1280]{1,0:T(1,128)S(1)}, f32[1,1280]{1,0:T(1,128)}, u32[]{:S(2)}) copy-start(f32[1,1280]{1,0:T(1,128)} %stack.106) | copy-start | bytes 15364
  (215 other events, 1916.5 us)
Sparse Core Ops, SparseCore 0:
  53.6 106.8 all-reduce.12
  178.7 103.1 all-reduce.14
  387.3 105.0 all-reduce.16
  508.5 103.1 all-reduce.18
  715.6 107.7 all-reduce.20
  845.1 105.8 all-reduce.22
  1002.8 103.6 all-reduce.24
  1187.6 102.3 all-reduce.26
  1342.0 103.1 all-reduce.28
  1529.1 102.3 all-reduce.30
  1649.2 23.1 reduce-scatter.17
  1674.9 38.7 reduce-scatter.13
  1716.3 38.7 reduce-scatter.11
  1759.7 33.9 reduce-scatter.15
  1796.6 189.2 all-reduce.32
  1990.8 19.4 reduce-scatter.19
where the time goes:
time: 2030 us; the launch traced here: 2020 us
  waiting for transfers between devices  1450 us (71%)
  matrix products  252 us (12%)
  local copies, waits for them, and re-layouts  146 us (7%)
  other arithmetic  141 us (7%)
    psum x6, waiting for transfers between devices, partial_total(): return lax.psum(term.astype(jnp.bfloat16), 'tensor').astype(jnp.float32)  706 us
    psum x5, waiting for transfers between devices, partial_back(): return lax.psum(term.astype(jnp.bfloat16), 'tensor').astype(jnp.float32)  503 us
    ppermute x4, waiting for transfers between devices, shifted(): return lax.ppermute(block, axis, route)  226 us
    dot_general x18, matrix products, matrix_product(): return jnp.dot(left, right, preferred_element_type=jnp.float32)  69 us
    dot_general x18, matrix products, inner_rows(): lax.dot_general(left, right, (((0,), (0,)), ((), ())), preferred_element_...  67.6 us
    unnamed x333, local copies, waits for them, and re-layouts  66.6 us
    dot_general x18, matrix products, outer_cols(): lax.dot_general(left, right, (((1,), (1,)), ((), ())), preferred_element_...  60.3 us
  transfers between devices with their start and end apart: 20, of which 17 were waited for; matrix products, arithmetic and copies ran while one was open for 8% of the time, Pallas kernels for 0%

commit v1 on v0

v1 whole, which is shorter than its diff:
```python
import functools
import math

import jax
import jax.numpy as jnp
from jax import lax
from jax.experimental import pallas as pl
from jax.experimental.pallas import tpu as pltpu
from jax.sharding import PartitionSpec as P

HEAD_SIZE = 80
HALF = HEAD_SIZE // 2
ROW = 512
QB = 128
GROUP = 8
EPS = 1e-06
BIG = 1000000000.0
SCALE = 1.0 / math.sqrt(HEAD_SIZE)
BF16 = jnp.bfloat16
F32 = jnp.float32


def dot_nn(a, b):
    return lax.dot_general(a, b, (((1,), (0,)), ((), ())), preferred_element_type=F32)


def dot_nt(a, b):
    return lax.dot_general(a, b, (((1,), (1,)), ((), ())), preferred_element_type=F32)


def dot_tn(a, b):
    return lax.dot_general(a, b, (((0,), (0,)), ((), ())), preferred_element_type=F32)


def rope_tables():
    freq = 10000.0 ** (-jnp.arange(HALF, dtype=F32) / HALF)
    ang = jnp.arange(ROW, dtype=F32)[:, None] * freq[None, :]
    cos, sin = jnp.cos(ang), jnp.sin(ang)
    cos_full = jnp.tile(jnp.concatenate([cos, cos], axis=1), (1, GROUP))
    sin_full = jnp.tile(jnp.concatenate([-sin, sin], axis=1), (1, GROUP))
    return cos_full, sin_full


def partner(x):
    width = x.shape[1]
    lane = lax.broadcasted_iota(jnp.int32, x.shape, 1)
    first = lax.rem(lane, HEAD_SIZE) < HALF
    return jnp.where(first, pltpu.roll(x, width - HALF, 1), pltpu.roll(x, HALF, 1))


def block_mask(i, seg_col, seg_row, obs_row):
    k0 = max(i - 1, 0) * QB
    k1 = (i + 1) * QB
    shape = (QB, k1 - k0)
    qi = lax.broadcasted_iota(jnp.int32, shape, 0) + i * QB
    kj = lax.broadcasted_iota(jnp.int32, shape, 1) + k0
    same = seg_col[i * QB:(i + 1) * QB, :] == seg_row[:, k0:k1]
    seen = (obs_row[:, k0:k1] == 1) | (kj == qi)
    return k0, k1, same & (kj <= qi) & seen


def softmax_block(q, k, allowed):
    s = jnp.where(allowed, dot_nt(q, k) * SCALE, -BIG)
    e = jnp.exp(s - jnp.max(s, axis=1, keepdims=True))
    return e * (1.0 / jnp.sum(e, axis=1, keepdims=True))


def attn_fwd_kernel(qp, kp, v, seg_col, seg_row, obs_row, cos, sin, q_out, k_out, o_out):
    x = qp[...]
    q_out[...] = (x * cos[...] + partner(x) * sin[...]).astype(BF16)
    x = kp[...]
    k_out[...] = (x * cos[...] + partner(x) * sin[...]).astype(BF16)
    sc, sr, ob = seg_col[...], seg_row[...], obs_row[...]
    for i in range(ROW // QB):
        k0, k1, allowed = block_mask(i, sc, sr, ob)
        for h in range(GROUP):
            c0, c1 = h * HEAD_SIZE, (h + 1) * HEAD_SIZE
            p = softmax_block(q_out[i * QB:(i + 1) * QB, c0:c1], k_out[k0:k1, c0:c1], allowed)
            o_out[i * QB:(i + 1) * QB, c0:c1] = dot_nn(p.astype(BF16), v[k0:k1, c0:c1]).astype(BF16)


def attn_bwd_kernel(q, k, v, do, seg_col, seg_row, obs_row, cos, sin, dqp, dkp, dv, dq_s, dk_s, dv_s):
    dk_s[...] = jnp.zeros_like(dk_s)
    dv_s[...] = jnp.zeros_like(dv_s)
    sc, sr, ob = seg_col[...], seg_row[...], obs_row[...]
    for i in range(ROW // QB):
        k0, k1, allowed = block_mask(i, sc, sr, ob)
        r0, r1 = i * QB, (i + 1) * QB
        for h in range(GROUP):
            c0, c1 = h * HEAD_SIZE, (h + 1) * HEAD_SIZE
            qi, ki, vi, di = q[r0:r1, c0:c1], k[k0:k1, c0:c1], v[k0:k1, c0:c1], do[r0:r1, c0:c1]
            p = softmax_block(qi, ki, allowed)
            dv_s[k0:k1, c0:c1] += dot_tn(p.astype(BF16), di)
            dp = dot_nt(di, vi)
            ds = (p * (dp - jnp.sum(p * dp, axis=1, keepdims=True))).astype(BF16)
            dq_s[r0:r1, c0:c1] = dot_nn(ds, ki) * SCALE
            dk_s[k0:k1, c0:c1] += dot_tn(ds, qi) * SCALE
    x = dq_s[...]
    dqp[...] = (x * cos[...] - partner(x) * sin[...]).astype(BF16)
    x = dk_s[...]
    dkp[...] = (x * cos[...] - partner(x) * sin[...]).astype(BF16)
    dv[...] = dv_s[...].astype(BF16)


def attn_specs(hd, rows):
    width = GROUP * HEAD_SIZE
    wide = pl.BlockSpec((ROW, width), lambda r, g: (r, g))
    col = pl.BlockSpec((ROW, 1), lambda r, g: (r, 0))
    row = pl.BlockSpec((1, ROW), lambda r, g: (0, r))
    table = pl.BlockSpec((ROW, width), lambda r, g: (0, 0))
    return wide, col, row, table, (rows // ROW, hd // width), width


def attention(qp, kp, v, seg, obs, tables):
    rows, hd = qp.shape
    wide, col, row, table, grid, width = attn_specs(hd, rows)
    out = jax.ShapeDtypeStruct((rows, hd), BF16)
    return pl.pallas_call(
        attn_fwd_kernel,
        grid=grid,
        in_specs=[wide, wide, wide, col, row, row, table, table],
        out_specs=[wide, wide, wide],
        out_shape=[out, out, out],
        compiler_params=pltpu.CompilerParams(vmem_limit_bytes=40 * 2**20),
        cost_estimate=pl.CostEstimate(flops=rows * hd * 2048, bytes_accessed=rows * hd * 16, transcendentals=rows * 4096),
    )(qp, kp, v, seg[:, None], seg[None, :], obs[None, :], *tables)


def attention_back(q, k, v, do, seg, obs, tables):
    rows, hd = q.shape
    wide, col, row, table, grid, width = attn_specs(hd, rows)
    out = jax.ShapeDtypeStruct((rows, hd), BF16)
    return pl.pallas_call(
        attn_bwd_kernel,
        grid=grid,
        in_specs=[wide, wide, wide, wide, col, row, row, table, table],
        out_specs=[wide, wide, wide],
        out_shape=[out, out, out],
        scratch_shapes=[pltpu.VMEM((ROW, width), F32)] * 3,
        compiler_params=pltpu.CompilerParams(vmem_limit_bytes=40 * 2**20),
        cost_estimate=pl.CostEstimate(flops=rows * hd * 5120, bytes_accessed=rows * hd * 14, transcendentals=rows * 4096),
    )(q, k, v, do, seg[:, None], seg[None, :], obs[None, :], *tables)


def forward(x, weights, gains, seg, obs, tables):
    wq, wk, wv, wo, w_in, w_down = weights
    r1 = lax.rsqrt(jnp.mean(x * x, axis=1, keepdims=True) + EPS)
    n1 = (x * r1 * gains[0]).astype(BF16)
    q, k, o = attention(dot_nt(n1, wq), dot_nt(n1, wk), dot_nt(n1, wv).astype(BF16), seg, obs, tables)
    v = dot_nt(n1, wv).astype(BF16)
    h2 = x + dot_nn(o, wo)
    r2 = lax.rsqrt(jnp.mean(h2 * h2, axis=1, keepdims=True) + EPS)
    n2 = (h2 * r2 * gains[1]).astype(BF16)
    us = [dot_nn(n2, w) for w in w_in]
    acts = [(u * lax.logistic(u)).astype(BF16) for u in us]
    out = h2
    for a, w in zip(acts, w_down):
        out = out + dot_nn(a, w)
    return out, (x, r1, n1, q, k, v, o, h2, r2, n2, us, acts)


def norm_back(g, dn, h, r, gain):
    y = gain * dn
    return g + r * y - h * (r * r * r) * jnp.mean(h * y, axis=1, keepdims=True)


def backward(g, kept, weights, gains, seg, obs, tables, with_grads):
    wq, wk, wv, wo, w_in, w_down = weights
    x, r1, n1, q, k, v, o, h2, r2, n2, us, acts = kept
    heads = len(w_in)
    gb = g.astype(BF16)
    dn2 = None
    g_down, g_in = [None] * heads, [None] * heads
    for s in reversed(range(heads)):
        sig = lax.logistic(us[s])
        du = (dot_nt(gb, w_down[s]) * sig * (1.0 + us[s] * (1.0 - sig))).astype(BF16)
        if with_grads:
            g_down[s] = dot_tn(gb, acts[s]).astype(BF16)
            g_in[s] = dot_tn(n2, du).astype(BF16)
        term = dot_nt(du, w_in[s])
        dn2 = term if dn2 is None else dn2 + term
    dh2 = norm_back(g, dn2, h2, r2, gains[1])
    ga = dh2.astype(BF16)
    do = dot_nt(ga, wo).astype(BF16)
    dqp, dkp, dv = attention_back(q, k, v, do, seg, obs, tables)
    dn1 = dot_nn(dqp, wq) + dot_nn(dkp, wk) + dot_nn(dv, wv)
    dh = norm_back(dh2, dn1, x, r1, gains[0])
    if not with_grads:
        return dh, None
    wide = wq.shape[0] // heads
    g_attn = [None] * heads
    parts = [dot_tn(n1, d).astype(BF16) for d in (dqp, dkp, dv)] + [dot_tn(ga, o).astype(BF16)]
    for s in range(heads):
        g_attn[s] = jnp.stack([part[:, s * wide:(s + 1) * wide] for part in parts], axis=1).reshape(wq.shape[1], 4 * wide)
    gain_terms = jnp.stack([jnp.sum(dn1 * x * r1, axis=0), jnp.sum(dn2 * h2 * r2, axis=0)])
    return dh, (g_attn, g_in, g_down, gain_terms)


def bits_of(n):
    return [1 << i for i in range(n.bit_length() - 1)]


def swap(x, axis, bit):
    n = lax.axis_size(axis)
    return lax.ppermute(x, axis, [(i, i ^ bit) for i in range(n)])


def turn(x, axis, step):
    n = lax.axis_size(axis)
    return lax.ppermute(x, axis, [(i, (i + step) % n) for i in range(n)])


def gather_shards(shard):
    n_dp, n_t = lax.axis_size("dp"), lax.axis_size("tensor")
    me = lax.axis_index("dp")
    rows = shard.shape[0] // n_dp
    piece = lax.dynamic_slice_in_dim(shard, me * rows, rows, 0)
    slots = []
    for _ in range(1, n_t):
        piece = turn(piece, "tensor", -1)
        have = {0: piece}
        for bit in reversed(bits_of(n_dp)):
            have.update({j ^ bit: swap(p, "dp", bit) for j, p in list(have.items())})
        slots.append([(me ^ j, p) for j, p in have.items()])
    return rows, slots


def gather_square(shard):
    rows, slots = gather_shards(shard)
    result = [shard]
    for slot in slots:
        full = jnp.zeros(shard.shape, shard.dtype)
        for at, p in slot:
            full = lax.dynamic_update_slice_in_dim(full, p, at * rows, 0)
        result.append(full)
    return result


def gather_heads(stack):
    kinds, hd, d = stack.shape
    n_t = lax.axis_size("tensor")
    rows, slots = gather_shards(stack.reshape(kinds * hd, d))
    full = jnp.zeros((kinds, n_t * hd, d), stack.dtype)
    full = lax.dynamic_update_slice(full, stack, (0, 0, 0))
    for s, slot in enumerate(slots):
        for at, p in slot:
            first = at * rows
            full = lax.dynamic_update_slice(full, p[None], (first // hd, (s + 1) * hd + lax.rem(first, hd), 0))
    return full


def reduce_blocks(parts):
    n_dp, n_t = lax.axis_size("dp"), lax.axis_size("tensor")
    me = lax.axis_index("dp")
    rows = parts[0].shape[0] // n_dp
    total = None
    for s in reversed(range(n_t)):
        term = parts[s].reshape(n_dp, rows, -1)
        for bit in bits_of(n_dp):
            view = term.reshape(-1, 2, rows, term.shape[-1])
            own = jnp.where(me & bit == 0, 0, 1)
            keep = lax.dynamic_index_in_dim(view, own, 1, keepdims=False)
            give = lax.dynamic_index_in_dim(view, 1 - own, 1, keepdims=False)
            term = (keep.astype(F32) + swap(give, "dp", bit).astype(F32)).astype(BF16)
        term = term.reshape(rows, -1)
        if total is not None:
            term = term.astype(F32) + turn(total, "tensor", 1).astype(F32)
            term = term if s == 0 else term.astype(BF16)
        total = term
    return total.astype(F32)


def spread_rows(block):
    n_t = lax.axis_size("tensor")
    me = lax.axis_index("tensor")
    full = jnp.zeros((n_t,) + block.shape, block.dtype)
    piece = block
    for s in range(n_t):
        full = lax.dynamic_update_slice(full, piece[None], (lax.rem(me + s, n_t), 0, 0))
        if s + 1 < n_t:
            piece = turn(piece, "tensor", -1)
    return full.reshape(n_t * block.shape[0], block.shape[1])


def own_rows(x, count):
    flat = x.reshape((-1,) + x.shape[2:])
    return lax.dynamic_slice_in_dim(flat, lax.axis_index("tensor") * count, count, 0)


def on_device(tokens, cotangent, seg_ids, observed, w_qkv, w_out, w_in, w_down, norm_gains):
    n_dp, n_t = lax.axis_size("dp"), lax.axis_size("tensor")
    w_qkv, w_out, w_in, w_down, gains = w_qkv[0], w_out[0], w_in[0], w_down[0], norm_gains[0]
    micro, rows, d = tokens.shape
    hd = w_out.shape[0]
    count = micro * rows // n_t
    is_first = lax.axis_index("section") == 0
    tables = rope_tables()

    heads = gather_heads(jnp.concatenate([jnp.swapaxes(w_qkv, 1, 2), w_out[None]], axis=0))
    weights = (heads[0], heads[1], heads[2], heads[3], gather_square(w_in), gather_square(w_down))

    x0 = own_rows(tokens, count)
    g1 = own_rows(cotangent, count)
    seg, obs = own_rows(seg_ids, count), own_rows(observed, count)

    out0, _ = forward(x0.astype(F32), weights, gains, seg, obs, tables)
    arriving = lax.ppermute(out0.astype(BF16), "section", [(0, 1)])
    x1 = jnp.where(is_first, x0, arriving)
    out1, kept = forward(x1.astype(F32), weights, gains, seg, obs, tables)
    layer_acts = spread_rows(out1.astype(BF16))
    dh1, _ = backward(g1.astype(F32), kept, weights, gains, seg, obs, tables, False)
    upstream = lax.ppermute(dh1.astype(BF16), "section", [(1, 0)])
    g0 = jnp.where(is_first, upstream, g1)
    dh0, (g_attn, g_in, g_down, gain_terms) = backward(g0.astype(F32), kept, weights, gains, seg, obs, tables, True)
    grad_acts = spread_rows(dh0.astype(BF16))

    r_down = reduce_blocks(g_down)
    r_in = reduce_blocks(g_in)
    r_attn = reduce_blocks(g_attn)
    r_gain = lax.psum(gain_terms, ("tensor", "dp"))
    piece = d // n_dp
    r_gain = lax.dynamic_slice_in_dim(r_gain, lax.axis_index("dp") * piece, piece, 1)
    r_qkv = jnp.stack([r_attn[:, i * hd:(i + 1) * hd] for i in range(3)])
    r_out = r_attn[:, 3 * hd:].T
    return (
        layer_acts.reshape(1, micro, rows, d),
        grad_acts.reshape(1, micro, rows, d),
        r_qkv[None],
        r_out[None],
        r_in[None],
        r_down.T[None],
        r_gain[None],
    )


def solution(mesh):
    return jax.shard_map(
        on_device,
        mesh=mesh,
        in_specs=(
            P(None, "dp", None),
            P(None, "dp", None),
            P(None, "dp"),
            P(None, "dp"),
            P("section", None, None, "tensor"),
            P("section", "tensor", None),
            P("section", None, "tensor"),
            P("section", "tensor", None),
            P("section", None, None),
        ),
        out_specs=(
            P("section", None, "dp", None),
            P("section", None, "dp", None),
            P("section", None, "dp", "tensor"),
            P("section", "tensor", "dp"),
            P("section", "dp", "tensor"),
            P("section", "tensor", "dp"),
            P("section", None, "dp"),
        ),
        check_vma=False,
    )
```

time: 2030 us -> 1280 us (0.63)
  waiting for transfers between devices: 1450 us -> 385 us
  local copies, waits for them, and re-layouts: 146 us -> 323 us
  Pallas kernels: 0 us -> 151 us
  other arithmetic: 141 us -> 38.6 us
  blocking collectives: 0 us -> 59.3 us
  starting transfers between devices: 14.3 us -> 59.8 us
    psum x11 -> x0, waiting for transfers between devices: 1210 us -> none  [the longest x6 706 us: partial_total(): return lax.psum(term.astype(jnp.bfloat16), 'tensor').astype(jnp.float32)]
    ppermute x4 -> x77, waiting for transfers between devices: 226 us -> 385 us  [the longest x24 244 us: turn(): return lax.ppermute(x, axis, [(i, (i + step) % n) for i in range(n)])]
    pallas_call x0 -> x4, Pallas kernels: none -> 151 us  [the longest x2 90 us: attention_back(): pl.pallas_call(attn_bwd_kernel, grid=grid, in_specs=[wide, wide, wide, wi...]
    dynamic_update_slice x0 -> x43, local copies, waits for them, and re-layouts: none -> 123 us  [the longest x12 57.5 us: gather_heads(): lax.dynamic_update_slice(full, p[None], (first // hd, (s + 1) * hd + lax....]
    psum x0 -> x1, blocking collectives: none -> 59.3 us  [on_device(): r_gain = lax.psum(gain_terms, ('tensor', 'dp'))]
    reduce_sum x18 -> x2, other arithmetic: 51.6 us -> 3.51 us  [forward(): r1 = lax.rsqrt(jnp.mean(x * x, axis=1, keepdims=True) + EPS)]
    ppermute x4 -> x77, starting transfers between devices: 12.3 us -> 59.8 us  [the longest x51 27.5 us: swap(): return lax.ppermute(x, axis, [(i, i ^ bit) for i in range(n)])]
    dynamic_slice x12 -> x9, local copies, waits for them, and re-layouts: 0.07 us -> 45.5 us  [the longest x4 44.1 us: reduce_blocks(): keep = lax.dynamic_index_in_dim(view, own, 1, keepdims=False)]
  transfers between devices with their start and end apart: 20 -> 77, of which waited for: 17 -> 28; matrix products, arithmetic and copies ran while one was open for 8% -> 38% of each run, Pallas kernels for 0% -> 6%
where the time goes in v1:
time: 1280 us; the launch traced here: 1270 us
  waiting for transfers between devices  385 us (30%)
  local copies, waits for them, and re-layouts  323 us (25%)
  matrix products  255 us (20%)
  Pallas kernels  151 us (12%)
  starting transfers between devices  59.8 us (5%)
  blocking collectives  59.3 us (5%)
  other arithmetic  38.6 us (3%)
    ppermute x24, waiting for transfers between devices, turn(): return lax.ppermute(x, axis, [(i, (i + step) % n) for i in range(n)])  244 us
    dot_general x20, matrix products, dot_nn(): lax.dot_general(a, b, (((1,), (0,)), ((), ())), preferred_element_type=F32)  108 us
    dot_general x20, matrix products, dot_nt(): lax.dot_general(a, b, (((1,), (1,)), ((), ())), preferred_element_type=F32)  104 us
    ppermute x51, waiting for transfers between devices, swap(): return lax.ppermute(x, axis, [(i, i ^ bit) for i in range(n)])  103 us
    pallas_call x2, Pallas kernels, attention_back(): pl.pallas_call(attn_bwd_kernel, grid=grid, in_specs=[wide, wide, wide, wi...  90 us
    unnamed x231, local copies, waits for them, and re-layouts  86.8 us
    pallas_call x2, Pallas kernels, attention(): pl.pallas_call(attn_fwd_kernel, grid=grid, in_specs=[wide, wide, wide, co...  60.9 us
    psum x1, blocking collectives, on_device(): r_gain = lax.psum(gain_terms, ('tensor', 'dp'))  59.3 us
  transfers between devices with their start and end apart: 77, of which 28 were waited for; matrix products, arithmetic and copies ran while one was open for 38% of the time, Pallas kernels for 6%

profile of v1, /device:TPU:0, one launch (start us, length us, event | category | flops | bytes accessed | tf_op | source)
XLA Modules:
  0.0 1273.5 jit_solution(12619148484092767021)
XLA Ops:
  12.2 16.4 %collective-permute-done = bf16[320,1280]{1,0:T(8,128)(2,1)} collective-permute-done((bf16[320,1280]{1,0:T(8,128)(2,1)S(1)}, bf16[320,1280]{1,0:T(8,128)(2,1)}, u32[]{:S(2)}, u32[]{:S(2)}) %collective-permute-start) | collective-permute-done | bytes 819232 | tf_op jit(solution)/shard_map/ppermute | solution.py:210
  34.4 11.7 collective-permute-done.16
  47.6 16.1 %collective-permute-done.12 = bf16[320,1280]{1,0:T(8,128)(2,1)} collective-permute-done((bf16[320,1280]{1,0:T(8,128)(2,1)S(1)}, bf16[320,1280]{1,0:T(8,128)(2,1)}, u32[]{:S(2)}, u32[]{:S(2)}) %collective-permute-start.12) | collective-permute-done | bytes 819232 | tf_op jit(solution)/shard_map/ppermute | solution.py:210
  68.8 11.4 collective-permute-done.4
  162.6 12.4 collective-permute-done.25
  180.0 11.6 collective-permute-done.28
  275.2 30.9 %shard_map.144 = (bf16[512,1280]{1,0:T(8,128)(2,1)}, bf16[512,1280]{1,0:T(8,128)(2,1)}, bf16[512,1280]{1,0:T(8,128)(2,1)S(1)}) custom-call(f32[512,1280]{1,0:T(8,128)S(1)} %fusion.71.qp, f32[512,1280]{1,0:T(8,128)S(1)} %fusion.75.kp, bf16[512,1280]{1,0:T(8,128)(2,1)S(1)} %convolution_convert_fusion.15.v, s32[512,1]{1,0:T(8,128)S(1)} %copy.32.seg_col, ...), custom_call_target="tpu_custom_call" | custom-call | flops 1342177280 | bytes 10485760 | tf_op jit(solution)/shard_map/pallas_call | solution.py:118
  358.8 27.9 %collective-permute-done.36 = bf16[512,1280]{1,0:T(8,128)(2,1)} collective-permute-done((bf16[512,1280]{1,0:T(8,128)(2,1)}, bf16[512,1280]{1,0:T(8,128)(2,1)}, u32[]{:S(2)}, u32[]{:S(2)}) %collective-permute-start.36) | collective-permute-done | bytes 1310752 | tf_op jit(solution)/shard_map/ppermute | solution.py:307
  401.4 30.0 %shard_map.145 = (bf16[512,1280]{1,0:T(8,128)(2,1)S(1)}, bf16[512,1280]{1,0:T(8,128)(2,1)S(1)}, bf16[512,1280]{1,0:T(8,128)(2,1)S(1)}) custom-call(f32[512,1280]{1,0:T(8,128)S(1)} %fusion.70.qp, f32[512,1280]{1,0:T(8,128)S(1)} %fusion.74.kp, bf16[512,1280]{1,0:T(8,128)(2,1)S(1)} %convolution_convert_fusion.14.v, s32[512,1]{1,0:T(8,128)S(1)} %copy.32.seg_col, ...), custom_call_target="tpu_custom_call" | custom-call | flops 1342177280 | bytes 10485760 | tf_op jit(solution)/shard_map/pallas_call | solution.py:118
  487.4 13.0 %multiply_reduce_fusion.2 = (f32[512]{0:T(512)}, f32[512,1280]{1,0:T(8,128)}) fusion(f32[512,1280]{1,0:T(8,128)} %copy-done.16, f32[512,1280]{1,0:T(8,128)} %fusion.32, f32[512,1280]{1,0:T(8,128)} %fusion.92, f32[512,1280]{1,0:T(8,128)} %fusion.93, bf16[1280,1280]{1,0:T(8,128)(2,1)} %constant_dynamic-update-slice_fusion.4, ...), kind=kOutput, calls=%fused_computation.137 | convolution fusion | flops 3365273088 | bytes 23600132 | tf_op jit(solution)/shard_map/dot_general | solution.py:28
  507.3 45.0 %shard_map.146 = (bf16[512,1280]{1,0:T(8,128)(2,1)S(1)}, bf16[512,1280]{1,0:T(8,128)(2,1)S(1)}, bf16[512,1280]{1,0:T(8,128)(2,1)S(1)}) custom-call(bf16[512,1280]{1,0:T(8,128)(2,1)S(1)} %copy-done.13, bf16[512,1280]{1,0:T(8,128)(2,1)S(1)} %copy-done.15, bf16[512,1280]{1,0:T(8,128)(2,1)S(1)} %copy-done.9, ...), custom_call_target="tpu_custom_call" | custom-call | flops 3355443200 | bytes 9175040 | tf_op jit(solution)/shard_map/pallas_call | solution.py:133
  589.1 10.0 collective-permute-done.40
  659.1 45.0 %shard_map.147 = (bf16[512,1280]{1,0:T(8,128)(2,1)S(1)}, bf16[512,1280]{1,0:T(8,128)(2,1)S(1)}, bf16[512,1280]{1,0:T(8,128)(2,1)S(1)}) custom-call(bf16[512,1280]{1,0:T(8,128)(2,1)S(1)} %copy-done.13, bf16[512,1280]{1,0:T(8,128)(2,1)S(1)} %copy-done.15, bf16[512,1280]{1,0:T(8,128)(2,1)S(1)} %copy-done.9, ...), custom_call_target="tpu_custom_call" | custom-call | flops 3355443200 | bytes 9175040 | tf_op jit(solution)/shard_map/pallas_call | solution.py:133
  728.5 59.3 %psum.7 = f32[2,1280]{1,0:T(2,128)S(1)} all-reduce(f32[2,1280]{1,0:T(2,128)S(1)} %pad_maximum_fusion.7), channel_id=1, replica_groups=mesh['section'=2,'tensor'=4,'dp'=4] {'tensor','dp'}, use_global_device_ids=true, to_apply=%region_10.11 | all-reduce | flops 2560 | bytes 20480 | tf_op jit(solution)/shard_map/psum | solution.py:320
  812.6 11.0 constant_dynamic-slice_fusion.20
  828.8 10.9 constant_dynamic-slice_fusion.17
  844.9 10.9 constant_dynamic-slice_fusion.14
  872.4 11.2 constant_dynamic-slice_fusion.11
  961.0 23.6 %collective-permute-done.38 = bf16[512,1280]{1,0:T(8,128)(2,1)S(1)} collective-permute-done((bf16[512,1280]{1,0:T(8,128)(2,1)}, bf16[512,1280]{1,0:T(8,128)(2,1)S(1)}, u32[]{:S(2)}, u32[]{:S(2)}) %collective-permute-start.38) | collective-permute-done | bytes 1310752 | tf_op jit(solution)/shard_map/ppermute | solution.py:210
  1011.3 33.7 %collective-permute-done.73 = bf16[1,320,1280]{2,1,0:T(8,128)(2,1)S(1)} collective-permute-done((bf16[1,320,1280]{2,1,0:T(8,128)(2,1)S(1)}, bf16[1,320,1280]{2,1,0:T(8,128)(2,1)S(1)}, u32[]{:S(2)}, u32[]{:S(2)}) %collective-permute-start.73) | collective-permute-done | bytes 819232 | tf_op jit(solution)/shard_map/ppermute | solution.py:205
  1045.3 17.3 %collective-permute-done.62 = bf16[1,320,1280]{2,1,0:T(8,128)(2,1)S(1)} collective-permute-done((bf16[1,320,1280]{2,1,0:T(8,128)(2,1)S(1)}, bf16[1,320,1280]{2,1,0:T(8,128)(2,1)S(1)}, u32[]{:S(2)}, u32[]{:S(2)}) %collective-permute-start.62) | collective-permute-done | bytes 819232 | tf_op jit(solution)/shard_map/ppermute | solution.py:205
  1062.8 17.3 %collective-permute-done.51 = bf16[1,320,1280]{2,1,0:T(8,128)(2,1)S(1)} collective-permute-done((bf16[1,320,1280]{2,1,0:T(8,128)(2,1)S(1)}, bf16[1,320,1280]{2,1,0:T(8,128)(2,1)S(1)}, u32[]{:S(2)}, u32[]{:S(2)}) %collective-permute-start.51) | collective-permute-done | bytes 819232 | tf_op jit(solution)/shard_map/ppermute | solution.py:205
  1085.9 17.7 %collective-permute-done.74 = bf16[320,1280]{1,0:T(8,128)(2,1)S(1)} collective-permute-done((bf16[320,1280]{1,0:T(8,128)(2,1)S(1)}, bf16[320,1280]{1,0:T(8,128)(2,1)S(1)}, u32[]{:S(2)}, u32[]{:S(2)}) %collective-permute-start.74) | collective-permute-done | bytes 819232 | tf_op jit(solution)/shard_map/ppermute | solution.py:210
  1104.0 10.7 collective-permute-done.49
  1123.6 15.0 %collective-permute-done.63 = bf16[320,1280]{1,0:T(8,128)(2,1)S(1)} collective-permute-done((bf16[320,1280]{1,0:T(8,128)(2,1)S(1)}, bf16[320,1280]{1,0:T(8,128)(2,1)S(1)}, u32[]{:S(2)}, u32[]{:S(2)}) %collective-permute-start.63) | collective-permute-done | bytes 819232 | tf_op jit(solution)/shard_map/ppermute | solution.py:210
  1138.9 27.8 %collective-permute-done.43 = bf16[512,1280]{1,0:T(8,128)(2,1)S(1)} collective-permute-done((bf16[512,1280]{1,0:T(8,128)(2,1)S(1)}, bf16[512,1280]{1,0:T(8,128)(2,1)S(1)}, u32[]{:S(2)}, u32[]{:S(2)}) %collective-permute-start.43) | collective-permute-done | bytes 1310752 | tf_op jit(solution)/shard_map/ppermute | solution.py:210
  1170.2 14.1 %collective-permute-done.53 = bf16[320,1280]{1,0:T(8,128)(2,1)S(1)} collective-permute-done((bf16[320,1280]{1,0:T(8,128)(2,1)S(1)}, bf16[320,1280]{1,0:T(8,128)(2,1)S(1)}, u32[]{:S(2)}, u32[]{:S(2)}) %collective-permute-start.53) | collective-permute-done | bytes 819232 | tf_op jit(solution)/shard_map/ppermute | solution.py:210
  1186.7 15.2 %collective-permute-done.75 = bf16[320,1280]{1,0:T(8,128)(2,1)S(1)} collective-permute-done((bf16[320,1280]{1,0:T(8,128)(2,1)S(1)}, bf16[320,1280]{1,0:T(8,128)(2,1)S(1)}, u32[]{:S(2)}, u32[]{:S(2)}) %collective-permute-start.75) | collective-permute-done | bytes 819232 | tf_op jit(solution)/shard_map/ppermute | solution.py:210
  1205.1 14.3 %collective-permute-done.64 = bf16[320,1280]{1,0:T(8,128)(2,1)S(1)} collective-permute-done((bf16[320,1280]{1,0:T(8,128)(2,1)S(1)}, bf16[320,1280]{1,0:T(8,128)(2,1)S(1)}, u32[]{:S(2)}, u32[]{:S(2)}) %collective-permute-start.64) | collective-permute-done | bytes 819232 | tf_op jit(solution)/shard_map/ppermute | solution.py:210
  1220.6 16.3 %collective-permute-done.54 = bf16[320,1280]{1,0:T(8,128)(2,1)S(1)} collective-permute-done((bf16[320,1280]{1,0:T(8,128)(2,1)S(1)}, bf16[320,1280]{1,0:T(8,128)(2,1)S(1)}, u32[]{:S(2)}, u32[]{:S(2)}) %collective-permute-start.54) | collective-permute-done | bytes 819232 | tf_op jit(solution)/shard_map/ppermute | solution.py:210
  1241.6 13.1 %collective-permute-done.76 = bf16[320,1280]{1,0:T(8,128)(2,1)} collective-permute-done((bf16[320,1280]{1,0:T(8,128)(2,1)}, bf16[320,1280]{1,0:T(8,128)(2,1)}, u32[]{:S(2)}, u32[]{:S(2)}) %collective-permute-start.76) | collective-permute-done | bytes 819232 | tf_op jit(solution)/shard_map/ppermute | solution.py:210
  1257.8 12.5 collective-permute-done.65
  (560 shorter events, 637.5 us)
Async XLA Ops:
  11.7 52.0 %collective-permute-start.12 = (bf16[320,1280]{1,0:T(8,128)(2,1)S(1)}, bf16[320,1280]{1,0:T(8,128)(2,1)}, u32[]{:S(2)}, u32[]{:S(2)}) collective-permute-start(bf16[320,1280]{1,0:T(8,128)(2,1)S(1)} %dynamic-slice_bitcast_fusion.9), channel_id=1, source_target_pairs={{0,12},{4,0},{8,4},{12,8},{1,13},{5,1},{9,5},{13,9},{2,14},{6,2},{... | collective-permute-start | bytes 2457608 | tf_op jit(solution)/shard_map/ppermute | solution.py:210
  30.1 38.5 %collective-permute-start.2 = (bf16[320,1280]{1,0:T(8,128)(2,1)}, bf16[320,1280]{1,0:T(8,128)(2,1)}, u32[]{:S(2)}, u32[]{:S(2)}) collective-permute-start(bf16[320,1280]{1,0:T(8,128)(2,1)} %collective-permute-done), channel_id=1, source_target_pairs={{0,1},{1,0},{2,3},{3,2},{4,5},{5,4},{6,7},{7,6},{8,9},{9,8},{10,11... | collective-permute-start | bytes 2457608 | tf_op jit(solution)/shard_map/ppermute | solution.py:205
  30.1 50.1 %collective-permute-start.4 = (bf16[320,1280]{1,0:T(8,128)(2,1)}, bf16[320,1280]{1,0:T(8,128)(2,1)}, u32[]{:S(2)}, u32[]{:S(2)}) collective-permute-start(bf16[320,1280]{1,0:T(8,128)(2,1)} %collective-permute-done), channel_id=1, source_target_pairs={{0,12},{4,0},{8,4},{12,8},{1,13},{5,1},{9,5},{13,9},{2,14},{6,2},{... | collective-permute-start | bytes 2457608 | tf_op jit(solution)/shard_map/ppermute | solution.py:210
  46.1 57.3 %collective-permute-start.17 = (bf16[320,1280]{1,0:T(8,128)(2,1)}, bf16[320,1280]{1,0:T(8,128)(2,1)}, u32[]{:S(2)}, u32[]{:S(2)}) collective-permute-start(bf16[320,1280]{1,0:T(8,128)(2,1)} %collective-permute-done.16), channel_id=1, source_target_pairs={{0,2},{1,3},{2,0},{3,1},{4,6},{5,7},{6,4},{7,5},{8,10},{9,11},{10,... | collective-permute-start | bytes 2457608 | tf_op jit(solution)/shard_map/ppermute | solution.py:205
  63.7 43.8 %collective-permute-start.18 = (bf16[320,1280]{1,0:T(8,128)(2,1)}, bf16[320,1280]{1,0:T(8,128)(2,1)}, u32[]{:S(2)}, u32[]{:S(2)}) collective-permute-start(bf16[320,1280]{1,0:T(8,128)(2,1)} %collective-permute-done.16), channel_id=1, source_target_pairs={{0,1},{1,0},{2,3},{3,2},{4,5},{5,4},{6,7},{7,6},{8,9},{9,8},{10,11... | collective-permute-start | bytes 2457608 | tf_op jit(solution)/shard_map/ppermute | solution.py:205
  66.5 49.8 %collective-permute-start.13 = (bf16[320,1280]{1,0:T(8,128)(2,1)}, bf16[320,1280]{1,0:T(8,128)(2,1)}, u32[]{:S(2)}, u32[]{:S(2)}) collective-permute-start(bf16[320,1280]{1,0:T(8,128)(2,1)} %collective-permute-done.12), channel_id=1, source_target_pairs={{0,2},{1,3},{2,0},{3,1},{4,6},{5,7},{6,4},{7,5},{8,10},{9,11},{10,... | collective-permute-start | bytes 2457608 | tf_op jit(solution)/shard_map/ppermute | solution.py:205
  68.5 51.3 %collective-permute-start.14 = (bf16[320,1280]{1,0:T(8,128)(2,1)}, bf16[320,1280]{1,0:T(8,128)(2,1)}, u32[]{:S(2)}, u32[]{:S(2)}) collective-permute-start(bf16[320,1280]{1,0:T(8,128)(2,1)} %collective-permute-done.12), channel_id=1, source_target_pairs={{0,1},{1,0},{2,3},{3,2},{4,5},{5,4},{6,7},{7,6},{8,9},{9,8},{10,11... | collective-permute-start | bytes 2457608 | tf_op jit(solution)/shard_map/ppermute | solution.py:205
  80.2 39.9 %collective-permute-start.20 = (bf16[320,1280]{1,0:T(8,128)(2,1)}, bf16[320,1280]{1,0:T(8,128)(2,1)}, u32[]{:S(2)}, u32[]{:S(2)}) collective-permute-start(bf16[320,1280]{1,0:T(8,128)(2,1)} %collective-permute-done.12), channel_id=1, source_target_pairs={{0,12},{4,0},{8,4},{12,8},{1,13},{5,1},{9,5},{13,9},{2,14},{6,2},{... | collective-permute-start | bytes 2457608 | tf_op jit(solution)/shard_map/ppermute | solution.py:210
  178.6 42.0 %collective-permute-start.23 = (bf16[320,1280]{1,0:T(8,128)(2,1)}, bf16[320,1280]{1,0:T(8,128)(2,1)}, u32[]{:S(2)}, u32[]{:S(2)}) collective-permute-start(bf16[320,1280]{1,0:T(8,128)(2,1)} %collective-permute-done.21), channel_id=1, source_target_pairs={{0,1},{1,0},{2,3},{3,2},{4,5},{5,4},{6,7},{7,6},{8,9},{9,8},{10,11... | collective-permute-start | bytes 2457608 | tf_op jit(solution)/shard_map/ppermute | solution.py:205
  199.7 46.1 %collective-permute-start.10 = (bf16[320,1280]{1,0:T(8,128)(2,1)}, bf16[320,1280]{1,0:T(8,128)(2,1)}, u32[]{:S(2)}, u32[]{:S(2)}) collective-permute-start(bf16[320,1280]{1,0:T(8,128)(2,1)} %collective-permute-done.8), channel_id=1, source_target_pairs={{0,1},{1,0},{2,3},{3,2},{4,5},{5,4},{6,7},{7,6},{8,9},{9,8},{10,11... | collective-permute-start | bytes 2457608 | tf_op jit(solution)/shard_map/ppermute | solution.py:205
  199.8 51.3 %collective-permute-start.27 = (bf16[320,1280]{1,0:T(8,128)(2,1)}, bf16[320,1280]{1,0:T(8,128)(2,1)}, u32[]{:S(2)}, u32[]{:S(2)}) collective-permute-start(bf16[320,1280]{1,0:T(8,128)(2,1)} %collective-permute-done.25), channel_id=1, source_target_pairs={{0,1},{1,0},{2,3},{3,2},{4,5},{5,4},{6,7},{7,6},{8,9},{9,8},{10,11... | collective-permute-start | bytes 2457608 | tf_op jit(solution)/shard_map/ppermute | solution.py:205
  245.9 84.9 %collective-permute-start.35 = (bf16[320,1280]{1,0:T(8,128)(2,1)}, bf16[320,1280]{1,0:T(8,128)(2,1)}, u32[]{:S(2)}, u32[]{:S(2)}) collective-permute-start(bf16[320,1280]{1,0:T(8,128)(2,1)} %collective-permute-done.33), channel_id=1, source_target_pairs={{0,1},{1,0},{2,3},{3,2},{4,5},{5,4},{6,7},{7,6},{8,9},{9,8},{10,11... | collective-permute-start | bytes 2457608 | tf_op jit(solution)/shard_map/ppermute | solution.py:205
  251.2 91.5 %collective-permute-start.31 = (bf16[320,1280]{1,0:T(8,128)(2,1)}, bf16[320,1280]{1,0:T(8,128)(2,1)}, u32[]{:S(2)}, u32[]{:S(2)}) collective-permute-start(bf16[320,1280]{1,0:T(8,128)(2,1)} %collective-permute-done.29), channel_id=1, source_target_pairs={{0,1},{1,0},{2,3},{3,2},{4,5},{5,4},{6,7},{7,6},{8,9},{9,8},{10,11... | collective-permute-start | bytes 2457608 | tf_op jit(solution)/shard_map/ppermute | solution.py:205
  586.6 366.7 %collective-permute-start.37 = (bf16[512,1280]{1,0:T(8,128)(2,1)}, bf16[512,1280]{1,0:T(8,128)(2,1)}, u32[]{:S(2)}, u32[]{:S(2)}) collective-permute-start(bf16[512,1280]{1,0:T(8,128)(2,1)} %get-tuple-element.84), channel_id=1, source_target_pairs={{0,12},{4,0},{8,4},{12,8},{1,13},{5,1},{9,5},{13,9},{2,14},{6,2},{... | collective-permute-start | bytes 3932168 | tf_op jit(solution)/shard_map/ppermute | solution.py:210
  791.4 194.4 %collective-permute-start.66 = (bf16[2,320,1280]{2,1,0:T(8,128)(2,1)}, bf16[2,320,1280]{2,1,0:T(8,128)(2,1)}, u32[]{:S(2)}, u32[]{:S(2)}) collective-permute-start(bf16[2,320,1280]{2,1,0:T(8,128)(2,1)} %dynamic-slice_bitcast_fusion.3), channel_id=1, source_target_pairs={{0,1},{1,0},{2,3},{3,2},{4,5},{5,4},{6,7},{7,6},{8,9},{9,8},{10,11... | collective-permute-start | bytes 4915208 | tf_op jit(solution)/shard_map/ppermute | solution.py:205
  794.2 195.3 %collective-permute-start.68 = (bf16[2,320,1280]{2,1,0:T(8,128)(2,1)}, bf16[2,320,1280]{2,1,0:T(8,128)(2,1)}, u32[]{:S(2)}, u32[]{:S(2)}) collective-permute-start(bf16[2,320,1280]{2,1,0:T(8,128)(2,1)} %dynamic-slice_bitcast_fusion.2), channel_id=1, source_target_pairs={{0,1},{1,0},{2,3},{3,2},{4,5},{5,4},{6,7},{7,6},{8,9},{9,8},{10,11... | collective-permute-start | bytes 4915208 | tf_op jit(solution)/shard_map/ppermute | solution.py:205
  796.1 195.7 %collective-permute-start.70 = (bf16[2,320,1280]{2,1,0:T(8,128)(2,1)}, bf16[2,320,1280]{2,1,0:T(8,128)(2,1)}, u32[]{:S(2)}, u32[]{:S(2)}) collective-permute-start(bf16[2,320,1280]{2,1,0:T(8,128)(2,1)} %dynamic-slice_bitcast_fusion.1), channel_id=1, source_target_pairs={{0,1},{1,0},{2,3},{3,2},{4,5},{5,4},{6,7},{7,6},{8,9},{9,8},{10,11... | collective-permute-start | bytes 4915208 | tf_op jit(solution)/shard_map/ppermute | solution.py:205
  869.6 88.4 %collective-permute-start.41 = (bf16[512,1280]{1,0:T(8,128)(2,1)}, bf16[512,1280]{1,0:T(8,128)(2,1)}, u32[]{:S(2)}, u32[]{:S(2)}) collective-permute-start(bf16[512,1280]{1,0:T(8,128)(2,1)} %get-tuple-element.41), channel_id=1, source_target_pairs={{0,12},{4,0},{8,4},{12,8},{1,13},{5,1},{9,5},{13,9},{2,14},{6,2},{... | collective-permute-start | bytes 3932168 | tf_op jit(solution)/shard_map/ppermute | solution.py:210
  1002.4 78.0 %collective-permute-start.42 = (bf16[512,1280]{1,0:T(8,128)(2,1)}, bf16[512,1280]{1,0:T(8,128)(2,1)S(1)}, u32[]{:S(2)}, u32[]{:S(2)}) collective-permute-start(bf16[512,1280]{1,0:T(8,128)(2,1)} %collective-permute-done.41), channel_id=1, source_target_pairs={{0,12},{4,0},{8,4},{12,8},{1,13},{5,1},{9,5},{13,9},{2,14},{6,2},{... | collective-permute-start | bytes 3932168 | tf_op jit(solution)/shard_map/ppermute | solution.py:210
  1004.9 78.1 %collective-permute-start.39 = (bf16[512,1280]{1,0:T(8,128)(2,1)S(1)}, bf16[512,1280]{1,0:T(8,128)(2,1)S(1)}, u32[]{:S(2)}, u32[]{:S(2)}) collective-permute-start(bf16[512,1280]{1,0:T(8,128)(2,1)S(1)} %collective-permute-done.38), channel_id=1, source_target_pairs={{0,12},{4,0},{8,4},{12,8},{1,13},{5,1},{9,5},{13,9},{2,14},{6,2},{... | collective-permute-start | bytes 3932168 | tf_op jit(solution)/shard_map/ppermute | solution.py:210
  1006.3 78.1 %collective-permute-start.71 = (bf16[1,320,1280]{2,1,0:T(8,128)(2,1)S(1)}, bf16[1,320,1280]{2,1,0:T(8,128)(2,1)S(1)}, u32[]{:S(2)}, u32[]{:S(2)}) collective-permute-start(bf16[1,320,1280]{2,1,0:T(8,128)(2,1)S(1)} %constant_dynamic-slice_fusion.2), channel_id=1, source_target_pairs={{0,2},{1,3},{2,0},{3,1},{4,6},{5,7},{6,4},{7,5},{8,10},{9,11},{10,... | collective-permute-start | bytes 2457608 | tf_op jit(solution)/shard_map/ppermute | solution.py:205
  1009.4 53.2 %collective-permute-start.62 = (bf16[1,320,1280]{2,1,0:T(8,128)(2,1)S(1)}, bf16[1,320,1280]{2,1,0:T(8,128)(2,1)S(1)}, u32[]{:S(2)}, u32[]{:S(2)}) collective-permute-start(bf16[1,320,1280]{2,1,0:T(8,128)(2,1)S(1)} %constant_dynamic-slice_fusion.5), channel_id=1, source_target_pairs={{0,2},{1,3},{2,0},{3,1},{4,6},{5,7},{6,4},{7,5},{8,10},{9,11},{10,... | collective-permute-start | bytes 2457608 | tf_op jit(solution)/shard_map/ppermute | solution.py:205
  1062.6 60.9 %collective-permute-start.60 = (bf16[1,320,1280]{2,1,0:T(8,128)(2,1)S(1)}, bf16[1,320,1280]{2,1,0:T(8,128)(2,1)S(1)}, u32[]{:S(2)}, u32[]{:S(2)}) collective-permute-start(bf16[1,320,1280]{2,1,0:T(8,128)(2,1)S(1)} %constant_dynamic-slice_fusion.6), channel_id=1, source_target_pairs={{0,2},{1,3},{2,0},{3,1},{4,6},{5,7},{6,4},{7,5},{8,10},{9,11},{10,... | collective-permute-start | bytes 2457608 | tf_op jit(solution)/shard_map/ppermute | solution.py:205
  1083.1 38.1 %collective-permute-start.52 = (bf16[320,1280]{1,0:T(8,128)(2,1)S(1)}, bf16[320,1280]{1,0:T(8,128)(2,1)S(1)}, u32[]{:S(2)}, u32[]{:S(2)}) collective-permute-start(bf16[320,1280]{1,0:T(8,128)(2,1)S(1)} %fusion.97), channel_id=1, source_target_pairs={{0,4},{4,8},{8,12},{12,0},{1,5},{5,9},{9,13},{13,1},{2,6},{6,10},{... | collective-permute-start | bytes 2457608 | tf_op jit(solution)/shard_map/ppermute | solution.py:210
  1084.4 54.2 %collective-permute-start.63 = (bf16[320,1280]{1,0:T(8,128)(2,1)S(1)}, bf16[320,1280]{1,0:T(8,128)(2,1)S(1)}, u32[]{:S(2)}, u32[]{:S(2)}) collective-permute-start(bf16[320,1280]{1,0:T(8,128)(2,1)S(1)} %fusion.101), channel_id=1, source_target_pairs={{0,4},{4,8},{8,12},{12,0},{1,5},{5,9},{9,13},{13,1},{2,6},{6,10},{... | collective-permute-start | bytes 2457608 | tf_op jit(solution)/shard_map/ppermute | solution.py:210
  1103.6 63.1 %collective-permute-start.43 = (bf16[512,1280]{1,0:T(8,128)(2,1)S(1)}, bf16[512,1280]{1,0:T(8,128)(2,1)S(1)}, u32[]{:S(2)}, u32[]{:S(2)}) collective-permute-start(bf16[512,1280]{1,0:T(8,128)(2,1)S(1)} %collective-permute-done.42), channel_id=1, source_target_pairs={{0,12},{4,0},{8,4},{12,8},{1,13},{5,1},{9,5},{13,9},{2,14},{6,2},{... | collective-permute-start | bytes 3932168 | tf_op jit(solution)/shard_map/ppermute | solution.py:210
  1114.7 126.9 %collective-permute-start.67 = (bf16[1,320,1280]{2,1,0:T(8,128)(2,1)}, bf16[1,320,1280]{2,1,0:T(8,128)(2,1)}, u32[]{:S(2)}, u32[]{:S(2)}) collective-permute-start(bf16[1,320,1280]{2,1,0:T(8,128)(2,1)} %constant_dynamic-slice_fusion.4), channel_id=1, source_target_pairs={{0,2},{1,3},{2,0},{3,1},{4,6},{5,7},{6,4},{7,5},{8,10},{9,11},{10,... | collective-permute-start | bytes 2457608 | tf_op jit(solution)/shard_map/ppermute | solution.py:205
  1121.2 63.4 %collective-permute-start.69 = (bf16[1,320,1280]{2,1,0:T(8,128)(2,1)S(1)}, bf16[1,320,1280]{2,1,0:T(8,128)(2,1)S(1)}, u32[]{:S(2)}, u32[]{:S(2)}) collective-permute-start(bf16[1,320,1280]{2,1,0:T(8,128)(2,1)S(1)} %constant_dynamic-slice_fusion.3), channel_id=1, source_target_pairs={{0,2},{1,3},{2,0},{3,1},{4,6},{5,7},{6,4},{7,5},{8,10},{9,11},{10,... | collective-permute-start | bytes 2457608 | tf_op jit(solution)/shard_map/ppermute | solution.py:205
  1123.5 46.2 %collective-permute-start.47 = (bf16[1,320,1280]{2,1,0:T(8,128)(2,1)S(1)}, bf16[1,320,1280]{2,1,0:T(8,128)(2,1)S(1)}, u32[]{:S(2)}, u32[]{:S(2)}) collective-permute-start(bf16[1,320,1280]{2,1,0:T(8,128)(2,1)S(1)} %constant_dynamic-slice_fusion.15), channel_id=1, source_target_pairs={{0,2},{1,3},{2,0},{3,1},{4,6},{5,7},{6,4},{7,5},{8,10},{9,11},{10,... | collective-permute-start | bytes 2457608 | tf_op jit(solution)/shard_map/ppermute | solution.py:205
  1138.6 45.7 %collective-permute-start.53 = (bf16[320,1280]{1,0:T(8,128)(2,1)S(1)}, bf16[320,1280]{1,0:T(8,128)(2,1)S(1)}, u32[]{:S(2)}, u32[]{:S(2)}) collective-permute-start(bf16[320,1280]{1,0:T(8,128)(2,1)S(1)} %fusion.82), channel_id=1, source_target_pairs={{0,4},{4,8},{8,12},{12,0},{1,5},{5,9},{9,13},{13,1},{2,6},{6,10},{... | collective-permute-start | bytes 2457608 | tf_op jit(solution)/shard_map/ppermute | solution.py:210
  1203.1 54.8 %collective-permute-start.56 = (bf16[1,320,1280]{2,1,0:T(8,128)(2,1)}, bf16[1,320,1280]{2,1,0:T(8,128)(2,1)}, u32[]{:S(2)}, u32[]{:S(2)}) collective-permute-start(bf16[1,320,1280]{2,1,0:T(8,128)(2,1)} %constant_dynamic-slice_fusion.8), channel_id=1, source_target_pairs={{0,2},{1,3},{2,0},{3,1},{4,6},{5,7},{6,4},{7,5},{8,10},{9,11},{10,... | collective-permute-start | bytes 2457608 | tf_op jit(solution)/shard_map/ppermute | solution.py:205
  1220.6 49.7 %collective-permute-start.65 = (bf16[320,1280]{1,0:T(8,128)(2,1)}, bf16[320,1280]{1,0:T(8,128)(2,1)}, u32[]{:S(2)}, u32[]{:S(2)}) collective-permute-start(bf16[320,1280]{1,0:T(8,128)(2,1)} %fusion.80), channel_id=1, source_target_pairs={{0,4},{4,8},{8,12},{12,0},{1,5},{5,9},{9,13},{13,1},{2,6},{6,10},{... | collective-permute-start | bytes 2457608 | tf_op jit(solution)/shard_map/ppermute | solution.py:210
  (155 other events, 2140.6 us)

commit v2 on v1

--- a/solution.py
+++ b/solution.py
@@ -18,6 +18,7 @@
 SCALE = 1.0 / math.sqrt(HEAD_SIZE)
 BF16 = jnp.bfloat16
 F32 = jnp.float32
+MESH = pl.DeviceIdType.MESH
 
 
 def dot_nn(a, b):
@@ -48,58 +49,72 @@
     return jnp.where(first, pltpu.roll(x, width - HALF, 1), pltpu.roll(x, HALF, 1))
 
 
-def block_mask(i, seg_col, seg_row, obs_row):
-    k0 = max(i - 1, 0) * QB
-    k1 = (i + 1) * QB
-    shape = (QB, k1 - k0)
-    qi = lax.broadcasted_iota(jnp.int32, shape, 0) + i * QB
-    kj = lax.broadcasted_iota(jnp.int32, shape, 1) + k0
-    same = seg_col[i * QB:(i + 1) * QB, :] == seg_row[:, k0:k1]
-    seen = (obs_row[:, k0:k1] == 1) | (kj == qi)
-    return k0, k1, same & (kj <= qi) & seen
-
-
-def softmax_block(q, k, allowed):
-    s = jnp.where(allowed, dot_nt(q, k) * SCALE, -BIG)
+def windows():
+    return [max(i - 1, 0) * QB for i in range(ROW // QB)]
+
+
+def write_mask(mask, seg_col, seg_row, obs_row):
+    for i, k0 in enumerate(windows()):
+        r = slice(i * QB, (i + 1) * QB)
+        shape = (QB, 2 * QB)
+        qi = lax.broadcasted_iota(jnp.int32, shape, 0) + i * QB
+        kj = lax.broadcasted_iota(jnp.int32, shape, 1) + k0
+        same = seg_col[r, :] == seg_row[:, k0:k0 + 2 * QB]
+        seen = (obs_row[:, k0:k0 + 2 * QB] == 1) | (kj == qi)
+        mask[r, :] = (same & (kj <= qi) & seen).astype(F32)
+
+
+def by_block(dot, left, right):
+    return jnp.concatenate(
+        [dot(left[i * QB:(i + 1) * QB], right[k0:k0 + 2 * QB]) for i, k0 in enumerate(windows())], axis=0
+    )
+
+
+def by_window(left, right):
+    n = ROW // QB
+    blocks = [None] * n
+    for i, k0 in enumerate(windows()):
+        r = slice(i * QB, (i + 1) * QB)
+        term = dot_tn(left[r], right[r])
+        for j in range(2):
+            at, part = k0 // QB + j, term[j * QB:(j + 1) * QB]
+            blocks[at] = part if blocks[at] is None else blocks[at] + part
+    return jnp.concatenate(blocks, axis=0)
+
+
+def probabilities(q, k, mask):
+    s = jnp.where(mask[...] > 0, by_block(dot_nt, q, k) * SCALE, -BIG)
     e = jnp.exp(s - jnp.max(s, axis=1, keepdims=True))
     return e * (1.0 / jnp.sum(e, axis=1, keepdims=True))
 
 
-def attn_fwd_kernel(qp, kp, v, seg_col, seg_row, obs_row, cos, sin, q_out, k_out, o_out):
+def attn_fwd_kernel(qp, kp, v, seg_col, seg_row, obs_row, cos, sin, q_out, k_out, o_out, mask):
     x = qp[...]
     q_out[...] = (x * cos[...] + partner(x) * sin[...]).astype(BF16)
     x = kp[...]
     k_out[...] = (x * cos[...] + partner(x) * sin[...]).astype(BF16)
-    sc, sr, ob = seg_col[...], seg_row[...], obs_row[...]
-    for i in range(ROW // QB):
-        k0, k1, allowed = block_mask(i, sc, sr, ob)
-        for h in range(GROUP):
-            c0, c1 = h * HEAD_SIZE, (h + 1) * HEAD_SIZE
-            p = softmax_block(q_out[i * QB:(i + 1) * QB, c0:c1], k_out[k0:k1, c0:c1], allowed)
-            o_out[i * QB:(i + 1) * QB, c0:c1] = dot_nn(p.astype(BF16), v[k0:k1, c0:c1]).astype(BF16)
-
-
-def attn_bwd_kernel(q, k, v, do, seg_col, seg_row, obs_row, cos, sin, dqp, dkp, dv, dq_s, dk_s, dv_s):
-    dk_s[...] = jnp.zeros_like(dk_s)
-    dv_s[...] = jnp.zeros_like(dv_s)
-    sc, sr, ob = seg_col[...], seg_row[...], obs_row[...]
-    for i in range(ROW // QB):
-        k0, k1, allowed = block_mask(i, sc, sr, ob)
-        r0, r1 = i * QB, (i + 1) * QB
-        for h in range(GROUP):
-            c0, c1 = h * HEAD_SIZE, (h + 1) * HEAD_SIZE
-            qi, ki, vi, di = q[r0:r1, c0:c1], k[k0:k1, c0:c1], v[k0:k1, c0:c1], do[r0:r1, c0:c1]
-            p = softmax_block(qi, ki, allowed)
-            dv_s[k0:k1, c0:c1] += dot_tn(p.astype(BF16), di)
-            dp = dot_nt(di, vi)
-            ds = (p * (dp - jnp.sum(p * dp, axis=1, keepdims=True))).astype(BF16)
-            dq_s[r0:r1, c0:c1] = dot_nn(ds, ki) * SCALE
-            dk_s[k0:k1, c0:c1] += dot_tn(ds, qi) * SCALE
+    write_mask(mask, seg_col, seg_row, obs_row)
+    for h in range(GROUP):
+        c = slice(h * HEAD_SIZE, (h + 1) * HEAD_SIZE)
+        p = probabilities(q_out[:, c], k_out[:, c], mask).astype(BF16)
+        o_out[:, c] = by_block(dot_nn, p, v[:, c]).astype(BF16)
+
+
+def attn_bwd_kernel(q, k, v, do, seg_col, seg_row, obs_row, cos, sin, dqp, dkp, dv, dq_s, dk_s, mask):
+    write_mask(mask, seg_col, seg_row, obs_row)
+    for h in range(GROUP):
+        c = slice(h * HEAD_SIZE, (h + 1) * HEAD_SIZE)
+        qh, kh, vh, dh = q[:, c], k[:, c], v[:, c], do[:, c]
+        p = probabilities(qh, kh, mask)
+        dv[:, c] = by_window(p.astype(BF16), dh).astype(BF16)
+        dp = by_block(dot_nt, dh, vh)
+        ds = (p * (dp - jnp.sum(p * dp, axis=1, keepdims=True))).astype(BF16)
+        dq_s[:, c] = by_block(dot_nn, ds, kh) * SCALE
+        dk_s[:, c] = by_window(ds, qh) * SCALE
     x = dq_s[...]
     dqp[...] = (x * cos[...] - partner(x) * sin[...]).astype(BF16)
     x = dk_s[...]
     dkp[...] = (x * cos[...] - partner(x) * sin[...]).astype(BF16)
-    dv[...] = dv_s[...].astype(BF16)
 
 
 def attn_specs(hd, rows):
@@ -121,6 +136,7 @@
         in_specs=[wide, wide, wide, col, row, row, table, table],
         out_specs=[wide, wide, wide],
         out_shape=[out, out, out],
+        scratch_shapes=[pltpu.VMEM((ROW, 2 * QB), F32)],
         compiler_params=pltpu.CompilerParams(vmem_limit_bytes=40 * 2**20),
         cost_estimate=pl.CostEstimate(flops=rows * hd * 2048, bytes_accessed=rows * hd * 16, transcendentals=rows * 4096),
     )(qp, kp, v, seg[:, None], seg[None, :], obs[None, :], *tables)
@@ -136,7 +152,7 @@
         in_specs=[wide, wide, wide, wide, col, row, row, table, table],
         out_specs=[wide, wide, wide],
         out_shape=[out, out, out],
-        scratch_shapes=[pltpu.VMEM((ROW, width), F32)] * 3,
+        scratch_shapes=[pltpu.VMEM((ROW, width), F32)] * 2 + [pltpu.VMEM((ROW, 2 * QB), F32)],
         compiler_params=pltpu.CompilerParams(vmem_limit_bytes=40 * 2**20),
         cost_estimate=pl.CostEstimate(flops=rows * hd * 5120, bytes_accessed=rows * hd * 14, transcendentals=rows * 4096),
     )(q, k, v, do, seg[:, None], seg[None, :], obs[None, :], *tables)
@@ -196,78 +212,468 @@
     return dh, (g_attn, g_in, g_down, gain_terms)
 
 
-def bits_of(n):
+def ring_bits(n):
     return [1 << i for i in range(n.bit_length() - 1)]
 
 
-def swap(x, axis, bit):
-    n = lax.axis_size(axis)
-    return lax.ppermute(x, axis, [(i, i ^ bit) for i in range(n)])
+def low_bit(j):
+    return j & -j
+
+
+class Links:
+    def __init__(self, n_dp, n_t):
+        self.n_dp, self.n_t = n_dp, n_t
+        self.me, self.z = lax.axis_index("dp"), lax.axis_index("tensor")
+        self.down = lax.rem(self.z + n_t - 1, n_t)
+        self.up = lax.rem(self.z + 1, n_t)
+        self.bits = ring_bits(n_dp)
+        self.sent = {}
+
+    def flip(self, bit):
+        return self.me + bit - 2 * bit * lax.rem(self.me // bit, 2)
+
+    def mix(self, j):
+        at = self.me
+        for bit in self.bits:
+            if j & bit:
+                at = at + bit - 2 * bit * lax.rem(self.me // bit, 2)
+        return at
+
+    def own_bit(self, bit):
+        return lax.rem(self.me // bit, 2)
+
+    def greet(self, axes):
+        barrier = pltpu.get_barrier_semaphore()
+        for where in axes:
+            pl.semaphore_signal(barrier, inc=1, device_id=where, device_id_type=MESH)
+        pl.semaphore_wait(barrier, len(axes))
+
+    def send(self, src, dst, send_sem, recv_sem, where, tag=None):
+        copy = pltpu.make_async_remote_copy(
+            src_ref=src, dst_ref=dst, send_sem=send_sem, recv_sem=recv_sem, device_id=where, device_id_type=MESH
+        )
+        copy.start()
+        self.sent.setdefault(tag, []).append(copy)
+
+    def finish(self, tag):
+        for copy in self.sent.pop(tag, ()):
+            copy.wait_send()
+
+    def arrived(self, ref, sem, send_sem, where):
+        pltpu.make_async_remote_copy(
+            src_ref=ref, dst_ref=ref, send_sem=send_sem, recv_sem=sem, device_id=where, device_id_type=MESH
+        ).wait_recv()
+
+    def drain(self):
+        for tag in list(self.sent):
+            self.finish(tag)
+
+
+class Gather:
+    def __init__(self, links, own, full, z_send, z_recv, p_send, p_recv):
+        self.l, self.own, self.full = links, own, full
+        self.z_send, self.z_recv, self.p_send, self.p_recv = z_send, z_recv, p_send, p_recv
+        self.rows = own[0].shape[0] // links.n_dp
+        self.split, self.units = gather_units(self.rows, links.n_t)
+        self.part = self.rows // self.split
+        self.at = {u: i for i, u in enumerate(self.units)}
+        self.next = 0
+
+    def piece(self, m, slot, index, h):
+        first = pl.multiple_of(index * self.rows + h * self.part, 16)
+        if slot == 0:
+            return self.own[m].at[pl.ds(first, self.part), :]
+        return self.full.at[m, slot, pl.ds(first, self.part), :]
+
+    def send_z(self, i):
+        m, k, h = self.units[i]
+        l = self.l
+        l.send(self.piece(m, k - 1, l.me, h), self.piece(m, k, l.me, h), self.z_send.at[i], self.z_recv.at[i], {"tensor": l.down})
+
+    def advance(self, seen, ahead=3):
+        while self.next < len(self.units) and self.next <= seen + ahead:
+            m, k, h = self.units[self.next]
+            if k > 1 and self.at[(m, k - 1, h)] > seen:
+                break
+            self.send_z(self.next)
+            self.next += 1
+
+    def share(self, i, j):
+        m, k, h = self.units[i]
+        l = self.l
+        for bit in reversed(l.bits):
+            if j == 0 or bit < low_bit(j):
+                ref = self.piece(m, k, l.mix(j), h)
+                l.send(ref, ref, self.p_send.at[i, j ^ bit], self.p_recv.at[i, j ^ bit], {"dp": l.flip(bit)})
+
+    def take(self, i):
+        m, k, h = self.units[i]
+        l = self.l
+        l.arrived(self.piece(m, k, l.me, h), self.z_recv.at[i], self.z_send.at[i], {"tensor": l.up})
+        self.advance(i)
+        self.share(i, 0)
+
+    def order(self):
+        return sorted(range(1, self.l.n_dp), key=lambda j: (-low_bit(j), j))
+
+    def relay(self, i):
+        m, k, h = self.units[i]
+        l = self.l
+        for j in self.order():
+            l.arrived(self.piece(m, k, l.mix(j), h), self.p_recv.at[i, j], self.p_send.at[i, j], {"dp": l.flip(low_bit(j))})
+            self.share(i, j)
+
+
+def gather_units(rows, n_t):
+    split = 2 if rows % 32 == 0 else 1
+    units = [(0, k, h) for k in range(1, n_t) for h in range(split)]
+    units += [(m, k, h) for k in range(1, n_t) for m in (1, 2) for h in range(split)]
+    return split, units
+
+
+def gather_kernel(n_dp, n_t, a_own, i_own, d_own, full, local, z_send, z_recv, p_send, p_recv):
+    l = Links(n_dp, n_t)
+    g = Gather(l, (a_own, i_own, d_own), full, z_send, z_recv, p_send, p_recv)
+    l.greet([{"tensor": l.up}] + [{"dp": l.flip(b)} for b in l.bits])
+    g.advance(-1)
+    copies = [pltpu.make_async_copy(g.own[m], full.at[m, 0], local.at[m]) for m in range(3)]
+    for c in copies:
+        c.start()
+    lag = 2
+    for i in range(len(g.units) + lag):
+        if i < len(g.units):
+            g.take(i)
+        if i >= lag:
+            g.relay(i - lag)
+    for c in copies:
+        c.wait()
+    l.drain()
+
+
+def gather_weights(a_own, i_own, d_own):
+    n_dp, n_t = lax.axis_size("dp"), lax.axis_size("tensor")
+    count = len(gather_units(a_own.shape[0] // n_dp, n_t)[1])
+    dma = pltpu.SemaphoreType.DMA
+    return pl.pallas_call(
+        functools.partial(gather_kernel, n_dp, n_t),
+        out_shape=jax.ShapeDtypeStruct((3, n_t) + a_own.shape, a_own.dtype),
+        in_specs=[pl.BlockSpec(memory_space=pl.ANY)] * 3,
+        out_specs=pl.BlockSpec(memory_space=pl.ANY),
+        scratch_shapes=[dma((3,)), dma((count,)), dma((count,)), dma((count, n_dp)), dma((count, n_dp))],
+        compiler_params=pltpu.CompilerParams(collective_id=0, has_side_effects=True),
+    )(a_own, i_own, d_own)
+
+
+def level_start(n_dp, level):
+    return sum(n_dp >> (t + 1) for t in range(level))
+
+
+def add_rows(out, *terms):
+    rows = out.shape[0]
+
+    def body(r, _):
+        at = pl.ds(pl.multiple_of(r * 16, 16), 16)
+        total = terms[0][at, :].astype(F32)
+        for t in terms[1:]:
+            total = total + t[at, :].astype(F32)
+        out[at, :] = total.astype(out.dtype)
+        return 0
+
+    lax.fori_loop(0, rows // 16, body, 0)
+
+
+REDUCE_REFS = 19
+
+
+def reduce_scratch(n_dp, n_t, count, rows, c):
+    dma = pltpu.SemaphoreType.DMA
+    half = n_dp // 2
+    return [
+        pltpu.VMEM((3, n_dp, rows, c), BF16),
+        pltpu.VMEM((2, half, rows, c), BF16),
+        pltpu.VMEM((2, half, rows, c), BF16),
+        pltpu.VMEM((2, 3, rows, c), BF16),
+        pltpu.VMEM((3, rows, c), BF16),
+        pltpu.VMEM((rows, c), F32),
+        dma((count, n_dp)),
+        dma((count, n_dp)),
+        dma((count,)),
+        dma((count,)),
+        dma((2,)),
+        dma((2,)),
+        dma((2, 3)),
+        dma(()),
+    ]
+
+
+def reduce_hbm(n_dp, n_t, count, rows, c):
+    return [
+        jax.ShapeDtypeStruct((count, n_dp // 2, rows, c), BF16),
+        jax.ShapeDtypeStruct((count, n_dp - 1, rows, c), BF16),
+        jax.ShapeDtypeStruct((count, rows, c), BF16),
+    ]
+
+
+class Reduce:
+    def __init__(self, links, order, out, hbm, scratch):
+        self.l, self.order, self.out = links, order, out
+        self.sums, self.got, self.ring = hbm
+        (self.block, self.fetched, self.half, self.terms, self.moving, self.final,
+         self.c_send, self.c_recv, self.z_send, self.z_recv,
+         self.f_sem, self.s_sem, self.t_sem, self.o_sem) = scratch
+        self.at = {o: i for i, o in enumerate(order)}
+        self.levels = len(links.bits)
+        self.under_way = {}
+        self.storing = False
+
+    def before(self, i):
+        m, s = self.order[i]
+        return self.at.get((m, s + 1))
+
+    def offsets(self, level):
+        bits = self.l.bits[level + 1:]
+        return [sum(b for n, b in enumerate(bits) if k >> n & 1) for k in range(1 << len(bits))]
+
+    def mine(self, level):
+        return lax.rem(self.l.me, 1 << (level + 1))
+
+    def give(self, i, level, source):
+        l, bit = self.l, self.l.bits[level]
+        there = self.mine(level) + bit - 2 * bit * l.own_bit(bit)
+        for n, off in enumerate(self.offsets(level)):
+            at = (i, level_start(l.n_dp, level) + n)
+            l.send(source(there + off), self.got.at[at], self.c_send.at[at], self.c_recv.at[at], {"dp": l.flip(bit)}, (i, level))
+
+    def receive(self, i, level):
+        l = self.l
+        for n, _ in enumerate(self.offsets(level)):
+            at = (i, level_start(l.n_dp, level) + n)
+            l.arrived(self.got.at[at], self.c_recv.at[at], self.c_send.at[at], {"dp": l.flip(l.bits[level])})
+
+    def clear(self, i):
+        self.l.finish((i - 3, 0))
+
+    def give_block(self, i):
+        self.give(i, 0, lambda piece: self.block.at[i % 3, piece])
+
+    def fetch_copy(self, i):
+        return pltpu.make_async_copy(self.got.at[i, pl.ds(0, self.l.n_dp // 2)], self.fetched.at[i % 2], self.f_sem.at[i % 2])
+
+    def fetch(self, i):
+        self.receive(i, 0)
+        self.fetch_copy(i).start()
+
+    def store_copy(self, i):
+        return pltpu.make_async_copy(self.half.at[i % 2], self.sums.at[i], self.s_sem.at[i % 2])
+
+    def add_first(self, i):
+        self.fetch_copy(i).wait()
+        for n in range(self.l.n_dp // 2):
+            add_rows(self.half.at[i % 2, n], self.block.at[i % 3, 2 * n + self.l.own_bit(1)], self.fetched.at[i % 2, n])
+        self.store_copy(i).start()
+
+    def give_next(self, i):
+        self.store_copy(i).wait()
+        self.give(i, 1, lambda piece: self.sums.at[i, piece // 2])
+
+    def steps(self, i):
+        count = len(self.order)
+        if i < count:
+            self.give_block(i)
+        if 0 <= i - 1 < count:
+            self.fetch(i - 1)
+        if 0 <= i - 2 < count:
+            self.add_first(i - 2)
+        if 0 <= i - 3 < count:
+            self.give_next(i - 3)
+
+    def middle(self, i, level):
+        l = self.l
+        self.receive(i, level)
+        for n, off in enumerate(self.offsets(level)):
+            piece = (self.mine(level) + off) // 2
+            loads = [
+                pltpu.make_async_copy(self.sums.at[i, piece], self.terms.at[0, 0], self.t_sem.at[0, 0]),
+                pltpu.make_async_copy(self.got.at[i, level_start(l.n_dp, level) + n], self.terms.at[0, 1], self.t_sem.at[0, 1]),
+            ]
+            for c in loads:
+                c.start()
+            for c in loads:
+                c.wait()
+            add_rows(self.terms.at[0, 2], self.terms.at[0, 0], self.terms.at[0, 1])
+            back = pltpu.make_async_copy(self.terms.at[0, 2], self.sums.at[i, piece], self.t_sem.at[0, 2])
+            back.start()
+            back.wait()
+        self.give(i, level + 1, lambda piece: self.sums.at[i, piece // 2])
+
+    def term_copies(self, i):
+        l = self.l
+        return [
+            pltpu.make_async_copy(self.sums.at[i, l.me // 2], self.terms.at[i % 2, 0], self.t_sem.at[i % 2, 0]),
+            pltpu.make_async_copy(self.got.at[i, l.n_dp - 2], self.terms.at[i % 2, 1], self.t_sem.at[i % 2, 1]),
+        ]
+
+    def ring_copy(self, i):
+        return pltpu.make_async_copy(self.ring.at[self.before(i)], self.terms.at[i % 2, 2], self.t_sem.at[i % 2, 2])
+
+    def collect(self, i):
+        self.receive(i, self.levels - 1)
+        for c in self.term_copies(i):
+            c.start()
+
+    def out_copy(self, m):
+        return pltpu.make_async_copy(self.final, self.out.at[m], self.o_sem)
+
+    def pass_on(self, i):
+        l = self.l
+        m, s = self.order[i]
+        b = self.before(i)
+        if b is not None:
+            l.arrived(self.ring.at[b], self.z_recv.at[b], self.z_send.at[b], {"tensor": l.down})
+            self.ring_copy(i).start()
+        for c in self.term_copies(i):
+            c.wait()
+        if b is not None:
+            self.ring_copy(i).wait()
+        terms = [self.terms.at[i % 2, t] for t in range(2 if b is None else 3)]
+        l.finish(("z", i - 3))
+        if s > 0:
+            add_rows(self.moving.at[i % 3], *terms)
+            l.send(self.moving.at[i % 3], self.ring.at[i], self.z_send.at[i], self.z_recv.at[i], {"tensor": l.up}, ("z", i))
+        else:
+            if self.storing is not False:
+                self.out_copy(self.storing).wait()
+            add_rows(self.final, *terms)
+            self.out_copy(m).start()
+            self.storing = m
+
+    def last_steps(self, i):
+        count = len(self.order)
+        if i < count:
+            for level in range(1, self.levels - 1):
+                self.middle(i, level)
+            self.collect(i)
+        if 0 <= i - 1 < count:
+            self.pass_on(i - 1)
+
+    def close(self):
+        self.out_copy(self.storing).wait()
+
+
+class Spread:
+    def __init__(self, links, block, out, send, recv, local):
+        self.l, self.block, self.out, self.send, self.recv = links, block, out, send, recv
+        self.copy = pltpu.make_async_copy(block, out.at[links.z], local)
+
+    def start(self):
+        self.copy.start()
+        l = self.l
+        l.send(self.block, self.out.at[l.z], self.send.at[0], self.recv.at[0], {"tensor": l.down})
+
+    def step(self, k):
+        l = self.l
+        at = lax.rem(l.z + k, l.n_t)
+        l.arrived(self.out.at[at], self.recv.at[k - 1], self.send.at[k - 1], {"tensor": l.up})
+        if k < l.n_t - 1:
+            l.send(self.out.at[at], self.out.at[at], self.send.at[k], self.recv.at[k], {"tensor": l.down})
+
+    def close(self):
+        self.copy.wait()
+
+
+class Total:
+    def __init__(self, links, block, buf, send, recv):
+        self.l, self.block, self.buf, self.s, self.r = links, block, buf, send, recv
+        self.levels = len(links.bits)
+        self.count = self.levels + links.n_t
+
+    def step(self, s):
+        l, buf = self.l, self.buf
+        if s == 0:
+            buf[1] = self.block[...]
+        else:
+            l.arrived(buf.at[2 * s], self.r.at[s - 1], self.s.at[s - 1], {"tensor": l.up})
+            if s <= self.levels:
+                buf[2 * s + 1] = buf[2 * s - 1] + buf[2 * s]
+        if s < self.levels:
+            l.send(buf.at[2 * s + 1], buf.at[2 * s + 2], self.s.at[s], self.r.at[s], {"dp": l.flip(l.bits[s])})
+        elif s < self.count - 1:
+            src = 2 * s + 1 if s == self.levels else 2 * s
+            l.send(buf.at[src], buf.at[2 * s + 2], self.s.at[s], self.r.at[s], {"tensor": l.down})
+
+    def result(self):
+        total = self.buf[2 * self.levels + 1]
+        for k in range(1, self.l.n_t):
+            total = total + self.buf[2 * (self.levels + k)]
+        return total
+
+
+def reduce_kernel(n_dp, n_t, blocks, acts, gains, out_acts, out_sums, out_gains, *refs):
+    l = Links(n_dp, n_t)
+    hbm, scratch, rest = refs[:3], refs[3:17], refs[17:]
+    gain_buf, g_send, g_recv, a_send, a_recv, a_local, b_sem = rest
+    count = blocks.shape[0]
+    mats = count // n_t
+    order = [(m, s) for m in range(mats) for s in reversed(range(n_t))]
+    r = Reduce(l, order, out_sums, hbm, scratch)
+    spread = Spread(l, acts, out_acts, a_send, a_recv, a_local)
+    total = Total(l, gains, gain_buf, g_send, g_recv)
+    l.greet([{"tensor": l.up}, {"tensor": l.down}] + [{"dp": l.flip(b)} for b in l.bits])
+    spread.start()
+
+    def load(i):
+        return pltpu.make_async_copy(blocks.at[i], r.block.at[i % 3], b_sem.at[i % 3])
+
+    load(0).start()
+    extra = 3
+    for i in range(count + extra):
+        if i < count:
+            load(i).wait()
+        r.steps(i)
+        if i + 1 < count:
+            if i + 1 >= 3:
+                r.clear(i + 1)
+            load(i + 1).start()
+        if i < total.count:
+            total.step(i)
+    for i in range(count + 1):
+        r.last_steps(i)
+        if i % 3 == 2 and 1 + i // 3 < n_t:
+            spread.step(1 + i // 3)
+    out_gains[...] = total.result()
+    r.close()
+    spread.close()
+    l.drain()
+
+
+def reduce_all(blocks, acts, gains):
+    n_dp, n_t = lax.axis_size("dp"), lax.axis_size("tensor")
+    count, _, rows, c = blocks.shape
+    mats = count // n_t
+    steps = len(ring_bits(n_dp)) + n_t
+    dma = pltpu.SemaphoreType.DMA
+    hbm, vmem = pl.BlockSpec(memory_space=pl.ANY), pl.BlockSpec(memory_space=pltpu.VMEM)
+    out = pl.pallas_call(
+        functools.partial(reduce_kernel, n_dp, n_t),
+        out_shape=[
+            jax.ShapeDtypeStruct((n_t,) + acts.shape, BF16),
+            jax.ShapeDtypeStruct((mats, rows, c), F32),
+            jax.ShapeDtypeStruct(gains.shape, F32),
+        ] + reduce_hbm(n_dp, n_t, count, rows, c),
+        in_specs=[hbm, hbm, vmem],
+        out_specs=[hbm, hbm, vmem, hbm, hbm, hbm],
+        scratch_shapes=reduce_scratch(n_dp, n_t, count, rows, c) + [
+            pltpu.VMEM((2 * steps,) + gains.shape, F32),
+            dma((steps,)), dma((steps,)), dma((n_t,)), dma((n_t,)), dma(()), dma((3,)),
+        ],
+        compiler_params=pltpu.CompilerParams(collective_id=1, has_side_effects=True, vmem_limit_bytes=60 * 2**20),
+    )(blocks, acts, gains)
+    return out[0], out[1], out[2]
 
 
 def turn(x, axis, step):
     n = lax.axis_size(axis)
     return lax.ppermute(x, axis, [(i, (i + step) % n) for i in range(n)])
-
-
-def gather_shards(shard):
-    n_dp, n_t = lax.axis_size("dp"), lax.axis_size("tensor")
-    me = lax.axis_index("dp")
-    rows = shard.shape[0] // n_dp
-    piece = lax.dynamic_slice_in_dim(shard, me * rows, rows, 0)
-    slots = []
-    for _ in range(1, n_t):
-        piece = turn(piece, "tensor", -1)
-        have = {0: piece}
-        for bit in reversed(bits_of(n_dp)):
-            have.update({j ^ bit: swap(p, "dp", bit) for j, p in list(have.items())})
-        slots.append([(me ^ j, p) for j, p in have.items()])
-    return rows, slots
-
-
-def gather_square(shard):
-    rows, slots = gather_shards(shard)
-    result = [shard]
-    for slot in slots:
-        full = jnp.zeros(shard.shape, shard.dtype)
-        for at, p in slot:
-            full = lax.dynamic_update_slice_in_dim(full, p, at * rows, 0)
-        result.append(full)
-    return result
-
-
-def gather_heads(stack):
-    kinds, hd, d = stack.shape
-    n_t = lax.axis_size("tensor")
-    rows, slots = gather_shards(stack.reshape(kinds * hd, d))
-    full = jnp.zeros((kinds, n_t * hd, d), stack.dtype)
-    full = lax.dynamic_update_slice(full, stack, (0, 0, 0))
-    for s, slot in enumerate(slots):
-        for at, p in slot:
-            first = at * rows
-            full = lax.dynamic_update_slice(full, p[None], (first // hd, (s + 1) * hd + lax.rem(first, hd), 0))
-    return full
-
-
-def reduce_blocks(parts):
-    n_dp, n_t = lax.axis_size("dp"), lax.axis_size("tensor")
-    me = lax.axis_index("dp")
-    rows = parts[0].shape[0] // n_dp
-    total = None
-    for s in reversed(range(n_t)):
-        term = parts[s].reshape(n_dp, rows, -1)
-        for bit in bits_of(n_dp):
-            view = term.reshape(-1, 2, rows, term.shape[-1])
-            own = jnp.where(me & bit == 0, 0, 1)
-            keep = lax.dynamic_index_in_dim(view, own, 1, keepdims=False)
-            give = lax.dynamic_index_in_dim(view, 1 - own, 1, keepdims=False)
-            term = (keep.astype(F32) + swap(give, "dp", bit).astype(F32)).astype(BF16)
-        term = term.reshape(rows, -1)
-        if total is not None:
-            term = term.astype(F32) + turn(total, "tensor", 1).astype(F32)
-            term = term if s == 0 else term.astype(BF16)
-        total = term
-    return total.astype(F32)
 
 
 def spread_rows(block):
@@ -296,8 +702,11 @@
     is_first = lax.axis_index("section") == 0
     tables = rope_tables()
 
-    heads = gather_heads(jnp.concatenate([jnp.swapaxes(w_qkv, 1, 2), w_out[None]], axis=0))
-    weights = (heads[0], heads[1], heads[2], heads[3], gather_square(w_in), gather_square(w_down))
+    stack = jnp.concatenate([jnp.swapaxes(w_qkv, 1, 2), w_out[None]], axis=0).reshape(4 * hd, d)
+    full = gather_weights(stack, w_in, w_down)
+    heads = full[0].reshape(n_t, 4, hd, d)
+    heads = [heads[:, kind].reshape(n_t * hd, d) for kind in range(4)]
+    weights = (*heads, [full[1, s] for s in range(n_t)], [full[2, s] for s in range(n_t)])
 
     x0 = own_rows(tokens, count)
     g1 = own_rows(cotangent, count)
@@ -312,14 +721,12 @@
     upstream = lax.ppermute(dh1.astype(BF16), "section", [(1, 0)])
     g0 = jnp.where(is_first, upstream, g1)
     dh0, (g_attn, g_in, g_down, gain_terms) = backward(g0.astype(F32), kept, weights, gains, seg, obs, tables, True)
-    grad_acts = spread_rows(dh0.astype(BF16))
-
-    r_down = reduce_blocks(g_down)
-    r_in = reduce_blocks(g_in)
-    r_attn = reduce_blocks(g_attn)
-    r_gain = lax.psum(gain_terms, ("tensor", "dp"))
     piece = d // n_dp
-    r_gain = lax.dynamic_slice_in_dim(r_gain, lax.axis_index("dp") * piece, piece, 1)
+    blocks = [g[s] for g in (g_down, g_in, g_attn) for s in reversed(range(n_t))]
+    blocks = jnp.stack(blocks).reshape(3 * n_t, n_dp, piece, -1)
+    gains_in = jnp.concatenate([gain_terms, jnp.zeros((6, d), F32)], axis=0)
+    grad_acts, (r_down, r_in, r_attn), r_gain = reduce_all(blocks, dh0.astype(BF16), gains_in)
+    r_gain = lax.dynamic_slice_in_dim(r_gain[:2], lax.axis_index("dp") * piece, piece, 1)
     r_qkv = jnp.stack([r_attn[:, i * hd:(i + 1) * hd] for i in range(3)])
     r_out = r_attn[:, 3 * hd:].T
     return (

time: 1280 us -> 1190 us (0.930)
  Pallas kernels: 151 us -> 707 us
  waiting for transfers between devices: 385 us -> 56.4 us
  local copies, waits for them, and re-layouts: 323 us -> 133 us
  blocking collectives: 59.3 us -> 0 us
  starting transfers between devices: 59.8 us -> 14.2 us
  other arithmetic: 38.6 us -> 25.4 us
    pallas_call x0 -> x2, Pallas kernels: none -> 612 us  [the longest x1 306 us: reduce_all(): pl.pallas_call(functools.partial(reduce_kernel, n_dp, n_t), out_shape=[ja...]
    ppermute x24 -> x3, waiting for transfers between devices: 244 us -> 15.7 us  [turn(): return lax.ppermute(x, axis, [(i, (i + step) % n) for i in range(n)])]
    dynamic_update_slice x37 -> x0, local copies, waits for them, and re-layouts: 113 us -> none  [the longest x12 57.5 us: gather_heads(): lax.dynamic_update_slice(full, p[None], (first // hd, (s + 1) * hd + lax....]
    ppermute x51 -> x0, waiting for transfers between devices: 103 us -> none  [swap(): return lax.ppermute(x, axis, [(i, i ^ bit) for i in range(n)])]
    psum x1 -> x0, blocking collectives: 59.3 us -> none  [on_device(): r_gain = lax.psum(gain_terms, ('tensor', 'dp'))]
    dynamic_slice x7 -> x0, local copies, waits for them, and re-layouts: 45.4 us -> none  [the longest x4 44.1 us: reduce_blocks(): keep = lax.dynamic_index_in_dim(view, own, 1, keepdims=False)]
    unnamed x231 -> x161, local copies, waits for them, and re-layouts: 86.8 us -> 42 us
    pallas_call x2, Pallas kernels: 90 us -> 59.2 us  [attention_back(): pl.pallas_call(attn_bwd_kernel, grid=grid, in_specs=[wide, wide, wide, wi...]
  transfers between devices with their start and end apart: 77 -> 5, of which waited for: 28 -> 3; matrix products, arithmetic and copies ran while one was open for 38% -> 18% of each run, Pallas kernels for 6% -> 28%
where the time goes in v2:
time: 1190 us; the launch traced here: 1180 us
  Pallas kernels  707 us (59%)
  matrix products  246 us (21%)
  local copies, waits for them, and re-layouts  133 us (11%)
  waiting for transfers between devices  56.4 us (5%)
  other arithmetic  25.4 us (2%)
  starting transfers between devices  14.2 us (1%)
    pallas_call x1, Pallas kernels, reduce_all(): pl.pallas_call(functools.partial(reduce_kernel, n_dp, n_t), out_shape=[ja...  306 us
    pallas_call x1, Pallas kernels, gather_weights(): pl.pallas_call(functools.partial(gather_kernel, n_dp, n_t), out_shape=jax...  306 us
    dot_general x20, matrix products, dot_nn(): lax.dot_general(a, b, (((1,), (0,)), ((), ())), preferred_element_type=F32)  109 us
    dot_general x20, matrix products, dot_nt(): lax.dot_general(a, b, (((1,), (1,)), ((), ())), preferred_element_type=F32)  98.3 us
    another operation x9, local copies, waits for them, and re-layouts, on_device(): blocks = jnp.stack(blocks).reshape(3 * n_t, n_dp, piece, -1)  59.9 us
    pallas_call x2, Pallas kernels, attention_back(): pl.pallas_call(attn_bwd_kernel, grid=grid, in_specs=[wide, wide, wide, wi...  59.2 us
    unnamed x161, local copies, waits for them, and re-layouts  42 us
    dot_general x12, matrix products, dot_tn(): lax.dot_general(a, b, (((0,), (0,)), ((), ())), preferred_element_type=F32)  39.2 us
  transfers between devices with their start and end apart: 5, of which 3 were waited for; matrix products, arithmetic and copies ran while one was open for 18% of the time, Pallas kernels for 28%

profile of v2, /device:TPU:0, one launch (start us, length us, event | category | flops | bytes accessed | tf_op | source)
XLA Modules:
  0.0 1184.5 jit_solution(15043213292734845363)
XLA Ops:
  12.7 305.7 %shard_map.144 = bf16[3,4,1280,1280]{3,2,1,0:T(8,128)(2,1)} custom-call(bf16[1280,1280]{1,0:T(8,128)(2,1)} %bitcast.294, bf16[1280,1280]{1,0:T(8,128)(2,1)} %bitcast.301, bf16[1280,1280]{1,0:T(8,128)(2,1)} %bitcast.302), custom_call_target="tpu_custom_call" | custom-call | tf_op jit(solution)/shard_map/pallas_call | solution.py:357
  336.2 18.4 %shard_map.145 = (bf16[512,1280]{1,0:T(8,128)(2,1)}, bf16[512,1280]{1,0:T(8,128)(2,1)}, bf16[512,1280]{1,0:T(8,128)(2,1)S(1)}) custom-call(f32[512,1280]{1,0:T(8,128)S(1)} %fusion.201.qp, f32[512,1280]{1,0:T(8,128)S(1)} %fusion.199.kp, bf16[512,1280]{1,0:T(8,128)(2,1)S(1)} %convolution_convert_fusion.15.v, s32[512,1]{1,0:T(8,128)S(1)} %copy.21.seg_col, ...), custom_call_target="tpu_custom_call" | custom-call | flops 1342177280 | bytes 10485760 | tf_op jit(solution)/shard_map/pallas_call | solution.py:133
  359.3 9.8 convolution_add_fusion.14
  369.1 9.8 convolution_add_fusion.13
  378.9 9.8 convolution_add_fusion.12
  388.7 9.6 fusion.87
  403.4 26.3 %collective-permute-done = bf16[512,1280]{1,0:T(8,128)(2,1)} collective-permute-done((bf16[512,1280]{1,0:T(8,128)(2,1)}, bf16[512,1280]{1,0:T(8,128)(2,1)}, u32[]{:S(2)}, u32[]{:S(2)}) %collective-permute-start) | collective-permute-done | bytes 1310752 | tf_op jit(solution)/shard_map/ppermute | solution.py:716
  438.4 17.8 %shard_map.146 = (bf16[512,1280]{1,0:T(8,128)(2,1)S(1)}, bf16[512,1280]{1,0:T(8,128)(2,1)S(1)}, bf16[512,1280]{1,0:T(8,128)(2,1)S(1)}) custom-call(f32[512,1280]{1,0:T(8,128)S(1)} %fusion.209.qp, f32[512,1280]{1,0:T(8,128)S(1)} %fusion.207.kp, bf16[512,1280]{1,0:T(8,128)(2,1)S(1)} %convolution_convert_fusion.14.v, s32[512,1]{1,0:T(8,128)S(1)} %copy.21.seg_col, ...), custom_call_target="tpu_custom_call" | custom-call | flops 1342177280 | bytes 10485760 | tf_op jit(solution)/shard_map/pallas_call | solution.py:133
  458.6 7.3 fusion.22
  465.9 5.5 fusion.33
  471.4 5.4 fusion.44
  476.8 5.5 fusion.54
  482.3 6.5 fusion.39
  488.9 5.5 fusion.28
  494.4 9.6 fusion.20
  504.0 10.2 convolution_add_fusion.9
  514.2 10.2 convolution_add_fusion.8
  524.3 10.9 multiply_reduce_fusion.2
  535.3 6.4 convolution_convert_fusion.13.do
  541.7 29.5 %shard_map.147 = (bf16[512,1280]{1,0:T(8,128)(2,1)S(1)}, bf16[512,1280]{1,0:T(8,128)(2,1)S(1)}, bf16[512,1280]{1,0:T(8,128)(2,1)S(1)}) custom-call(bf16[512,1280]{1,0:T(8,128)(2,1)S(1)} %copy-done.3, bf16[512,1280]{1,0:T(8,128)(2,1)S(1)} %copy-done.5, bf16[512,1280]{1,0:T(8,128)(2,1)S(1)} %copy-done.1, bf16[512,1280]{1,0:T(8,128)(2,1)S(1)} %convolution_convert_fusion.13.do, ...), custom_call_target="tpu_custom_call" | custom-call | flops 3355443200 | bytes 9175040 | tf_op jit(solution)/shard_map/pallas_call | solution.py:149
  582.8 5.6 fusion.15
  588.8 8.6 bitcast_dynamic-update-slice_fusion.3
  599.0 14.4 %collective-permute-done.4 = bf16[512,1280]{1,0:T(8,128)(2,1)S(1)} collective-permute-done((bf16[512,1280]{1,0:T(8,128)(2,1)}, bf16[512,1280]{1,0:T(8,128)(2,1)S(1)}, u32[]{:S(2)}, u32[]{:S(2)}) %collective-permute-start.4) | collective-permute-done | bytes 1310752 | tf_op jit(solution)/shard_map/ppermute | solution.py:721
  670.7 29.7 %shard_map.148 = (bf16[512,1280]{1,0:T(8,128)(2,1)S(1)}, bf16[512,1280]{1,0:T(8,128)(2,1)S(1)}, bf16[512,1280]{1,0:T(8,128)(2,1)S(1)}) custom-call(bf16[512,1280]{1,0:T(8,128)(2,1)S(1)} %copy-done.3, bf16[512,1280]{1,0:T(8,128)(2,1)S(1)} %copy-done.5, bf16[512,1280]{1,0:T(8,128)(2,1)S(1)} %copy-done.1, bf16[512,1280]{1,0:T(8,128)(2,1)S(1)} %convolution_convert_fusion.12.do, ...), custom_call_target="tpu_custom_call" | custom-call | flops 3355443200 | bytes 9175040 | tf_op jit(solution)/shard_map/pallas_call | solution.py:149
  740.3 7.3 copy.39
  750.9 8.8 reshape.141
  759.7 8.0 copy.38
  804.2 7.3 copy.40
  822.0 8.8 reshape.144
  830.7 7.3 copy.41
  840.0 305.9 %shard_map.149 = (bf16[4,512,1280]{2,1,0:T(8,128)(2,1)}, f32[3,320,1280]{2,1,0:T(8,128)}, f32[8,1280]{1,0:T(8,128)}, bf16[12,2,320,1280]{3,2,1,0:T(8,128)(2,1)},...) custom-call(bf16[12,4,320,1280]{3,2,1,0:T(8,128)(2,1)} %constant_dynamic-update-slice_fusion.blocks, ...), custom_call_target="tpu_custom_call" | custom-call | tf_op jit(solution)/shard_map/pallas_call | solution.py:656
  1164.9 15.7 %collective-permute-done.3 = bf16[512,1280]{1,0:T(8,128)(2,1)S(1)} collective-permute-done((bf16[512,1280]{1,0:T(8,128)(2,1)}, bf16[512,1280]{1,0:T(8,128)(2,1)S(1)}, u32[]{:S(2)}, u32[]{:S(2)}) %collective-permute-start.3) | collective-permute-done | bytes 1310752 | tf_op jit(solution)/shard_map/ppermute | solution.py:676
  (260 shorter events, 235.5 us)
Async XLA Ops:
  325.5 7.4 copy-start.23
  336.2 18.4 %copy-start.26 = (bf16[4,1,320,1280]{3,2,1,0:T(8,128)(2,1)S(1)}, bf16[4,1,320,1280]{3,2,1,0:T(8,128)(2,1)}, u32[]{:S(2)}) copy-start(bf16[4,1,320,1280]{3,2,1,0:T(8,128)(2,1)} %get-tuple-element.55) | copy-start | bytes 9830404
  398.3 31.5 %collective-permute-start = (bf16[512,1280]{1,0:T(8,128)(2,1)}, bf16[512,1280]{1,0:T(8,128)(2,1)}, u32[]{:S(2)}, u32[]{:S(2)}) collective-permute-start(bf16[512,1280]{1,0:T(8,128)(2,1)} %fusion.87), channel_id=1, source_target_pairs={{0,16},{1,17},{2,18},{3,19},{4,20},{5,21},{6,22},{7,23},{8,24},{9,... | collective-permute-start | bytes 3932168 | tf_op jit(solution)/shard_map/ppermute | solution.py:716
  402.8 28.8 %copy-start.18 = (bf16[4,1,320,1280]{3,2,1,0:T(8,128)(2,1)S(1)}, bf16[4,1,320,1280]{3,2,1,0:T(8,128)(2,1)}, u32[]{:S(2)}) copy-start(bf16[4,1,320,1280]{3,2,1,0:T(8,128)(2,1)} %copy-done.17) | copy-start | bytes 9830404
  431.6 24.6 %copy-start.11 = (bf16[512,1280]{1,0:T(8,128)(2,1)}, bf16[512,1280]{1,0:T(8,128)(2,1)S(1)}, u32[]{:S(2)}) copy-start(bf16[512,1280]{1,0:T(8,128)(2,1)S(1)} %get-tuple-element.54) | copy-start | bytes 3932164
  431.6 146.0 %copy-start.45 = (f32[512]{0:T(512)}, f32[512]{0:T(512)S(1)}, u32[]{:S(2)}) copy-start(f32[512]{0:T(512)S(1)} %get-tuple-element.82) | copy-start | bytes 6148
  438.4 17.9 %copy-start.27 = (bf16[4,1,320,1280]{3,2,1,0:T(8,128)(2,1)S(1)}, bf16[4,1,320,1280]{3,2,1,0:T(8,128)(2,1)}, u32[]{:S(2)}) copy-start(bf16[4,1,320,1280]{3,2,1,0:T(8,128)(2,1)} %get-tuple-element.55) | copy-start | bytes 9830404
  456.2 32.5 %slice-start = ((s8[39321600]{0:T(1024)(128)(4,1)}), s8[4194304]{0:T(1024)(128)(4,1)S(1)}, s32[]{:S(2)}) async-start(s8[39321600]{0:T(1024)(128)(4,1)} %bitcast.291), calls=%async_computation | async-start | bytes 8388608
  456.3 32.5 %slice-start.1 = ((s8[39321600]{0:T(1024)(128)(4,1)}), s8[4194304]{0:T(1024)(128)(4,1)S(1)}, s32[]{:S(2)}) async-start(s8[39321600]{0:T(1024)(128)(4,1)} %bitcast.291), calls=%async_computation.1 | async-start | bytes 8388608
  458.3 7.6 copy-start.8
  458.3 30.5 %slice-start.2 = ((s8[39321600]{0:T(1024)(128)(4,1)}), s8[4194304]{0:T(1024)(128)(4,1)S(1)}, s32[]{:S(2)}) async-start(s8[39321600]{0:T(1024)(128)(4,1)} %bitcast.291), calls=%async_computation.2 | async-start | bytes 8388608
  458.6 18.2 %copy-start.43 = (bf16[512,1280]{1,0:T(8,128)(2,1)}, bf16[512,1280]{1,0:T(8,128)(2,1)S(1)}, u32[]{:S(2)}) copy-start(bf16[512,1280]{1,0:T(8,128)(2,1)S(1)} %multiply_convert_fusion.4) | copy-start | bytes 3932164
  458.6 30.2 %slice-start.3 = ((s8[39321600]{0:T(1024)(128)(4,1)}), s8[4194304]{0:T(1024)(128)(4,1)S(1)}, s32[]{:S(2)}) async-start(s8[39321600]{0:T(1024)(128)(4,1)} %bitcast.291), calls=%async_computation.3 | async-start | bytes 8388608
  465.9 22.9 %slice-start.4 = ((s8[39321600]{0:T(1024)(128)(4,1)}), s8[4194304]{0:T(1024)(128)(4,1)S(1)}, s32[]{:S(2)}) async-start(s8[39321600]{0:T(1024)(128)(4,1)} %bitcast.291), calls=%async_computation.4 | async-start | bytes 8388608
  471.4 17.4 %slice-start.5 = ((s8[39321600]{0:T(1024)(128)(4,1)}), s8[4194304]{0:T(1024)(128)(4,1)S(1)}, s32[]{:S(2)}) async-start(s8[39321600]{0:T(1024)(128)(4,1)} %bitcast.291), calls=%async_computation.5 | async-start | bytes 8388608
  471.4 17.5 %slice-start.6 = ((s8[39321600]{0:T(1024)(128)(4,1)}), s8[4194304]{0:T(1024)(128)(4,1)S(1)}, s32[]{:S(2)}) async-start(s8[39321600]{0:T(1024)(128)(4,1)} %bitcast.291), calls=%async_computation.6 | async-start | bytes 8388608
  476.8 12.1 %slice-start.7 = ((s8[39321600]{0:T(1024)(128)(4,1)}), s8[4194304]{0:T(1024)(128)(4,1)S(1)}, s32[]{:S(2)}) async-start(s8[39321600]{0:T(1024)(128)(4,1)} %bitcast.291), calls=%async_computation.7 | async-start | bytes 8388608
  482.3 6.6 slice-start.8
  482.3 6.6 slice-start.9
  541.7 29.6 %copy-start.25 = (bf16[4,1,320,1280]{3,2,1,0:T(8,128)(2,1)S(1)}, bf16[4,1,320,1280]{3,2,1,0:T(8,128)(2,1)}, u32[]{:S(2)}) copy-start(bf16[4,1,320,1280]{3,2,1,0:T(8,128)(2,1)} %copy-done.23) | copy-start | bytes 9830404
  581.5 31.9 %collective-permute-start.4 = (bf16[512,1280]{1,0:T(8,128)(2,1)}, bf16[512,1280]{1,0:T(8,128)(2,1)S(1)}, u32[]{:S(2)}, u32[]{:S(2)}) collective-permute-start(bf16[512,1280]{1,0:T(8,128)(2,1)} %fusion.91), channel_id=1, source_target_pairs={{16,0},{17,1},{18,2},{19,3},{20,4},{21,5},{22,6},{23,7},{24,8},{25... | collective-permute-start | bytes 3932168 | tf_op jit(solution)/shard_map/ppermute | solution.py:721
  597.3 22.0 %copy-start.16 = (bf16[4,512,1280]{2,1,0:T(8,128)(2,1)}, bf16[4,512,1280]{2,1,0:T(8,128)(2,1)S(1)}, u32[]{:S(2)}) copy-start(bf16[4,512,1280]{2,1,0:T(8,128)(2,1)S(1)} %get-tuple-element.99) | copy-start | bytes 15728644
  597.3 17.7 %copy-start.54 = (f32[512,1280]{1,0:T(8,128)S(1)}, f32[512,1280]{1,0:T(8,128)}, u32[]{:S(2)}) copy-start(f32[512,1280]{1,0:T(8,128)} %fusion.54) | copy-start | bytes 7864324
  597.3 221.1 %collective-permute-start.1 = (bf16[512,1280]{1,0:T(8,128)(2,1)}, bf16[512,1280]{1,0:T(8,128)(2,1)}, u32[]{:S(2)}, u32[]{:S(2)}) collective-permute-start(bf16[512,1280]{1,0:T(8,128)(2,1)} %get-tuple-element.100), channel_id=1, source_target_pairs={{0,12},{4,0},{8,4},{12,8},{1,13},{5,1},{9,5},{13,9},{2,14},{6,2},{... | collective-permute-start | bytes 3932168 | tf_op jit(solution)/shard_map/ppermute | solution.py:676
  619.3 39.3 %copy-start.48 = (bf16[512,1280]{1,0:T(8,128)(2,1)}, bf16[512,1280]{1,0:T(8,128)(2,1)S(1)}, u32[]{:S(2)}) copy-start(bf16[512,1280]{1,0:T(8,128)(2,1)S(1)} %fusion.84) | copy-start | bytes 3932164
  627.2 27.5 %copy-start.57 = (bf16[512,1280]{1,0:T(8,128)(2,1)}, bf16[512,1280]{1,0:T(8,128)(2,1)S(1)}, u32[]{:S(2)}) copy-start(bf16[512,1280]{1,0:T(8,128)(2,1)S(1)} %fusion.81) | copy-start | bytes 3932164
  635.1 15.8 %copy-start.59 = (bf16[512,1280]{1,0:T(8,128)(2,1)}, bf16[512,1280]{1,0:T(8,128)(2,1)S(1)}, u32[]{:S(2)}) copy-start(bf16[512,1280]{1,0:T(8,128)(2,1)S(1)} %fusion.78) | copy-start | bytes 3932164
  804.2 10.9 copy-start.46
  818.5 332.9 %collective-permute-start.2 = (bf16[512,1280]{1,0:T(8,128)(2,1)}, bf16[512,1280]{1,0:T(8,128)(2,1)}, u32[]{:S(2)}, u32[]{:S(2)}) collective-permute-start(bf16[512,1280]{1,0:T(8,128)(2,1)} %collective-permute-done.1), channel_id=1, source_target_pairs={{0,12},{4,0},{8,4},{12,8},{1,13},{5,1},{9,5},{13,9},{2,14},{6,2},{... | collective-permute-start | bytes 3932168 | tf_op jit(solution)/shard_map/ppermute | solution.py:676
  1151.4 29.2 %collective-permute-start.3 = (bf16[512,1280]{1,0:T(8,128)(2,1)}, bf16[512,1280]{1,0:T(8,128)(2,1)S(1)}, u32[]{:S(2)}, u32[]{:S(2)}) collective-permute-start(bf16[512,1280]{1,0:T(8,128)(2,1)} %collective-permute-done.2), channel_id=1, source_target_pairs={{0,12},{4,0},{8,4},{12,8},{1,13},{5,1},{9,5},{13,9},{2,14},{6,2},{... | collective-permute-start | bytes 3932168 | tf_op jit(solution)/shard_map/ppermute | solution.py:676
  1158.2 23.5 %slice-start.11 = ((s8[5242880]{0:T(1024)(128)(4,1)}), s8[4194304]{0:T(1024)(128)(4,1)S(1)}, s32[]{:S(2)}) async-start(s8[5242880]{0:T(1024)(128)(4,1)} %bitcast.295), calls=%async_computation.11 | async-start | bytes 8388608
  1159.4 22.3 %slice-start.12 = ((s8[5242880]{0:T(1024)(128)(4,1)}), s8[1048576]{0:T(1024)(128)(4,1)S(1)}, s32[]{:S(2)}) async-start(s8[5242880]{0:T(1024)(128)(4,1)} %bitcast.295), calls=%async_computation.12 | async-start | bytes 2097152
  (47 other events, 154.3 us)

commit v3 on v2

v3 whole, which is shorter than its diff:
```python
import functools
import math

import jax
import jax.numpy as jnp
from jax import lax
from jax.experimental import pallas as pl
from jax.experimental.pallas import tpu as pltpu
from jax.sharding import PartitionSpec as P

HEAD_SIZE = 80
HALF = HEAD_SIZE // 2
ROW = 512
QB = 128
GROUP = 8
EPS = 1e-06
BIG = 1000000000.0
SCALE = 1.0 / math.sqrt(HEAD_SIZE)
BF16 = jnp.bfloat16
F32 = jnp.float32
MESH = pl.DeviceIdType.MESH


def dot_nn(a, b):
    return lax.dot_general(a, b, (((1,), (0,)), ((), ())), preferred_element_type=F32)


def dot_nt(a, b):
    return lax.dot_general(a, b, (((1,), (1,)), ((), ())), preferred_element_type=F32)


def dot_tn(a, b):
    return lax.dot_general(a, b, (((0,), (0,)), ((), ())), preferred_element_type=F32)


def rope_tables():
    freq = 10000.0 ** (-jnp.arange(HALF, dtype=F32) / HALF)
    ang = jnp.arange(ROW, dtype=F32)[:, None] * freq[None, :]
    cos, sin = jnp.cos(ang), jnp.sin(ang)
    cos_full = jnp.tile(jnp.concatenate([cos, cos], axis=1), (1, GROUP))
    sin_full = jnp.tile(jnp.concatenate([-sin, sin], axis=1), (1, GROUP))
    return cos_full, sin_full


def partner(x):
    width = x.shape[1]
    lane = lax.broadcasted_iota(jnp.int32, x.shape, 1)
    first = lax.rem(lane, HEAD_SIZE) < HALF
    return jnp.where(first, pltpu.roll(x, width - HALF, 1), pltpu.roll(x, HALF, 1))


def windows():
    return [max(i - 1, 0) * QB for i in range(ROW // QB)]


def write_mask(mask, seg_col, seg_row, obs_row):
    for i, k0 in enumerate(windows()):
        r = slice(i * QB, (i + 1) * QB)
        shape = (QB, 2 * QB)
        qi = lax.broadcasted_iota(jnp.int32, shape, 0) + i * QB
        kj = lax.broadcasted_iota(jnp.int32, shape, 1) + k0
        same = seg_col[r, :] == seg_row[:, k0:k0 + 2 * QB]
        seen = (obs_row[:, k0:k0 + 2 * QB] == 1) | (kj == qi)
        mask[r, :] = (same & (kj <= qi) & seen).astype(F32)


def by_block(dot, left, right):
    return jnp.concatenate(
        [dot(left[i * QB:(i + 1) * QB], right[k0:k0 + 2 * QB]) for i, k0 in enumerate(windows())], axis=0
    )


def by_window(left, right):
    n = ROW // QB
    blocks = [None] * n
    for i, k0 in enumerate(windows()):
        r = slice(i * QB, (i + 1) * QB)
        term = dot_tn(left[r], right[r])
        for j in range(2):
            at, part = k0 // QB + j, term[j * QB:(j + 1) * QB]
            blocks[at] = part if blocks[at] is None else blocks[at] + part
    return jnp.concatenate(blocks, axis=0)


def probabilities(q, k, mask):
    s = jnp.where(mask[...] > 0, by_block(dot_nt, q, k) * SCALE, -BIG)
    e = jnp.exp(s - jnp.max(s, axis=1, keepdims=True))
    return e * (1.0 / jnp.sum(e, axis=1, keepdims=True))


def ring_bits(n):
    return [1 << i for i in range(n.bit_length() - 1)]


def low_bit(j):
    return j & -j


class Links:
    def __init__(self, n_dp, n_t):
        self.n_dp, self.n_t = n_dp, n_t
        self.me, self.z = lax.axis_index("dp"), lax.axis_index("tensor")
        self.down = lax.rem(self.z + n_t - 1, n_t)
        self.up = lax.rem(self.z + 1, n_t)
        self.bits = ring_bits(n_dp)
        self.sent, self.recording = {}, True

    def flip(self, bit):
        return self.me + bit - 2 * bit * lax.rem(self.me // bit, 2)

    def mix(self, j):
        at = self.me
        for bit in self.bits:
            if j & bit:
                at = at + bit - 2 * bit * lax.rem(self.me // bit, 2)
        return at

    def own_bit(self, bit):
        return lax.rem(self.me // bit, 2)

    def greet(self, axes):
        barrier = pltpu.get_barrier_semaphore()
        for where in axes:
            pl.semaphore_signal(barrier, inc=1, device_id=where, device_id_type=MESH)
        pl.semaphore_wait(barrier, len(axes))

    def send(self, src, dst, send_sem, recv_sem, where, tag=None, again=None):
        pltpu.make_async_remote_copy(
            src_ref=src, dst_ref=dst, send_sem=send_sem, recv_sem=recv_sem, device_id=where, device_id_type=MESH
        ).start()
        if self.recording:
            self.sent.setdefault(tag, []).append(again or (lambda: (src, send_sem)))

    def finish(self, tag):
        for again in self.sent.pop(tag, ()):
            ref, sem = again()
            pltpu.make_async_remote_copy(
                src_ref=ref, dst_ref=ref, send_sem=sem, recv_sem=sem, device_id={"tensor": self.down}, device_id_type=MESH
            ).wait_send()

    def arrived(self, ref, sem, send_sem, where):
        pltpu.make_async_remote_copy(
            src_ref=ref, dst_ref=ref, send_sem=send_sem, recv_sem=sem, device_id=where, device_id_type=MESH
        ).wait_recv()

    def drain(self):
        for tag in list(self.sent):
            self.finish(tag)


class Gather:
    def __init__(self, links, own, full, z_send, z_recv, p_send, p_recv):
        self.l, self.own, self.full = links, own, full
        self.z_send, self.z_recv, self.p_send, self.p_recv = z_send, z_recv, p_send, p_recv
        self.rows = own[0].shape[0] // links.n_dp
        self.split, self.units = gather_units(self.rows, links.n_t)
        self.part = self.rows // self.split
        self.at = {u: i for i, u in enumerate(self.units)}

    def piece(self, m, slot, index, h):
        first = pl.multiple_of(index * self.rows + h * self.part, 16)
        if slot == 0:
            return self.own[m].at[pl.ds(first, self.part), :]
        return self.full.at[m, slot, pl.ds(first, self.part), :]

    def send_z(self, m, k, h):
        l = self.l
        i = self.at[(m, k, h)]
        l.send(self.piece(m, k - 1, l.me, h), self.piece(m, k, l.me, h), self.z_send.at[i], self.z_recv.at[i], {"tensor": l.down},
               again=lambda: (self.like(), self.z_send.at[i]))

    def like(self):
        return self.full.at[0, 1, pl.ds(0, self.part), :]

    def start(self):
        for m, k, h in self.units:
            if k == 1:
                self.send_z(m, k, h)

    def share(self, i, j):
        m, k, h = self.units[i]
        l = self.l
        for bit in reversed(l.bits):
            if j == 0 or bit < low_bit(j):
                ref = self.piece(m, k, l.mix(j), h)
                l.send(ref, ref, self.p_send.at[i, j ^ bit], self.p_recv.at[i, j ^ bit], {"dp": l.flip(bit)},
                       again=lambda at=j ^ bit: (self.like(), self.p_send.at[i, at]))

    def take(self, i):
        m, k, h = self.units[i]
        l = self.l
        l.arrived(self.piece(m, k, l.me, h), self.z_recv.at[i], self.z_send.at[i], {"tensor": l.up})
        if k + 1 < l.n_t:
            self.send_z(m, k + 1, h)
        self.share(i, 0)

    def relay(self, i):
        m, k, h = self.units[i]
        l = self.l
        for j in sorted(range(1, l.n_dp), key=lambda j: (-low_bit(j), j)):
            l.arrived(self.piece(m, k, l.mix(j), h), self.p_recv.at[i, j], self.p_send.at[i, j], {"dp": l.flip(low_bit(j))})
            self.share(i, j)

    def walk(self, lag=2):
        for i in range(len(self.units) + lag):
            if i < len(self.units):
                self.take(i)
            if i >= lag:
                self.relay(i - lag)
                yield self.units[i - lag]


def gather_units(rows, n_t):
    split = 2 if rows % 32 == 0 else 1
    return split, [(m, k, h) for k in range(1, n_t) for m in range(3) for h in range(split)]


def level_start(n_dp, level):
    return sum(n_dp >> (t + 1) for t in range(level))


def add_rows(out, *terms):
    rows = out.shape[0]

    def body(r, _):
        at = pl.ds(pl.multiple_of(r * 16, 16), 16)
        total = terms[0][at, :].astype(F32)
        for t in terms[1:]:
            total = total + t[at, :].astype(F32)
        out[at, :] = total.astype(out.dtype)
        return 0

    lax.fori_loop(0, rows // 16, body, 0)


def reduce_scratch(n_dp, n_t, count, rows, c):
    dma = pltpu.SemaphoreType.DMA
    half = n_dp // 2
    return [
        pltpu.VMEM((3, n_dp * rows, c), BF16),
        pltpu.VMEM((2, half, rows, c), BF16),
        pltpu.VMEM((3, rows, c), BF16),
        pltpu.VMEM((3, rows, c), BF16),
        pltpu.VMEM((rows, c), F32),
        dma((count, n_dp)),
        dma((count, n_dp)),
        dma((count,)),
        dma((count,)),
        dma((2,)),
        dma((2,)),
        dma((3,)),
        dma(()),
    ]


def reduce_hbm(n_dp, n_t, count, rows, c):
    return [
        jax.ShapeDtypeStruct((count, n_dp // 2, rows, c), BF16),
        jax.ShapeDtypeStruct((count, n_dp - 1, rows, c), BF16),
        jax.ShapeDtypeStruct((count, rows, c), BF16),
    ]


class Reduce:
    def __init__(self, links, order, out, hbm, scratch):
        self.l, self.order, self.out = links, order, out
        self.sums, self.got, self.ring = hbm
        (self.block, self.fetched, self.terms, self.moving, self.final,
         self.c_send, self.c_recv, self.z_send, self.z_recv,
         self.f_sem, self.s_sem, self.t_sem, self.o_sem) = scratch
        self.at = {o: i for i, o in enumerate(order)}
        self.levels = len(links.bits)
        self.rows = self.fetched.shape[2]
        self.storing = None

    def before(self, i):
        m, s = self.order[i]
        return self.at.get((m, s + 1))

    def offsets(self, level):
        bits = self.l.bits[level + 1:]
        return [sum(b for n, b in enumerate(bits) if k >> n & 1) for k in range(1 << len(bits))]

    def mine(self, level):
        return lax.rem(self.l.me, 1 << (level + 1))

    def give(self, i, level, source):
        l, bit = self.l, self.l.bits[level]
        there = self.mine(level) + bit - 2 * bit * l.own_bit(bit)
        for n, off in enumerate(self.offsets(level)):
            at = (i, level_start(l.n_dp, level) + n)
            l.send(source(there + off), self.got.at[at], self.c_send.at[at], self.c_recv.at[at], {"dp": l.flip(bit)}, (i, level),
                   again=lambda at=at: (self.got.at[at], self.c_send.at[at]))

    def receive(self, i, level):
        l = self.l
        for n, _ in enumerate(self.offsets(level)):
            at = (i, level_start(l.n_dp, level) + n)
            l.arrived(self.got.at[at], self.c_recv.at[at], self.c_send.at[at], {"dp": l.flip(l.bits[level])})

    def clear(self, i):
        self.l.finish((i - 3, 0))

    def piece(self, i, p):
        return self.block.at[i % 3, pl.ds(pl.multiple_of(p * self.rows, 16), self.rows), :]

    def give_block(self, i):
        self.give(i, 0, lambda p: self.piece(i, p))

    def fetch_copy(self, i):
        return pltpu.make_async_copy(self.got.at[i, pl.ds(0, self.l.n_dp // 2)], self.fetched.at[i % 2], self.f_sem.at[i % 2])

    def fetch(self, i):
        self.receive(i, 0)
        self.fetch_copy(i).start()

    def store_copy(self, i):
        return pltpu.make_async_copy(self.fetched.at[i % 2], self.sums.at[i], self.s_sem.at[i % 2])

    def add_first(self, i):
        self.fetch_copy(i).wait()
        for n in range(self.l.n_dp // 2):
            here = self.fetched.at[i % 2, n]
            add_rows(here, self.piece(i, 2 * n + self.l.own_bit(1)), here)
        self.store_copy(i).start()

    def give_next(self, i):
        self.store_copy(i).wait()
        self.give(i, 1, lambda piece: self.sums.at[i, piece // 2])

    def steps(self, i):
        count = len(self.order)
        if i < count:
            self.give_block(i)
        if 0 <= i - 3 < count:
            self.give_next(i - 3)
        if 0 <= i - 1 < count:
            self.fetch(i - 1)
        if 0 <= i - 2 < count:
            self.add_first(i - 2)

    def middle(self, i, level):
        l = self.l
        self.receive(i, level)
        for n, off in enumerate(self.offsets(level)):
            piece = (self.mine(level) + off) // 2
            loads = [
                pltpu.make_async_copy(self.sums.at[i, piece], self.terms.at[0], self.t_sem.at[0]),
                pltpu.make_async_copy(self.got.at[i, level_start(l.n_dp, level) + n], self.terms.at[1], self.t_sem.at[1]),
            ]
            for c in loads:
                c.start()
            for c in loads:
                c.wait()
            add_rows(self.terms.at[2], self.terms.at[0], self.terms.at[1])
            back = pltpu.make_async_copy(self.terms.at[2], self.sums.at[i, piece], self.t_sem.at[2])
            back.start()
            back.wait()
        self.give(i, level + 1, lambda piece: self.sums.at[i, piece // 2])

    def term_copies(self, i):
        l = self.l
        return [
            pltpu.make_async_copy(self.sums.at[i, l.me // 2], self.terms.at[0], self.t_sem.at[0]),
            pltpu.make_async_copy(self.got.at[i, l.n_dp - 2], self.terms.at[1], self.t_sem.at[1]),
        ]

    def ring_copy(self, i):
        return pltpu.make_async_copy(self.ring.at[self.before(i)], self.terms.at[2], self.t_sem.at[2])

    def collect(self, i):
        self.receive(i, self.levels - 1)
        for c in self.term_copies(i):
            c.start()

    def out_copy(self, m):
        return pltpu.make_async_copy(self.final, self.out.at[m], self.o_sem)

    def pass_on(self, i):
        l = self.l
        m, s = self.order[i]
        b = self.before(i)
        if b is not None:
            l.arrived(self.ring.at[b], self.z_recv.at[b], self.z_send.at[b], {"tensor": l.down})
            self.ring_copy(i).start()
        for c in self.term_copies(i):
            c.wait()
        if b is not None:
            self.ring_copy(i).wait()
        terms = [self.terms.at[t] for t in range(2 if b is None else 3)]
        l.finish(("z", i - 3))
        if s > 0:
            add_rows(self.moving.at[i % 3], *terms)
            l.send(self.moving.at[i % 3], self.ring.at[i], self.z_send.at[i], self.z_recv.at[i], {"tensor": l.up}, ("z", i),
                   again=lambda: (self.moving.at[i % 3], self.z_send.at[i]))
        else:
            if self.storing is not None:
                self.out_copy(self.storing).wait()
            add_rows(self.final, *terms)
            self.out_copy(m).start()
            self.storing = m

    def last_step(self, i):
        for level in range(1, self.levels - 1):
            self.middle(i, level)
        self.collect(i)
        self.pass_on(i)

    def close(self):
        self.out_copy(self.storing).wait()


class Spread:
    def __init__(self, links, block, out, send, recv):
        self.l, self.block, self.out, self.send, self.recv = links, block, out, send, recv

    def pass_on(self, source, at, k):
        l = self.l
        l.send(source, self.out.at[at], self.send.at[k], self.recv.at[k], {"tensor": l.down},
               again=lambda: (self.out.at[0], self.send.at[k]))

    def start(self):
        self.pass_on(self.block, self.l.z, 0)

    def step(self, k):
        l = self.l
        at = lax.rem(l.z + k, l.n_t)
        l.arrived(self.out.at[at], self.recv.at[k - 1], self.send.at[k - 1], {"tensor": l.up})
        if k < l.n_t - 1:
            self.pass_on(self.out.at[at], at, k)


class Total:
    def __init__(self, links, block, buf, send, recv):
        self.l, self.block, self.buf, self.s, self.r = links, block, buf, send, recv
        self.levels = len(links.bits)
        self.count = self.levels + links.n_t

    def step(self, s):
        l, buf = self.l, self.buf
        if s == 0:
            buf[1] = self.block[...]
        else:
            l.arrived(buf.at[2 * s], self.r.at[s - 1], self.s.at[s - 1], {"tensor": l.up})
            if s <= self.levels:
                buf[2 * s + 1] = buf[2 * s - 1] + buf[2 * s]
        if s < self.levels:
            l.send(buf.at[2 * s + 1], buf.at[2 * s + 2], self.s.at[s], self.r.at[s], {"dp": l.flip(l.bits[s])})
        elif s < self.count - 1:
            src = 2 * s + 1 if s == self.levels else 2 * s
            l.send(buf.at[src], buf.at[2 * s + 2], self.s.at[s], self.r.at[s], {"tensor": l.down})

    def result(self):
        total = self.buf[2 * self.levels + 1]
        for k in range(1, self.l.n_t):
            total = total + self.buf[2 * (self.levels + k)]
        return total


def row_loop(rows, step, body):
    def turn(r, _):
        body(pl.ds(pl.multiple_of(r * step, step), step))
        return 0

    lax.fori_loop(0, rows // step, turn, 0)


def norm_rows(source, gain, out):
    def body(at):
        h = source[at, :].astype(F32)
        r = lax.rsqrt(jnp.mean(h * h, axis=1, keepdims=True) + EPS)
        out[at, :] = (h * r * gain).astype(BF16)

    row_loop(source.shape[0], 32, body)


def attend_slot(qkv, o, mask):
    heads = o.shape[1] // HEAD_SIZE
    for h in range(heads):
        q, k, v = (slice((t * heads + h) * HEAD_SIZE, (t * heads + h + 1) * HEAD_SIZE) for t in range(3))
        p = probabilities(qkv[:, q], qkv[:, k], mask).astype(BF16)
        o[:, q] = by_block(dot_nn, p, qkv[:, v]).astype(BF16)


class Loader:
    def __init__(self, buf, sem, blocks):
        self.buf, self.sem, self.blocks = buf, sem, blocks

    def copy(self, j):
        slot = j % self.buf.shape[0]
        return pltpu.make_async_copy(self.blocks[j], self.buf.at[slot], self.sem.at[slot])

    def start(self, j):
        if j < len(self.blocks):
            self.copy(j).start()

    def wait(self, j):
        self.copy(j).wait()
        return self.buf.at[j % self.buf.shape[0]]


def forward_kernel(
    n_dp, n_t, a_own, i_own, d_own, x0, gains, seg_col, seg_row, obs_row, cos, sin,
    full, xs, qkv_out, o_out, h2_out, act_out, slope_out, out,
    x, n, proj, qkv, o, h2, acc, act, slope, outb, mask, wbuf,
    w_sem, s_sem, y_send, y_recv, x_sem, z_send, z_recv, p_send, p_recv,
):
    l = Links(n_dp, n_t)
    section = lax.axis_index("section")
    first, second = section == 0, section != 0
    own = (a_own, i_own, d_own)
    g = Gather(l, own, full, z_send, z_recv, p_send, p_recv)
    other = {"section": 1 - section}
    l.greet([{"tensor": l.up}, other] + [{"dp": l.flip(b)} for b in l.bits])
    g.start()
    rows, d = x.shape
    wide = o.shape[2]

    def block(m, slot):
        return own[m] if slot == 0 else full.at[m, slot]

    order = [(0, s) for s in range(n_t)] + [(m, s) for s in range(n_t) for m in (1, 2)]
    load = Loader(wbuf, w_sem, [block(m, s) for m, s in order])
    stores = []

    def store(src, dst, sem):
        copy = pltpu.make_async_copy(src, dst, sem)
        copy.start()
        stores.append(copy)

    @pl.when(first)
    def _():
        copy = pltpu.make_async_copy(x0, x, x_sem)
        copy.start()
        copy.wait()

    write_mask(mask, seg_col, seg_row, obs_row)
    l.recording = False

    @pl.when(second)
    def _():
        for _ in g.walk():
            pass
        load.start(0)
        load.start(1)
        pltpu.make_async_remote_copy(
            src_ref=outb, dst_ref=x, send_sem=y_send, recv_sem=y_recv, device_id=other, device_id_type=MESH
        ).wait_recv()

    l.recording = True
    walk = g.walk()

    def until(m, slot):
        if slot > 0:
            for unit in walk:
                if unit == (m, slot, g.split - 1):
                    return

    store(x, xs, s_sem.at[0])
    norm_rows(x, gains[0:1, :], n)
    for s in range(n_t):
        @pl.when(first)
        def _():
            until(0, s)
            load.start(s)

        @pl.when(second)
        def _():
            load.start(s + 2)

        w = load.wait(s)
        proj[:, 0:3 * wide] = dot_nt(n[...], w[0:3 * wide, :])

        def turn_rows(at):
            v = proj[at, 0:2 * wide]
            qkv[s, at, 0:2 * wide] = (v * cos[at, :] + partner(v) * sin[at, :]).astype(BF16)
            qkv[s, at, 2 * wide:3 * wide] = proj[at, 2 * wide:3 * wide].astype(BF16)

        row_loop(rows, 32, turn_rows)
        attend_slot(qkv.at[s], o.at[s], mask)
        term = dot_nn(o[s], w[3 * wide:, :])
        if s == 0:
            acc[...] = term
        else:
            acc[...] = acc[...] + term
        store(qkv.at[s], qkv_out.at[s], s_sem.at[1 + s])
        store(o.at[s], o_out.at[s], s_sem.at[1 + n_t + s])

    def middle(at):
        h = x[at, :].astype(F32) + acc[at, :]
        h2[at, :] = h
        acc[at, :] = h
        r = lax.rsqrt(jnp.mean(h * h, axis=1, keepdims=True) + EPS)
        n[at, :] = (h * r * gains[1:2, :]).astype(BF16)

    row_loop(rows, 32, middle)
    store(h2, h2_out, s_sem.at[1 + 2 * n_t])
    spare = 2 + 2 * n_t
    for s in range(n_t):
        j = n_t + 2 * s

        @pl.when(first)
        def _():
            until(2, s)
            load.start(j)
            load.start(j + 1)

        @pl.when(second)
        def _():
            load.start(j + 2)

        w = load.wait(j)
        proj[...] = dot_nn(n[...], w[...])
        if s >= 2:
            for copy in stores[-4:-2]:
                copy.wait()
            del stores[-4:-2]

        def silu(at):
            u = proj[at, :]
            sig = lax.logistic(u)
            act[s % 2, at, :] = (u * sig).astype(BF16)
            slope[s % 2, at, :] = (sig * (1.0 + u * (1.0 - sig))).astype(BF16)

        row_loop(rows, 32, silu)

        @pl.when(second)
        def _():
            load.start(j + 3)

        w = load.wait(j + 1)
        acc[...] = acc[...] + dot_nn(act[s % 2], w[...])
        store(act.at[s % 2], act_out.at[s], s_sem.at[spare + 2 * (s % 2)])
        store(slope.at[s % 2], slope_out.at[s], s_sem.at[spare + 2 * (s % 2) + 1])

    def finish(at):
        outb[at, :] = acc[at, :].astype(BF16)

    row_loop(rows, 32, finish)
    over = pltpu.make_async_remote_copy(
        src_ref=outb, dst_ref=x, send_sem=y_send, recv_sem=y_recv, device_id=other, device_id_type=MESH
    )

    @pl.when(first)
    def _():
        over.start()

    store(outb, out, x_sem)
    for copy in stores:
        copy.wait()

    @pl.when(first)
    def _():
        over.wait_send()

    l.drain()


def run_forward(a_own, i_own, d_own, x0, gains, seg, obs, tables):
    n_dp, n_t = lax.axis_size("dp"), lax.axis_size("tensor")
    rows, d = x0.shape
    wide = a_own.shape[0] // 4
    count = len(gather_units(a_own.shape[0] // n_dp, n_t)[1])
    dma = pltpu.SemaphoreType.DMA
    hbm, vmem = pl.BlockSpec(memory_space=pl.ANY), pl.BlockSpec(memory_space=pltpu.VMEM)

    def shape(*s, t=BF16):
        return jax.ShapeDtypeStruct(s, t)

    return pl.pallas_call(
        functools.partial(forward_kernel, n_dp, n_t),
        out_shape=[
            shape(3, n_t, *a_own.shape), shape(rows, d), shape(n_t, rows, 3 * wide), shape(n_t, rows, wide),
            shape(rows, d, t=F32), shape(n_t, rows, i_own.shape[1]), shape(n_t, rows, i_own.shape[1]), shape(rows, d),
        ],
        in_specs=[hbm] * 4 + [vmem] * 6,
        out_specs=[hbm] * 8,
        scratch_shapes=[
            pltpu.VMEM((rows, d), BF16),
            pltpu.VMEM((rows, d), BF16),
            pltpu.VMEM((rows, d), F32),
            pltpu.VMEM((n_t, rows, 3 * wide), BF16),
            pltpu.VMEM((n_t, rows, wide), BF16),
            pltpu.VMEM((rows, d), F32),
            pltpu.VMEM((rows, d), F32),
            pltpu.VMEM((2, rows, d), BF16),
            pltpu.VMEM((2, rows, d), BF16),
            pltpu.VMEM((rows, d), BF16),
            pltpu.VMEM((ROW, 2 * QB), F32),
            pltpu.VMEM((3,) + a_own.shape, BF16),
            dma((3,)), dma((6 + 2 * n_t,)), dma(()), dma(()), dma(()),
            dma((count,)), dma((count,)), dma((count, n_dp)), dma((count, n_dp)),
        ],
        compiler_params=pltpu.CompilerParams(collective_id=0, has_side_effects=True, vmem_limit_bytes=60 * 2**20),
    )(a_own, i_own, d_own, x0, gains, seg[:, None], seg[None, :], obs[None, :], *tables)


def attend_slot_back(qkv, do, dqk, dcat, mask):
    wide = do.shape[1]
    heads = wide // HEAD_SIZE
    for h in range(heads):
        q, k, v = (slice((t * heads + h) * HEAD_SIZE, (t * heads + h + 1) * HEAD_SIZE) for t in range(3))
        qh, kh, vh, dh = qkv[:, q], qkv[:, k], qkv[:, v], do[:, q]
        p = probabilities(qh, kh, mask)
        dcat[:, v] = by_window(p.astype(BF16), dh).astype(BF16)
        dp = by_block(dot_nt, dh, vh)
        ds = (p * (dp - jnp.sum(p * dp, axis=1, keepdims=True))).astype(BF16)
        dqk[:, q] = by_block(dot_nn, ds, kh) * SCALE
        dqk[:, k] = by_window(ds, qh) * SCALE


def outer_product(out, left, right):
    step = left.shape[1] // 2

    def turn(j, _):
        at = pl.ds(pl.multiple_of(j * step, 128), step)
        out[at, :] = dot_tn(left[:, at], right[...]).astype(BF16)
        return 0

    lax.fori_loop(0, 2, turn, 0)


def norm_back_rows(g, dn, h, gain, gain_sum, write):
    gain_sum[...] = jnp.zeros_like(gain_sum)
    step = 32

    def body(at):
        hr, dr = h[at, :].astype(F32), dn[at, :]
        r = lax.rsqrt(jnp.mean(hr * hr, axis=1, keepdims=True) + EPS)
        y = gain * dr
        gain_sum[...] += jnp.sum((dr * hr * r).reshape(step // 8, 8, -1), axis=0)
        write(at, g[at, :].astype(F32) + r * y - hr * (r * r * r) * jnp.mean(hr * y, axis=1, keepdims=True))

    row_loop(h.shape[0], step, body)


def backward_kernel(
    n_dp, n_t, a_own, i_own, d_own, full, cot, xs, qkv_in, o_in, h2_in, act_in, slope_in, out_in, gains,
    seg_col, seg_row, obs_row, cos, sin,
    layer_acts, grad_acts, out_sums, out_gains, hbm_sums, hbm_got, hbm_ring, du_hbm,
    gbuf, act, du, n, h2, x, dn, ga, proj, qkv, o, do, dcat, dhb, mask, wbuf, gain0, gain1, gain_buf,
    w_sem, l_sem, a_sem, u_sem, q_sem, st_sem, y_send, y_recv, s1_send, s1_recv, s2_send, s2_recv, t_send, t_recv,
    *reduce_refs,
):
    section = lax.axis_index("section")
    first, second = section == 0, section != 0
    other = {"section": 1 - section}
    l, l2 = Links(n_dp, n_t), Links(n_dp, n_t)
    own = (a_own, i_own, d_own)
    rows, d = h2.shape
    wide = do.shape[1]
    slots = list(reversed(range(n_t)))
    order = [(m, s) for s in slots for m in (2, 1)] + [(0, s) for s in slots]
    ff = 2 * n_t
    hbm = (hbm_sums, hbm_got, hbm_ring)
    r = Reduce(l, order, out_sums, hbm, reduce_refs)
    r2 = Reduce(l2, order, out_sums, hbm, reduce_refs)
    spread1 = Spread(l, out_in, layer_acts, s1_send, s1_recv)
    spread1b = Spread(l2, out_in, layer_acts, s1_send, s1_recv)
    spread2 = Spread(l, dhb, grad_acts, s2_send, s2_recv)
    load = Loader(wbuf, w_sem, [own[m] if s == 0 else full.at[m, s] for m, s in order])

    l.greet([{"tensor": l.up}, {"tensor": l.down}, other] + [{"dp": l.flip(b)} for b in l.bits])
    spread1.start()
    load.start(0)
    load.start(1)

    def local(src, dst, sem):
        return pltpu.make_async_copy(src, dst, sem)

    acts_in = local(out_in, dhb, l_sem.at[0])
    acts_out = local(dhb, layer_acts.at[l.z], l_sem.at[0])
    h2_copy = local(h2_in, h2, l_sem.at[1])
    x_copy = local(xs, x, l_sem.at[2])
    o_copy = local(o_in, o, l_sem.at[3])
    for c in (acts_in, h2_copy, x_copy, o_copy):
        c.start()

    def act_copy(j):
        return local(act_in.at[slots[j]], act.at[j % 2], a_sem.at[j % 2])

    def slope_copy(j):
        return local(slope_in.at[slots[j]], du.at[j % 2], u_sem.at[j % 2])

    def du_out(j):
        return local(du.at[j % 2], du_hbm.at[slots[j]], st_sem.at[j % 2])

    def du_in(j):
        return local(du_hbm.at[slots[j]], du.at[j % 2], u_sem.at[j % 2])

    def qkv_copy(j):
        return local(qkv_in.at[slots[j]], qkv.at[j % 2], q_sem.at[j % 2])

    act_copy(0).start()
    slope_copy(0).start()
    write_mask(mask, seg_col, seg_row, obs_row)
    h2_copy.wait()
    norm_rows(h2, gains[1:2, :], n)
    acts_in.wait()
    acts_out.start()
    arrival = pltpu.make_async_remote_copy(
        src_ref=dhb, dst_ref=gbuf, send_sem=y_send, recv_sem=y_recv, device_id=other, device_id_type=MESH
    )
    cot_copy = local(cot, gbuf, l_sem.at[4])

    @pl.when(second)
    def _():
        cot_copy.start()
        cot_copy.wait()

    @pl.when(first)
    def _():
        for k in range(1, n_t - 1):
            spread1.step(k)
        arrival.wait_recv()

    def block_of(reducer, i):
        if i >= 3:
            reducer.clear(i)
        return reducer.block.at[i % 3]

    for j in range(n_t):
        if j + 1 < n_t:
            act_copy(j + 1).start()
            if j + 1 >= 2:
                du_out(j - 1).wait()
            slope_copy(j + 1).start()
        w = load.wait(2 * j)
        proj[...] = dot_nt(gbuf[...], w[...])
        load.start(2 * j + 2)
        slope_copy(j).wait()

        def scale(at):
            du[j % 2, at, :] = (proj[at, :] * du[j % 2, at, :].astype(F32)).astype(BF16)

        row_loop(rows, 32, scale)
        du_out(j).start()
        act_copy(j).wait()

        @pl.when(first)
        def _():
            outer_product(block_of(r, 2 * j), gbuf, act.at[j % 2])
            r.steps(2 * j)

        w = load.wait(2 * j + 1)
        if j == 0:
            dn[...] = dot_nt(du[j % 2], w[...])
        else:
            dn[...] = dn[...] + dot_nt(du[j % 2], w[...])
        load.start(2 * j + 3)

        @pl.when(first)
        def _():
            outer_product(block_of(r, 2 * j + 1), n, du.at[j % 2])
            r.steps(2 * j + 1)

    for j in range(max(n_t - 2, 0), n_t):
        du_out(j).wait()

    @pl.when(second)
    def _():
        for k in range(1, n_t - 1):
            spread1b.step(k)

    qkv_copy(0).start()

    def write_middle(at, value):
        h2[at, :] = value
        ga[at, :] = value.astype(BF16)

    norm_back_rows(gbuf, dn, h2, gains[1:2, :], gain1, write_middle)
    o_copy.wait()

    for j, s in enumerate(slots):
        if j + 1 < n_t:
            qkv_copy(j + 1).start()
        w = load.wait(ff + j)
        load.start(ff + j + 2)
        do[...] = dot_nt(ga[...], w[3 * wide:, :]).astype(BF16)
        qkv_copy(j).wait()
        attend_slot_back(qkv.at[j % 2], do, proj, dcat.at[s], mask)

        def turn_back(at):
            v = proj[at, 0:2 * wide]
            dcat[s, at, 0:2 * wide] = (v * cos[at, :] - partner(v) * sin[at, :]).astype(BF16)

        row_loop(rows, 32, turn_back)
        if j == 0:
            dn[...] = dot_nn(dcat[s], w[0:3 * wide, :])
        else:
            dn[...] = dn[...] + dot_nn(dcat[s], w[0:3 * wide, :])
        if j < 2:
            @pl.when(first)
            def _():
                r.last_step(j)
    x_copy.wait()
    acts_out.wait()

    def write_input(at, value):
        dhb[at, :] = value.astype(BF16)

    norm_back_rows(h2, dn, x, gains[0:1, :], gain0, write_input)
    over = pltpu.make_async_remote_copy(
        src_ref=dhb, dst_ref=gbuf, send_sem=y_send, recv_sem=y_recv, device_id=other, device_id_type=MESH
    )

    @pl.when(second)
    def _():
        over.start()

    spread2.start()
    grads_out = local(dhb, grad_acts.at[l.z], l_sem.at[0])
    grads_out.start()

    @pl.when(second)
    def _():
        du_in(0).start()
        act_copy(0).start()
        for j in range(n_t):
            if j + 1 < n_t:
                act_copy(j + 1).start()
                du_in(j + 1).start()
            act_copy(j).wait()
            outer_product(block_of(r2, 2 * j), gbuf, act.at[j % 2])
            r2.steps(2 * j)
            du_in(j).wait()
            outer_product(block_of(r2, 2 * j + 1), n, du.at[j % 2])
            r2.steps(2 * j + 1)
        r2.last_step(0)
        r2.last_step(1)

    total = Total(l, gain0, gain_buf, t_send, t_recv)
    gain0[0:1, :] = jnp.sum(gain0[...], axis=0, keepdims=True)
    gain0[1:2, :] = jnp.sum(gain1[...], axis=0, keepdims=True)
    norm_rows(x, gains[0:1, :], n)
    for j, s in enumerate(slots):
        b = block_of(r, ff + j)
        step = d // 2

        def turn(c, _):
            at = pl.ds(pl.multiple_of(c * step, 128), step)
            b[at, 0:3 * wide] = dot_tn(n[:, at], dcat[s]).astype(BF16)
            b[at, 3 * wide:] = dot_tn(ga[:, at], o[s]).astype(BF16)
            return 0

        lax.fori_loop(0, 2, turn, 0)
        r.steps(ff + j)
        total.step(j)
    for i in range(3):
        r.steps(ff + n_t + i)
        total.step(n_t + i) if n_t + i < total.count else None
    for t in range(n_t + 3, total.count):
        total.step(t)
    for i in range(2, len(order)):
        r.last_step(i)
        if i == 3 or i == 5:
            spread2.step((i - 1) // 2)
    spread1.step(n_t - 1)
    spread2.step(n_t - 1)
    out_gains[...] = total.result()
    r.close()
    grads_out.wait()

    @pl.when(second)
    def _():
        over.wait_send()

    l.drain()


def run_backward(a_own, i_own, d_own, kept, cot, gains, seg, obs, tables):
    n_dp, n_t = lax.axis_size("dp"), lax.axis_size("tensor")
    rows, d = cot.shape
    wide = a_own.shape[0] // 4
    piece = d // n_dp
    count = 3 * n_t
    steps = len(ring_bits(n_dp)) + n_t
    dma = pltpu.SemaphoreType.DMA
    hbm, vmem = pl.BlockSpec(memory_space=pl.ANY), pl.BlockSpec(memory_space=pltpu.VMEM)

    def shape(*s, t=BF16):
        return jax.ShapeDtypeStruct(s, t)

    def buf(*s, t=BF16):
        return pltpu.VMEM(s, t)

    return pl.pallas_call(
        functools.partial(backward_kernel, n_dp, n_t),
        out_shape=[
            shape(n_t, rows, d), shape(n_t, rows, d), shape(3, piece, d, t=F32), shape(8, d, t=F32),
            *reduce_hbm(n_dp, n_t, count, piece, d), shape(n_t, rows, d),
        ],
        in_specs=[hbm] * 12 + [vmem] * 6,
        out_specs=[hbm] * 3 + [vmem] + [hbm] * 4,
        scratch_shapes=[
            buf(rows, d), buf(2, rows, d), buf(2, rows, d), buf(rows, d), buf(rows, d, t=F32), buf(rows, d),
            buf(rows, d, t=F32), buf(rows, d), buf(rows, d, t=F32), buf(2, rows, 3 * wide), buf(n_t, rows, wide),
            buf(rows, wide), buf(n_t, rows, 3 * wide), buf(rows, d), buf(ROW, 2 * QB, t=F32), buf(3, *a_own.shape),
            buf(8, d, t=F32), buf(8, d, t=F32), buf(2 * steps, 8, d, t=F32),
            dma((3,)), dma((5,)), dma((2,)), dma((2,)), dma((2,)), dma((2,)), dma(()), dma(()),
            dma((n_t,)), dma((n_t,)), dma((n_t,)), dma((n_t,)), dma((steps,)), dma((steps,)),
            *reduce_scratch(n_dp, n_t, count, piece, d),
        ],
        compiler_params=pltpu.CompilerParams(collective_id=1, has_side_effects=True, vmem_limit_bytes=62 * 2**20),
    )(a_own, i_own, d_own, kept[0], cot, *kept[1:], gains, seg[:, None], seg[None, :], obs[None, :], *tables)


def own_rows(x, count):
    flat = x.reshape((-1,) + x.shape[2:])
    return lax.dynamic_slice_in_dim(flat, lax.axis_index("tensor") * count, count, 0)


def on_device(tokens, cotangent, seg_ids, observed, w_qkv, w_out, w_in, w_down, norm_gains):
    n_dp, n_t = lax.axis_size("dp"), lax.axis_size("tensor")
    w_qkv, w_out, w_in, w_down, gains = w_qkv[0], w_out[0], w_in[0], w_down[0], norm_gains[0]
    micro, rows, d = tokens.shape
    hd = w_out.shape[0]
    count = micro * rows // n_t
    tables = rope_tables()
    stack = jnp.concatenate([jnp.swapaxes(w_qkv, 1, 2), w_out[None]], axis=0).reshape(4 * hd, d)
    x0 = own_rows(tokens, count)
    g1 = own_rows(cotangent, count)
    seg, obs = own_rows(seg_ids, count), own_rows(observed, count)
    kept = run_forward(stack, w_in, w_down, x0, gains, seg, obs, tables)
    layer_acts, grad_acts, sums, gain = run_backward(stack, w_in, w_down, kept, g1, gains, seg, obs, tables)[:4]
    piece = d // n_dp
    gain = lax.dynamic_slice_in_dim(gain[:2], lax.axis_index("dp") * piece, piece, 1)
    r_attn, r_in, r_down = sums[0], sums[1], sums[2]
    r_qkv = jnp.stack([r_attn[:, i * hd:(i + 1) * hd] for i in range(3)])
    return (
        layer_acts.reshape(1, micro, rows, d),
        grad_acts.reshape(1, micro, rows, d),
        r_qkv[None],
        r_attn[:, 3 * hd:].T[None],
        r_in[None],
        r_down.T[None],
        gain[None],
    )


def solution(mesh):
    return jax.shard_map(
        on_device,
        mesh=mesh,
        in_specs=(
            P(None, "dp", None),
            P(None, "dp", None),
            P(None, "dp"),
            P(None, "dp"),
            P("section", None, None, "tensor"),
            P("section", "tensor", None),
            P("section", None, "tensor"),
            P("section", "tensor", None),
            P("section", None, None),
        ),
        out_specs=(
            P("section", None, "dp", None),
            P("section", None, "dp", None),
            P("section", None, "dp", "tensor"),
            P("section", "tensor", "dp"),
            P("section", "dp", "tensor"),
            P("section", "tensor", "dp"),
            P("section", None, "dp"),
        ),
        check_vma=False,
    )
```

time: 1190 us -> 829 us (0.70)
  matrix products: 246 us -> 0 us
  local copies, waits for them, and re-layouts: 133 us -> 25.1 us
  Pallas kernels: 707 us -> 790 us
  waiting for transfers between devices: 56.4 us -> 0 us
  other arithmetic: 25.4 us -> 3.6 us
  starting transfers between devices: 14.2 us -> 0 us
    dot_general x52 -> x0, matrix products: 246 us -> none  [the longest x20 109 us: dot_nn(): lax.dot_general(a, b, (((1,), (0,)), ((), ())), preferred_element_type=F32)]
    pallas_call x6 -> x2, Pallas kernels: 707 us -> 790 us  [the longest x1 548 us: run_backward(): pl.pallas_call(functools.partial(backward_kernel, n_dp, n_t), out_shape=[...]
    another operation x15 -> x0, local copies, waits for them, and re-layouts: 65.9 us -> none  [the longest x9 59.9 us: on_device(): blocks = jnp.stack(blocks).reshape(3 * n_t, n_dp, piece, -1)]
    ppermute x5 -> x0, waiting for transfers between devices: 56.4 us -> none  [the longest x1 26.3 us: on_device(): arriving = lax.ppermute(out0.astype(BF16), 'section', [(0, 1)])]
    unnamed x161 -> x15, local copies, waits for them, and re-layouts: 42 us -> 10.5 us
    ppermute x5 -> x0, starting transfers between devices: 14.2 us -> none  [the longest x3 8.39 us: turn(): return lax.ppermute(x, axis, [(i, (i + step) % n) for i in range(n)])]
  transfers between devices with their start and end apart: 5 -> 0, of which waited for: 3 -> 0; matrix products, arithmetic and copies ran while one was open for 18% -> 0% of each run, Pallas kernels for 28% -> 0%
where the time goes in v3:
time: 829 us; the launch traced here: 820 us
  Pallas kernels  790 us (95%)
  local copies, waits for them, and re-layouts  25.1 us (3%)
    pallas_call x1, Pallas kernels, run_backward(): pl.pallas_call(functools.partial(backward_kernel, n_dp, n_t), out_shape=[...  548 us
    pallas_call x1, Pallas kernels, run_forward(): pl.pallas_call(functools.partial(forward_kernel, n_dp, n_t), out_shape=[s...  242 us

profile of v3, /device:TPU:0, one launch (start us, length us, event | category | flops | bytes accessed | tf_op | source)
XLA Modules:
  0.0 819.9 jit_solution(15553502664275720890)
XLA Ops:
  0.7 0.7 copy.29
  1.4 0.1 dynamic_slice.16
  1.4 0.0 copy-start.2
  1.4 0.7 copy.28
  2.1 0.6 dynamic_slice.17
  2.8 0.4 fusion.2
  3.2 0.9 copy.17.seg_col
  4.0 0.1 tile.8
  4.2 1.5 copy.18.cos
  5.7 0.0 copy-done.2
  5.7 0.1 tile.20
  5.8 1.5 copy.19.sin
  7.3 0.0 copy-start
  7.3 0.0 copy-start.1
  7.3 3.5 constant_dynamic-slice_fusion
  10.8 0.0 copy-done
  10.8 0.0 copy-done.1
  10.8 2.0 pad_maximum_fusion
  12.8 242.4 %shard_map.144 = (bf16[3,4,1280,1280]{3,2,1,0:T(8,128)(2,1)}, bf16[512,1280]{1,0:T(8,128)(2,1)}, bf16[4,512,960]{2,1,0:T(8,128)(2,1)}, bf16[4,512,320]{2,1,0:T(8...) custom-call(bf16[1280,1280]{1,0:T(8,128)(2,1)} %bitcast.46, ...), custom_call_target="tpu_custom_call" | custom-call | tf_op jit(solution)/shard_map/pallas_call | solution.py:670
  255.3 547.7 %shard_map.145 = (bf16[4,512,1280]{2,1,0:T(8,128)(2,1)}, bf16[4,512,1280]{2,1,0:T(8,128)(2,1)}, f32[3,320,1280]{2,1,0:T(8,128)}, f32[8,1280]{1,0:T(8,128)}, bf16...) custom-call(bf16[1280,1280]{1,0:T(8,128)(2,1)} %bitcast.47, ...), custom_call_target="tpu_custom_call" | custom-call | tf_op jit(solution)/shard_map/pallas_call | solution.py:987
  802.9 0.8 slice.31
  803.7 0.7 dynamic-slice_bitcast_fusion
  804.4 4.4 slice_bitcast_fusion
  808.8 0.3 slice_bitcast_fusion.2
  809.1 1.0 copy.23
  810.1 0.0 slice-start
  810.1 1.2 maximum_bitcast_fusion
  811.3 0.0 slice-start.1
  811.3 5.8 copy.32
  817.1 0.0 slice-done
  817.1 0.0 slice-done.1
  817.1 2.4 copy.33
  (3 shorter events, 0.0 us)
Async XLA Ops:
  1.4 4.2 copy-start.2
  7.3 3.5 copy-start
  7.3 3.5 copy-start.1
  810.1 7.0 slice-start
  811.3 5.8 slice-start.1

commit v4 on v3

--- a/solution.py
+++ b/solution.py
@@ -115,6 +115,10 @@
                 at = at + bit - 2 * bit * lax.rem(self.me // bit, 2)
         return at
 
+    def place(self, table):
+        n = self.n_t
+        return sum(v * (1 - ((self.z - k) * (self.z - k) + n * n - 1) // (n * n)) for k, v in enumerate(table))
+
     def own_bit(self, bit):
         return lax.rem(self.me // bit, 2)
 
@@ -124,19 +128,25 @@
             pl.semaphore_signal(barrier, inc=1, device_id=where, device_id_type=MESH)
         pl.semaphore_wait(barrier, len(axes))
 
-    def send(self, src, dst, send_sem, recv_sem, where, tag=None, again=None):
+    def send(self, src, dst, send_sem, recv_sem, where, tag=None, again=None, when=None):
         pltpu.make_async_remote_copy(
             src_ref=src, dst_ref=dst, send_sem=send_sem, recv_sem=recv_sem, device_id=where, device_id_type=MESH
         ).start()
         if self.recording:
-            self.sent.setdefault(tag, []).append(again or (lambda: (src, send_sem)))
+            self.sent.setdefault(tag, []).append((again or (lambda: (src, send_sem)), when))
 
     def finish(self, tag):
-        for again in self.sent.pop(tag, ()):
+        def left(again):
             ref, sem = again()
             pltpu.make_async_remote_copy(
                 src_ref=ref, dst_ref=ref, send_sem=sem, recv_sem=sem, device_id={"tensor": self.down}, device_id_type=MESH
             ).wait_send()
+
+        for again, when in self.sent.pop(tag, ()):
+            if when is None:
+                left(again)
+            else:
+                pl.when(when())(functools.partial(left, again))
 
     def arrived(self, ref, sem, send_sem, where):
         pltpu.make_async_remote_copy(
@@ -174,7 +184,7 @@
 
     def start(self):
         for m, k, h in self.units:
-            if k == 1:
+            if k == 1 and m < 2:
                 self.send_z(m, k, h)
 
     def share(self, i, j):
@@ -192,6 +202,8 @@
         l.arrived(self.piece(m, k, l.me, h), self.z_recv.at[i], self.z_send.at[i], {"tensor": l.up})
         if k + 1 < l.n_t:
             self.send_z(m, k + 1, h)
+        if (m, k) == (0, 1):
+            self.send_z(2, 1, h)
         self.share(i, 0)
 
     def relay(self, i):
@@ -212,7 +224,10 @@
 
 def gather_units(rows, n_t):
     split = 2 if rows % 32 == 0 else 1
-    return split, [(m, k, h) for k in range(1, n_t) for m in range(3) for h in range(split)]
+    heads = [(0, k) for k in range(1, n_t)]
+    rest = [(m, k) for k in range(1, n_t) for m in (1, 2)]
+    mixed = [u for pair in zip(heads, rest) for u in pair] + rest[len(heads):]
+    return split, [(m, k, h) for m, k in mixed for h in range(split)]
 
 
 def level_start(n_dp, level):
@@ -245,7 +260,7 @@
         dma((count, n_dp)),
         dma((count, n_dp)),
         dma((count,)),
-        dma((count,)),
+        dma((count // n_t, n_t, 2)),
         dma((2,)),
         dma((2,)),
         dma((3,)),
@@ -257,25 +272,36 @@
     return [
         jax.ShapeDtypeStruct((count, n_dp // 2, rows, c), BF16),
         jax.ShapeDtypeStruct((count, n_dp - 1, rows, c), BF16),
-        jax.ShapeDtypeStruct((count, rows, c), BF16),
+        jax.ShapeDtypeStruct((count // n_t, n_t, 2, rows, c), BF16),
     ]
 
 
+def line_order(n_t):
+    return [sorted(range(n_t), key=lambda s: (-abs(s - z), -max(s, n_t - 1 - s))) for z in range(n_t)]
+
+
+class Places:
+    def __init__(self, links):
+        n_t = links.n_t
+        orders = line_order(n_t)
+        self.shard = [links.place([o[j] for o in orders]) for j in range(n_t)]
+        self.slot = [links.place([(o[j] - z) % n_t for z, o in enumerate(orders)]) for j in range(n_t - 1)] + [0]
+        self.up = [links.place([int(o[j] > z) for z, o in enumerate(orders)]) for j in range(n_t)]
+        self.below = (links.z + n_t - 1) // n_t
+        self.above = (2 * n_t - 2 - links.z) // n_t
+
+
 class Reduce:
-    def __init__(self, links, order, out, hbm, scratch):
-        self.l, self.order, self.out = links, order, out
+    def __init__(self, links, places, order, out, hbm, scratch):
+        self.l, self.places, self.order, self.out = links, places, order, out
         self.sums, self.got, self.ring = hbm
         (self.block, self.fetched, self.terms, self.moving, self.final,
          self.c_send, self.c_recv, self.z_send, self.z_recv,
          self.f_sem, self.s_sem, self.t_sem, self.o_sem) = scratch
-        self.at = {o: i for i, o in enumerate(order)}
+        self.moves = []
         self.levels = len(links.bits)
         self.rows = self.fetched.shape[2]
         self.storing = None
-
-    def before(self, i):
-        m, s = self.order[i]
-        return self.at.get((m, s + 1))
 
     def offsets(self, level):
         bits = self.l.bits[level + 1:]
@@ -298,9 +324,6 @@
             at = (i, level_start(l.n_dp, level) + n)
             l.arrived(self.got.at[at], self.c_recv.at[at], self.c_send.at[at], {"dp": l.flip(l.bits[level])})
 
-    def clear(self, i):
-        self.l.finish((i - 3, 0))
-
     def piece(self, i, p):
         return self.block.at[i % 3, pl.ds(pl.multiple_of(p * self.rows, 16), self.rows), :]
 
@@ -328,16 +351,29 @@
         self.store_copy(i).wait()
         self.give(i, 1, lambda piece: self.sums.at[i, piece // 2])
 
-    def steps(self, i):
-        count = len(self.order)
-        if i < count:
-            self.give_block(i)
-        if 0 <= i - 3 < count:
-            self.give_next(i - 3)
-        if 0 <= i - 1 < count:
-            self.fetch(i - 1)
-        if 0 <= i - 2 < count:
-            self.add_first(i - 2)
+    def push(self, i):
+        self.give_block(i)
+        self.moves.append([i, 0])
+
+    def pump(self):
+        for move in list(self.moves):
+            i, stage = move
+            if stage == 1 and any(o[0] == i - 2 for o in self.moves):
+                break
+            if stage > 0:
+                (self.fetch, self.add_first, self.give_next)[stage - 1](i)
+            move[1] += 1
+            if move[1] == 4:
+                self.moves.remove(move)
+
+    def flush(self, i=None):
+        while any(i is None or o[0] <= i for o in self.moves):
+            self.pump()
+
+    def clear(self, i):
+        while any(o[0] == i - 3 and o[1] < 3 for o in self.moves):
+            self.pump()
+        self.l.finish((i - 3, 0))
 
     def middle(self, i, level):
         l = self.l
@@ -365,9 +401,6 @@
             pltpu.make_async_copy(self.got.at[i, l.n_dp - 2], self.terms.at[1], self.t_sem.at[1]),
         ]
 
-    def ring_copy(self, i):
-        return pltpu.make_async_copy(self.ring.at[self.before(i)], self.terms.at[2], self.t_sem.at[2])
-
     def collect(self, i):
         self.receive(i, self.levels - 1)
         for c in self.term_copies(i):
@@ -376,31 +409,52 @@
     def out_copy(self, m):
         return pltpu.make_async_copy(self.final, self.out.at[m], self.o_sem)
 
+    def come(self, m, s, way):
+        l = self.l
+        ref = self.ring.at[m, s, way]
+        l.arrived(ref, self.z_recv.at[m, s, way], self.z_send.at[0], {"tensor": l.down})
+        copy = pltpu.make_async_copy(ref, self.terms.at[2], self.t_sem.at[2])
+        copy.start()
+        copy.wait()
+
     def pass_on(self, i):
-        l = self.l
-        m, s = self.order[i]
-        b = self.before(i)
-        if b is not None:
-            l.arrived(self.ring.at[b], self.z_recv.at[b], self.z_send.at[b], {"tensor": l.down})
-            self.ring_copy(i).start()
-        for c in self.term_copies(i):
-            c.wait()
-        if b is not None:
-            self.ring_copy(i).wait()
-        terms = [self.terms.at[t] for t in range(2 if b is None else 3)]
+        l, p = self.l, self.places
+        m, j = self.order[i]
         l.finish(("z", i - 3))
-        if s > 0:
-            add_rows(self.moving.at[i % 3], *terms)
-            l.send(self.moving.at[i % 3], self.ring.at[i], self.z_send.at[i], self.z_recv.at[i], {"tensor": l.up}, ("z", i),
-                   again=lambda: (self.moving.at[i % 3], self.z_send.at[i]))
+        terms = [self.terms.at[t] for t in range(3)]
+        if j < l.n_t - 1:
+            s, up, out = p.shard[j], p.up[j], self.moving.at[i % 3]
+            behind = up * p.below + (1 - up) * p.above
+            for c in self.term_copies(i):
+                c.wait()
+
+            @pl.when(behind == 1)
+            def _():
+                self.come(m, s, 1 - up)
+                add_rows(out, *terms)
+
+            @pl.when(behind == 0)
+            def _():
+                add_rows(out, *terms[:2])
+
+            l.send(out, self.ring.at[m, s, 1 - up], self.z_send.at[i], self.z_recv.at[m, s, 1 - up], {"tensor": l.z + 2 * up - 1},
+                   ("z", i), again=lambda: (self.moving.at[i % 3], self.z_send.at[i]))
         else:
             if self.storing is not None:
                 self.out_copy(self.storing).wait()
-            add_rows(self.final, *terms)
+            for c in self.term_copies(i):
+                c.wait()
+            add_rows(self.final, *terms[:2])
+            for way, there in ((0, p.below), (1, p.above)):
+                @pl.when(there == 1)
+                def _():
+                    self.come(m, l.z, way)
+                    add_rows(self.final, self.final, terms[2])
             self.out_copy(m).start()
             self.storing = m
 
     def last_step(self, i):
+        self.flush(i)
         for level in range(1, self.levels - 1):
             self.middle(i, level)
         self.collect(i)
@@ -411,23 +465,39 @@
 
 
 class Spread:
-    def __init__(self, links, block, out, send, recv):
-        self.l, self.block, self.out, self.send, self.recv = links, block, out, send, recv
-
-    def pass_on(self, source, at, k):
-        l = self.l
-        l.send(source, self.out.at[at], self.send.at[k], self.recv.at[k], {"tensor": l.down},
-               again=lambda: (self.out.at[0], self.send.at[k]))
+    def __init__(self, links, places, block, out, send, recv):
+        self.l, self.places, self.block, self.out, self.send, self.recv = links, places, block, out, send, recv
+
+    def pass_on(self, source, at, way, k):
+        l, p = self.l, self.places
+        l.send(source, self.out.at[at], self.send.at[way, k], self.recv.at[way, k], {"tensor": l.z + 1 - 2 * way},
+               again=lambda: (self.out.at[0], self.send.at[way, k]),
+               when=lambda: ((p.above, p.below)[way] == 1) if k == 0 else self.passes(way, k))
+
+    def passes(self, way, k):
+        z, n = self.l.z, self.l.n_t
+        return (z >= k) & (z < n - 1) if way == 0 else (z < n - k) & (z > 0)
 
     def start(self):
-        self.pass_on(self.block, self.l.z, 0)
+        p = self.places
+        for way, there in ((0, p.above), (1, p.below)):
+            @pl.when(there == 1)
+            def _():
+                self.pass_on(self.block, self.l.z, way, 0)
 
     def step(self, k):
         l = self.l
-        at = lax.rem(l.z + k, l.n_t)
-        l.arrived(self.out.at[at], self.recv.at[k - 1], self.send.at[k - 1], {"tensor": l.up})
-        if k < l.n_t - 1:
-            self.pass_on(self.out.at[at], at, k)
+        for way in range(2):
+            at = l.z + k * (2 * way - 1)
+
+            @pl.when(l.z >= k if way == 0 else l.z < l.n_t - k)
+            def _():
+                l.arrived(self.out.at[at], self.recv.at[way, k - 1], self.send.at[way, k - 1], {"tensor": l.down})
+
+            if k < l.n_t - 1:
+                @pl.when(self.passes(way, k))
+                def _():
+                    self.pass_on(self.out.at[at], at, way, k)
 
 
 class Total:
@@ -548,13 +618,16 @@
         ).wait_recv()
 
     l.recording = True
-    walk = g.walk()
+    walk, here = g.walk(), set()
 
     def until(m, slot):
-        if slot > 0:
-            for unit in walk:
-                if unit == (m, slot, g.split - 1):
-                    return
+        while slot > 0 and (m, slot, g.split - 1) not in here:
+            here.add(next(walk))
+
+    def tick():
+        @pl.when(first)
+        def _():
+            here.add(next(walk, None))
 
     store(x, xs, s_sem.at[0])
     norm_rows(x, gains[0:1, :], n)
@@ -577,7 +650,9 @@
             qkv[s, at, 2 * wide:3 * wide] = proj[at, 2 * wide:3 * wide].astype(BF16)
 
         row_loop(rows, 32, turn_rows)
+        tick()
         attend_slot(qkv.at[s], o.at[s], mask)
+        tick()
         term = dot_nn(o[s], w[3 * wide:, :])
         if s == 0:
             acc[...] = term
@@ -623,6 +698,8 @@
             slope[s % 2, at, :] = (sig * (1.0 + u * (1.0 - sig))).astype(BF16)
 
         row_loop(rows, 32, silu)
+        if s > 0:
+            tick()
 
         @pl.when(second)
         def _():
@@ -637,6 +714,7 @@
         outb[at, :] = acc[at, :].astype(BF16)
 
     row_loop(rows, 32, finish)
+    assert len(here - {None}) == len(g.units)
     over = pltpu.make_async_remote_copy(
         src_ref=outb, dst_ref=x, send_sem=y_send, recv_sem=y_recv, device_id=other, device_id_type=MESH
     )
@@ -739,26 +817,31 @@
     seg_col, seg_row, obs_row, cos, sin,
     layer_acts, grad_acts, out_sums, out_gains, hbm_sums, hbm_got, hbm_ring, du_hbm,
     gbuf, act, du, n, h2, x, dn, ga, proj, qkv, o, do, dcat, dhb, mask, wbuf, gain0, gain1, gain_buf,
-    w_sem, l_sem, a_sem, u_sem, q_sem, st_sem, y_send, y_recv, s1_send, s1_recv, s2_send, s2_recv, t_send, t_recv,
+    w_sem, l_sem, o_sem, a_sem, u_sem, q_sem, st_sem, y_send, y_recv, s1_send, s1_recv, s2_send, s2_recv, t_send, t_recv,
     *reduce_refs,
 ):
     section = lax.axis_index("section")
     first, second = section == 0, section != 0
     other = {"section": 1 - section}
-    l, l2 = Links(n_dp, n_t), Links(n_dp, n_t)
+    l, l2, l3 = (Links(n_dp, n_t) for _ in range(3))
     own = (a_own, i_own, d_own)
     rows, d = h2.shape
     wide = do.shape[1]
-    slots = list(reversed(range(n_t)))
-    order = [(m, s) for s in slots for m in (2, 1)] + [(0, s) for s in slots]
+    places = Places(l)
+    slots = places.slot
+    order = [(m, j) for j in range(n_t) for m in (2, 1)] + [(0, j) for j in range(n_t)]
     ff = 2 * n_t
     hbm = (hbm_sums, hbm_got, hbm_ring)
-    r = Reduce(l, order, out_sums, hbm, reduce_refs)
-    r2 = Reduce(l2, order, out_sums, hbm, reduce_refs)
-    spread1 = Spread(l, out_in, layer_acts, s1_send, s1_recv)
-    spread1b = Spread(l2, out_in, layer_acts, s1_send, s1_recv)
-    spread2 = Spread(l, dhb, grad_acts, s2_send, s2_recv)
-    load = Loader(wbuf, w_sem, [own[m] if s == 0 else full.at[m, s] for m, s in order])
+    r = Reduce(l, places, order, out_sums, hbm, reduce_refs)
+    rm = Reduce(l3, places, order, out_sums, hbm, reduce_refs)
+    inner = places.below * places.above == 1
+    end_first, inner_first = first & ~inner, first & inner
+    r2 = Reduce(l2, places, order, out_sums, hbm, reduce_refs)
+    spread1 = Spread(l, places, out_in, layer_acts, s1_send, s1_recv)
+    spread1b = Spread(l2, places, out_in, layer_acts, s1_send, s1_recv)
+    spread2 = Spread(l, places, dhb, grad_acts, s2_send, s2_recv)
+    spread2b = Spread(l2, places, dhb, grad_acts, s2_send, s2_recv)
+    load = Loader(wbuf, w_sem, [own[m] if j == n_t - 1 else full.at[m, slots[j]] for m, j in order])
 
     l.greet([{"tensor": l.up}, {"tensor": l.down}, other] + [{"dp": l.flip(b)} for b in l.bits])
     spread1.start()
@@ -772,8 +855,8 @@
     acts_out = local(dhb, layer_acts.at[l.z], l_sem.at[0])
     h2_copy = local(h2_in, h2, l_sem.at[1])
     x_copy = local(xs, x, l_sem.at[2])
-    o_copy = local(o_in, o, l_sem.at[3])
-    for c in (acts_in, h2_copy, x_copy, o_copy):
+    o_copies = [local(o_in.at[slots[j]], o.at[j], o_sem.at[j]) for j in range(n_t)]
+    for c in (acts_in, h2_copy, x_copy, *o_copies):
         c.start()
 
     def act_copy(j):
@@ -839,8 +922,10 @@
 
         @pl.when(first)
         def _():
+            r.pump()
             outer_product(block_of(r, 2 * j), gbuf, act.at[j % 2])
-            r.steps(2 * j)
+            r.pump()
+            r.push(2 * j)
 
         w = load.wait(2 * j + 1)
         if j == 0:
@@ -851,16 +936,18 @@
 
         @pl.when(first)
         def _():
+            r.pump()
             outer_product(block_of(r, 2 * j + 1), n, du.at[j % 2])
-            r.steps(2 * j + 1)
+            r.pump()
+            r.push(2 * j + 1)
+
+        if j >= 2:
+            @pl.when(end_first)
+            def _():
+                r.last_step(j - 2)
 
     for j in range(max(n_t - 2, 0), n_t):
         du_out(j).wait()
-
-    @pl.when(second)
-    def _():
-        for k in range(1, n_t - 1):
-            spread1b.step(k)
 
     qkv_copy(0).start()
 
@@ -869,30 +956,44 @@
         ga[at, :] = value.astype(BF16)
 
     norm_back_rows(gbuf, dn, h2, gains[1:2, :], gain1, write_middle)
-    o_copy.wait()
-
-    for j, s in enumerate(slots):
+    for c in o_copies:
+        c.wait()
+
+    for j in range(n_t):
         if j + 1 < n_t:
             qkv_copy(j + 1).start()
         w = load.wait(ff + j)
         load.start(ff + j + 2)
         do[...] = dot_nt(ga[...], w[3 * wide:, :]).astype(BF16)
         qkv_copy(j).wait()
-        attend_slot_back(qkv.at[j % 2], do, proj, dcat.at[s], mask)
+        @pl.when(first)
+        def _():
+            r.pump()
+
+        attend_slot_back(qkv.at[j % 2], do, proj, dcat.at[j], mask)
 
         def turn_back(at):
             v = proj[at, 0:2 * wide]
-            dcat[s, at, 0:2 * wide] = (v * cos[at, :] - partner(v) * sin[at, :]).astype(BF16)
+            dcat[j, at, 0:2 * wide] = (v * cos[at, :] - partner(v) * sin[at, :]).astype(BF16)
 
         row_loop(rows, 32, turn_back)
         if j == 0:
-            dn[...] = dot_nn(dcat[s], w[0:3 * wide, :])
+            dn[...] = dot_nn(dcat[j], w[0:3 * wide, :])
         else:
-            dn[...] = dn[...] + dot_nn(dcat[s], w[0:3 * wide, :])
+            dn[...] = dn[...] + dot_nn(dcat[j], w[0:3 * wide, :])
+        @pl.when(first)
+        def _():
+            r.pump()
+
+        if j != 1:
+            @pl.when(end_first)
+            def _():
+                r.last_step((2, None, 3, 4)[j])
+
         if j < 2:
-            @pl.when(first)
+            @pl.when(inner_first)
             def _():
-                r.last_step(j)
+                rm.last_step(j)
     x_copy.wait()
     acts_out.wait()
 
@@ -922,39 +1023,63 @@
                 du_in(j + 1).start()
             act_copy(j).wait()
             outer_product(block_of(r2, 2 * j), gbuf, act.at[j % 2])
-            r2.steps(2 * j)
+            r2.pump()
+            r2.push(2 * j)
             du_in(j).wait()
             outer_product(block_of(r2, 2 * j + 1), n, du.at[j % 2])
-            r2.steps(2 * j + 1)
-        r2.last_step(0)
-        r2.last_step(1)
+            r2.pump()
+            r2.push(2 * j + 1)
+        spread1b.step(1)
+        r2.flush()
 
     total = Total(l, gain0, gain_buf, t_send, t_recv)
     gain0[0:1, :] = jnp.sum(gain0[...], axis=0, keepdims=True)
     gain0[1:2, :] = jnp.sum(gain1[...], axis=0, keepdims=True)
     norm_rows(x, gains[0:1, :], n)
-    for j, s in enumerate(slots):
+    for j in range(n_t):
         b = block_of(r, ff + j)
         step = d // 2
 
         def turn(c, _):
             at = pl.ds(pl.multiple_of(c * step, 128), step)
-            b[at, 0:3 * wide] = dot_tn(n[:, at], dcat[s]).astype(BF16)
-            b[at, 3 * wide:] = dot_tn(ga[:, at], o[s]).astype(BF16)
+            b[at, 0:3 * wide] = dot_tn(n[:, at], dcat[j]).astype(BF16)
+            b[at, 3 * wide:] = dot_tn(ga[:, at], o[j]).astype(BF16)
             return 0
 
         lax.fori_loop(0, 2, turn, 0)
-        r.steps(ff + j)
-        total.step(j)
-    for i in range(3):
-        r.steps(ff + n_t + i)
-        total.step(n_t + i) if n_t + i < total.count else None
-    for t in range(n_t + 3, total.count):
+        r.pump()
+        r.push(ff + j)
+    r.flush()
+
+    @pl.when(inner_first)
+    def _():
+        for i in range(2, 5):
+            rm.last_step(i)
+
+    @pl.when(second)
+    def _():
+        for i in range(5):
+            r2.last_step(i)
+        for k in range(2, n_t - 1):
+            spread1b.step(k)
+
+    for i in range(5, len(order)):
+        r.last_step(i)
+        if i == 5 or i == 7:
+            @pl.when(inner)
+            def _():
+                spread2.step((i - 3) // 2)
+        if i >= 6 and i - 6 < total.count:
+            total.step(i - 6)
+    for t in range(len(order) - 6, total.count):
         total.step(t)
-    for i in range(2, len(order)):
-        r.last_step(i)
-        if i == 3 or i == 5:
-            spread2.step((i - 1) // 2)
+    l2.recording = False
+
+    @pl.when(~inner)
+    def _():
+        for k in range(1, n_t - 1):
+            spread2b.step(k)
+
     spread1.step(n_t - 1)
     spread2.step(n_t - 1)
     out_gains[...] = total.result()
@@ -997,8 +1122,8 @@
             buf(rows, d, t=F32), buf(rows, d), buf(rows, d, t=F32), buf(2, rows, 3 * wide), buf(n_t, rows, wide),
             buf(rows, wide), buf(n_t, rows, 3 * wide), buf(rows, d), buf(ROW, 2 * QB, t=F32), buf(3, *a_own.shape),
             buf(8, d, t=F32), buf(8, d, t=F32), buf(2 * steps, 8, d, t=F32),
-            dma((3,)), dma((5,)), dma((2,)), dma((2,)), dma((2,)), dma((2,)), dma(()), dma(()),
-            dma((n_t,)), dma((n_t,)), dma((n_t,)), dma((n_t,)), dma((steps,)), dma((steps,)),
+            dma((3,)), dma((5,)), dma((n_t,)), dma((2,)), dma((2,)), dma((2,)), dma((2,)), dma(()), dma(()),
+            dma((2, n_t)), dma((2, n_t)), dma((2, n_t)), dma((2, n_t)), dma((steps,)), dma((steps,)),
             *reduce_scratch(n_dp, n_t, count, piece, d),
         ],
         compiler_params=pltpu.CompilerParams(collective_id=1, has_side_effects=True, vmem_limit_bytes=62 * 2**20),

time: 829 us -> 713 us (0.86)
  Pallas kernels: 790 us -> 669 us
    pallas_call x1, Pallas kernels: 548 us -> 433 us  [run_backward(): pl.pallas_call(functools.partial(backward_kernel, n_dp, n_t), out_shape=[...]
where the time goes in v4:
time: 713 us; the launch traced here: 699 us
  Pallas kernels  669 us (94%)
  local copies, waits for them, and re-layouts  25.1 us (4%)
    pallas_call x1, Pallas kernels, run_backward(): pl.pallas_call(functools.partial(backward_kernel, n_dp, n_t), out_shape=[...  433 us
    pallas_call x1, Pallas kernels, run_forward(): pl.pallas_call(functools.partial(forward_kernel, n_dp, n_t), out_shape=[s...  236 us

profile of v4, /device:TPU:0, one launch (start us, length us, event | category | flops | bytes accessed | tf_op | source)
XLA Modules:
  0.0 698.6 jit_solution(14305995965898648917)
XLA Ops:
  0.7 0.7 copy.29
  1.4 0.1 dynamic_slice.16
  1.4 0.0 copy-start.2
  1.4 0.7 copy.28
  2.1 0.7 dynamic_slice.17
  2.8 0.4 fusion.2
  3.2 0.9 copy.17.seg_col
  4.1 0.1 tile.8
  4.2 1.5 copy.18.cos
  5.7 0.0 copy-done.2
  5.7 0.1 tile.20
  5.8 1.5 copy.19.sin
  7.3 0.0 copy-start
  7.3 0.0 copy-start.1
  7.3 3.5 constant_dynamic-slice_fusion
  10.8 0.0 copy-done
  10.8 0.0 copy-done.1
  10.8 2.0 pad_maximum_fusion
  12.8 236.0 %shard_map.144 = (bf16[3,4,1280,1280]{3,2,1,0:T(8,128)(2,1)}, bf16[512,1280]{1,0:T(8,128)(2,1)}, bf16[4,512,960]{2,1,0:T(8,128)(2,1)}, bf16[4,512,320]{2,1,0:T(8...) custom-call(bf16[1280,1280]{1,0:T(8,128)(2,1)} %bitcast.46, ...), custom_call_target="tpu_custom_call" | custom-call | tf_op jit(solution)/shard_map/pallas_call | solution.py:748
  248.9 432.6 %shard_map.145 = (bf16[4,512,1280]{2,1,0:T(8,128)(2,1)}, bf16[4,512,1280]{2,1,0:T(8,128)(2,1)}, f32[3,320,1280]{2,1,0:T(8,128)}, f32[8,1280]{1,0:T(8,128)}, bf16...) custom-call(bf16[1280,1280]{1,0:T(8,128)(2,1)} %bitcast.47, ...), custom_call_target="tpu_custom_call" | custom-call | tf_op jit(solution)/shard_map/pallas_call | solution.py:1112
  681.5 0.8 slice.31
  682.3 0.7 dynamic-slice_bitcast_fusion
  683.0 4.4 slice_bitcast_fusion
  687.4 0.3 slice_bitcast_fusion.2
  687.7 1.0 copy.23
  688.7 0.0 slice-start
  688.7 1.2 maximum_bitcast_fusion
  689.9 0.0 slice-start.1
  689.9 5.8 copy.32
  695.7 0.0 slice-done
  695.7 0.0 slice-done.1
  695.7 2.4 copy.33
  (3 shorter events, 0.0 us)
Async XLA Ops:
  1.4 4.3 copy-start.2
  7.3 3.5 copy-start
  7.3 3.5 copy-start.1
  688.7 7.0 slice-start
  689.9 5.8 slice-start.1

commit v5 on v4

--- a/solution.py
+++ b/solution.py
@@ -3,6 +3,7 @@
 
 import jax
 import jax.numpy as jnp
+import numpy as np
 from jax import lax
 from jax.experimental import pallas as pl
 from jax.experimental.pallas import tpu as pltpu
@@ -53,29 +54,37 @@
     return [max(i - 1, 0) * QB for i in range(ROW // QB)]
 
 
-def write_mask(mask, seg_col, seg_row, obs_row):
+def write_mask(mask, seg_col, seg_row, obs_col):
     for i, k0 in enumerate(windows()):
-        r = slice(i * QB, (i + 1) * QB)
-        shape = (QB, 2 * QB)
-        qi = lax.broadcasted_iota(jnp.int32, shape, 0) + i * QB
-        kj = lax.broadcasted_iota(jnp.int32, shape, 1) + k0
-        same = seg_col[r, :] == seg_row[:, k0:k0 + 2 * QB]
-        seen = (obs_row[:, k0:k0 + 2 * QB] == 1) | (kj == qi)
-        mask[r, :] = (same & (kj <= qi) & seen).astype(F32)
-
-
-def by_block(dot, left, right):
+        keys, queries = slice(k0, k0 + 2 * QB), slice(i * QB, (i + 1) * QB)
+        shape = (2 * QB, QB)
+        kj = lax.broadcasted_iota(jnp.int32, shape, 0) + k0
+        qi = lax.broadcasted_iota(jnp.int32, shape, 1) + i * QB
+        same = seg_col[keys, :] == seg_row[:, queries]
+        seen = (obs_col[keys, :] == 1) | (kj == qi)
+        mask[:, queries] = (same & (kj <= qi) & seen).astype(F32)
+
+
+def query_block(x, i):
+    return x[:, i * QB:(i + 1) * QB]
+
+
+def by_window(keys, queries):
     return jnp.concatenate(
-        [dot(left[i * QB:(i + 1) * QB], right[k0:k0 + 2 * QB]) for i, k0 in enumerate(windows())], axis=0
+        [dot_nt(keys[k0:k0 + 2 * QB], queries[i * QB:(i + 1) * QB]) for i, k0 in enumerate(windows())], axis=1
     )
 
 
-def by_window(left, right):
-    n = ROW // QB
-    blocks = [None] * n
+def to_queries(weights, keys):
+    return jnp.concatenate(
+        [dot_tn(query_block(weights, i), keys[k0:k0 + 2 * QB]) for i, k0 in enumerate(windows())], axis=0
+    )
+
+
+def to_keys(weights, queries):
+    blocks = [None] * (ROW // QB)
     for i, k0 in enumerate(windows()):
-        r = slice(i * QB, (i + 1) * QB)
-        term = dot_tn(left[r], right[r])
+        term = dot_nn(query_block(weights, i), queries[i * QB:(i + 1) * QB])
         for j in range(2):
             at, part = k0 // QB + j, term[j * QB:(j + 1) * QB]
             blocks[at] = part if blocks[at] is None else blocks[at] + part
@@ -83,9 +92,9 @@
 
 
 def probabilities(q, k, mask):
-    s = jnp.where(mask[...] > 0, by_block(dot_nt, q, k) * SCALE, -BIG)
-    e = jnp.exp(s - jnp.max(s, axis=1, keepdims=True))
-    return e * (1.0 / jnp.sum(e, axis=1, keepdims=True))
+    s = jnp.where(mask[...] > 0, by_window(k, q) * SCALE, -BIG)
+    e = jnp.exp(s - jnp.max(s, axis=0, keepdims=True))
+    return e * (1.0 / jnp.sum(e, axis=0, keepdims=True))
 
 
 def ring_bits(n):
@@ -159,33 +168,37 @@
 
 
 class Gather:
-    def __init__(self, links, own, full, z_send, z_recv, p_send, p_recv):
-        self.l, self.own, self.full = links, own, full
+    def __init__(self, links, own, full, parts, z_send, z_recv, p_send, p_recv):
+        self.l, self.own, self.full, self.parts = links, own, full, parts
         self.z_send, self.z_recv, self.p_send, self.p_recv = z_send, z_recv, p_send, p_recv
         self.rows = own[0].shape[0] // links.n_dp
-        self.split, self.units = gather_units(self.rows, links.n_t)
-        self.part = self.rows // self.split
+        self.units = [(m, k, h) for m, k in gather_order(links.n_t) for h in range(len(parts))]
         self.at = {u: i for i, u in enumerate(self.units)}
 
     def piece(self, m, slot, index, h):
-        first = pl.multiple_of(index * self.rows + h * self.part, 16)
+        off, size = self.parts[h]
+        first = pl.multiple_of(index * self.rows + off, 16)
         if slot == 0:
-            return self.own[m].at[pl.ds(first, self.part), :]
-        return self.full.at[m, slot, pl.ds(first, self.part), :]
+            return self.own[m].at[pl.ds(first, size), :]
+        return self.full.at[m, slot, pl.ds(first, size), :]
+
+    def like(self, h):
+        return self.full.at[0, 1, pl.ds(0, self.parts[h][1]), :]
 
     def send_z(self, m, k, h):
         l = self.l
         i = self.at[(m, k, h)]
         l.send(self.piece(m, k - 1, l.me, h), self.piece(m, k, l.me, h), self.z_send.at[i], self.z_recv.at[i], {"tensor": l.down},
-               again=lambda: (self.like(), self.z_send.at[i]))
-
-    def like(self):
-        return self.full.at[0, 1, pl.ds(0, self.part), :]
+               again=lambda: (self.like(h), self.z_send.at[i]))
+
+    def advance(self, taken):
+        for unit in due(self.units, self.issued, taken, 2 * len(self.parts)):
+            self.send_z(*unit)
+            self.issued += 1
 
     def start(self):
-        for m, k, h in self.units:
-            if k == 1 and m < 2:
-                self.send_z(m, k, h)
+        self.issued = 0
+        self.advance(0)
 
     def share(self, i, j):
         m, k, h = self.units[i]
@@ -194,16 +207,13 @@
             if j == 0 or bit < low_bit(j):
                 ref = self.piece(m, k, l.mix(j), h)
                 l.send(ref, ref, self.p_send.at[i, j ^ bit], self.p_recv.at[i, j ^ bit], {"dp": l.flip(bit)},
-                       again=lambda at=j ^ bit: (self.like(), self.p_send.at[i, at]))
+                       again=lambda at=j ^ bit: (self.like(h), self.p_send.at[i, at]))
 
     def take(self, i):
         m, k, h = self.units[i]
         l = self.l
         l.arrived(self.piece(m, k, l.me, h), self.z_recv.at[i], self.z_send.at[i], {"tensor": l.up})
-        if k + 1 < l.n_t:
-            self.send_z(m, k + 1, h)
-        if (m, k) == (0, 1):
-            self.send_z(2, 1, h)
+        self.advance(i + 1)
         self.share(i, 0)
 
     def relay(self, i):
@@ -213,21 +223,125 @@
             l.arrived(self.piece(m, k, l.mix(j), h), self.p_recv.at[i, j], self.p_send.at[i, j], {"dp": l.flip(low_bit(j))})
             self.share(i, j)
 
-    def walk(self, lag=2):
+    def walk(self, lent=None, lag=2):
         for i in range(len(self.units) + lag):
             if i < len(self.units):
+                m, k, h = self.units[i]
                 self.take(i)
+                if lent is not None and h == 0:
+                    lent.take_back(m, k)
+            done = None
             if i >= lag:
                 self.relay(i - lag)
-                yield self.units[i - lag]
-
-
-def gather_units(rows, n_t):
-    split = 2 if rows % 32 == 0 else 1
+                m, k, h = self.units[i - lag]
+                if h == len(self.parts) - 1:
+                    if lent is not None:
+                        lent.finish_back(m, k)
+                    done = (m, k)
+            yield done
+
+
+class Lend:
+    def __init__(self, links, own, full, held, y_send, y_recv, z_send, z_recv, p_send, p_recv, b_send, b_recv):
+        self.l, self.own, self.full, self.held = links, own, full, held
+        self.y_send, self.y_recv, self.z_send, self.z_recv = y_send, y_recv, z_send, z_recv
+        self.p_send, self.p_recv, self.b_send, self.b_recv = p_send, p_recv, b_send, b_recv
+        self.rows = own[0].shape[0] // links.n_dp
+        self.size = held.shape[3]
+        self.even = [j for j in range(0, links.n_dp, 2)]
+        self.where = {"section": 1 - lax.axis_index("section")}
+
+    def rows_of(self, j):
+        return pl.ds(pl.multiple_of(self.l.mix(j) * self.rows, 16), self.size)
+
+    def like(self):
+        return self.held.at[0, 0, 0]
+
+    def send(self, src, dst, sems, at, where):
+        self.l.send(src, dst, sems[0].at[at], sems[1].at[at], where, again=lambda: (self.like(), sems[0].at[at]))
+
+    def arrived(self, ref, sems, at):
+        self.l.arrived(ref, sems[1].at[at], sems[0].at[at], self.where)
+
+    def give(self):
+        for m in range(3):
+            self.send(self.own[m].at[self.rows_of(0), :], self.held.at[m, 0, self.l.me], (self.y_send, self.y_recv), (m,), self.where)
+
+    def take_back(self, m, k):
+        for j in self.even:
+            ref = self.full.at[m, k, self.rows_of(j), :]
+            self.arrived(ref, (self.b_send, self.b_recv), (m, k, j))
+            self.send(ref, ref, (self.p_send, self.p_recv), (m, k, j + 1), {"dp": self.l.flip(1)})
+
+    def finish_back(self, m, k):
+        for j in self.even:
+            self.arrived(self.full.at[m, k, self.rows_of(j + 1), :], (self.p_send, self.p_recv), (m, k, j + 1))
+
+    def ring(self, m, k):
+        l = self.l
+        self.send(self.held.at[m, k - 1, l.me], self.held.at[m, k, l.me], (self.z_send, self.z_recv), (m, k), {"tensor": l.down})
+
+    def back(self, m, k, j):
+        l = self.l
+        self.send(self.held.at[m, k, l.mix(j)], self.full.at[m, k, self.rows_of(j), :], (self.b_send, self.b_recv), (m, k, j), self.where)
+
+    def share(self, m, k, j):
+        l = self.l
+        for bit in reversed(l.bits[1:]):
+            if j == 0 or bit < low_bit(j):
+                ref = self.held.at[m, k, l.mix(j)]
+                self.send(ref, ref, (self.p_send, self.p_recv), (m, k, j ^ bit), {"dp": l.flip(bit)})
+
+    def serve(self, lag=1):
+        l = self.l
+        units = gather_order(l.n_t)
+        issued = 0
+        started = False
+        for i in range(len(units) + lag):
+            for m, k in due(units, issued, i, 3):
+                if k == 1:
+                    self.arrived(self.held.at[m, 0, l.me], (self.y_send, self.y_recv), (m,))
+                self.ring(m, k)
+                issued += 1
+            if issued == len(units) and not started:
+                started = True
+                yield
+            if i < len(units):
+                m, k = units[i]
+                self.arrived(self.held.at[m, k, l.me], (self.z_send, self.z_recv), (m, k))
+                self.share(m, k, 0)
+                self.back(m, k, 0)
+            if i >= lag:
+                m, k = units[i - lag]
+                for j in sorted(self.even[1:], key=lambda j: (-low_bit(j), j)):
+                    self.arrived(self.held.at[m, k, l.mix(j)], (self.p_send, self.p_recv), (m, k, j))
+                    self.share(m, k, j)
+                    self.back(m, k, j)
+
+
+def gather_order(n_t):
     heads = [(0, k) for k in range(1, n_t)]
     rest = [(m, k) for k in range(1, n_t) for m in (1, 2)]
-    mixed = [u for pair in zip(heads, rest) for u in pair] + rest[len(heads):]
-    return split, [(m, k, h) for m, k in mixed for h in range(split)]
+    return [u for pair in zip(heads, rest) for u in pair] + rest[len(heads):]
+
+
+def due(units, issued, taken, ahead):
+    found = []
+    while issued < min(len(units), taken + ahead):
+        m, k, *h = units[issued]
+        if k > 1 and units.index((m, k - 1, *h)) >= taken:
+            break
+        found.append(units[issued])
+        issued += 1
+    return found
+
+
+def gather_parts(rows):
+    lent = rows // 4 // 16 * 16
+    if rows % 32:
+        return lent, [(lent, rows - lent)], [(0, rows)]
+    cut = lent + (rows - lent + 31) // 32 * 16
+    return lent, [(lent, cut - lent), (cut, rows - cut)], [(0, rows // 2), (rows // 2, rows // 2)]
 
 
 def level_start(n_dp, level):
@@ -544,12 +658,17 @@
     row_loop(source.shape[0], 32, body)
 
 
+def own_block(ref, z, rows):
+    per = ref.shape[1] // rows
+    return ref.at[z // per, pl.ds(pl.multiple_of(lax.rem(z, per) * rows, rows), rows), :]
+
+
 def attend_slot(qkv, o, mask):
     heads = o.shape[1] // HEAD_SIZE
     for h in range(heads):
         q, k, v = (slice((t * heads + h) * HEAD_SIZE, (t * heads + h + 1) * HEAD_SIZE) for t in range(3))
         p = probabilities(qkv[:, q], qkv[:, k], mask).astype(BF16)
-        o[:, q] = by_block(dot_nn, p, qkv[:, v]).astype(BF16)
+        o[:, q] = to_queries(p, qkv[:, v]).astype(BF16)
 
 
 class Loader:
@@ -570,19 +689,22 @@
 
 
 def forward_kernel(
-    n_dp, n_t, a_own, i_own, d_own, x0, gains, seg_col, seg_row, obs_row, cos, sin,
-    full, xs, qkv_out, o_out, h2_out, act_out, slope_out, out,
-    x, n, proj, qkv, o, h2, acc, act, slope, outb, mask, wbuf,
-    w_sem, s_sem, y_send, y_recv, x_sem, z_send, z_recv, p_send, p_recv,
+    n_dp, n_t, a_own, i_own, d_own, x0, gains, seg_col, seg_row, obs_col, cos_in, sin_in,
+    full, xs, qkv_out, o_out, h2_out, act_out, slope_out, out, held,
+    x, n, proj, qkv, o, h2, acc, act, slope, outb, mask, wbuf, cos, sin,
+    c_sem, w_sem, s_sem, y_send, y_recv, x_sem, z_send, z_recv, p_send, p_recv,
+    *lend_sems,
 ):
-    l = Links(n_dp, n_t)
+    l, l1 = Links(n_dp, n_t), Links(n_dp, n_t)
     section = lax.axis_index("section")
     first, second = section == 0, section != 0
     own = (a_own, i_own, d_own)
-    g = Gather(l, own, full, z_send, z_recv, p_send, p_recv)
+    _, parts0, parts1 = gather_parts(a_own.shape[0] // n_dp)
+    g0 = Gather(l, own, full, parts0, z_send, z_recv, p_send, p_recv)
+    g1 = Gather(l1, own, full, parts1, z_send, z_recv, p_send, p_recv)
+    lend0, lend1 = Lend(l, own, full, held, *lend_sems), Lend(l1, own, full, held, *lend_sems)
     other = {"section": 1 - section}
     l.greet([{"tensor": l.up}, other] + [{"dp": l.flip(b)} for b in l.bits])
-    g.start()
     rows, d = x.shape
     wide = o.shape[2]
 
@@ -598,43 +720,55 @@
         copy.start()
         stores.append(copy)
 
+    walks, here = (g0.walk(lend0), g1.walk()), (set(), set())
+
+    def until(section, m, slot):
+        while slot > 0 and (m, slot) not in here[section]:
+            here[section].add(next(walks[section]))
+
+    def tick(*sections):
+        for at in sections:
+            @pl.when((first, second)[at])
+            def _():
+                here[at].add(next(walks[at], None))
+
+    tables = [pltpu.make_async_copy(t, to, c_sem.at[i]) for i, (t, to) in enumerate(((cos_in, cos), (sin_in, sin)))]
+    for c in tables:
+        c.start()
+
     @pl.when(first)
     def _():
+        lend0.give()
+        g0.start()
         copy = pltpu.make_async_copy(x0, x, x_sem)
         copy.start()
         copy.wait()
 
-    write_mask(mask, seg_col, seg_row, obs_row)
-    l.recording = False
+    write_mask(mask, seg_col, seg_row, obs_col)
+    for c in tables:
+        c.wait()
 
     @pl.when(second)
     def _():
-        for _ in g.walk():
+        lending = lend1.serve()
+        next(lending)
+        g1.start()
+        for _ in lending:
             pass
+        until(1, 0, n_t - 1)
         load.start(0)
         load.start(1)
+        until(1, 2, n_t - 2)
         pltpu.make_async_remote_copy(
             src_ref=outb, dst_ref=x, send_sem=y_send, recv_sem=y_recv, device_id=other, device_id_type=MESH
         ).wait_recv()
-
-    l.recording = True
-    walk, here = g.walk(), set()
-
-    def until(m, slot):
-        while slot > 0 and (m, slot, g.split - 1) not in here:
-            here.add(next(walk))
-
-    def tick():
-        @pl.when(first)
-        def _():
-            here.add(next(walk, None))
 
     store(x, xs, s_sem.at[0])
     norm_rows(x, gains[0:1, :], n)
     for s in range(n_t):
         @pl.when(first)
         def _():
-            until(0, s)
+            until(0, 0, s)
             load.start(s)
 
         @pl.when(second)
@@ -650,9 +784,9 @@
             qkv[s, at, 2 * wide:3 * wide] = proj[at, 2 * wide:3 * wide].astype(BF16)
 
         row_loop(rows, 32, turn_rows)
-        tick()
+        tick(0)
         attend_slot(qkv.at[s], o.at[s], mask)
-        tick()
+        tick(0, 1)
         term = dot_nn(o[s], w[3 * wide:, :])
         if s == 0:
             acc[...] = term
@@ -676,13 +810,19 @@
 
         @pl.when(first)
         def _():
-            until(2, s)
+            until(0, 2, s)
             load.start(j)
             load.start(j + 1)
 
         @pl.when(second)
         def _():
-            load.start(j + 2)
+            if s == n_t - 1:
+                until(1, 2, s)
+                load.start(j)
+                load.start(j + 1)
+            elif s < n_t - 2:
+                until(1, 1, s + 1)
+                load.start(j + 2)
 
         w = load.wait(j)
         proj[...] = dot_nn(n[...], w[...])
@@ -698,12 +838,13 @@
             slope[s % 2, at, :] = (sig * (1.0 + u * (1.0 - sig))).astype(BF16)
 
         row_loop(rows, 32, silu)
-        if s > 0:
-            tick()
+        tick(*((1,) if s == 0 else (0, 1)))
 
         @pl.when(second)
         def _():
-            load.start(j + 3)
+            if s < n_t - 2:
+                until(1, 2, s + 1)
+                load.start(j + 3)
 
         w = load.wait(j + 1)
         acc[...] = acc[...] + dot_nn(act[s % 2], w[...])
@@ -714,7 +855,7 @@
         outb[at, :] = acc[at, :].astype(BF16)
 
     row_loop(rows, 32, finish)
-    assert len(here - {None}) == len(g.units)
+    assert all(len(h - {None}) == 3 * (n_t - 1) for h in here)
     over = pltpu.make_async_remote_copy(
         src_ref=outb, dst_ref=x, send_sem=y_send, recv_sem=y_recv, device_id=other, device_id_type=MESH
     )
@@ -730,15 +871,19 @@
     @pl.when(first)
     def _():
         over.wait_send()
-
-    l.drain()
+        l.drain()
+
+    @pl.when(second)
+    def _():
+        l1.drain()
 
 
 def run_forward(a_own, i_own, d_own, x0, gains, seg, obs, tables):
     n_dp, n_t = lax.axis_size("dp"), lax.axis_size("tensor")
     rows, d = x0.shape
     wide = a_own.shape[0] // 4
-    count = len(gather_units(a_own.shape[0] // n_dp, n_t)[1])
+    lent, parts, _ = gather_parts(a_own.shape[0] // n_dp)
+    count = 3 * (n_t - 1) * len(parts)
     dma = pltpu.SemaphoreType.DMA
     hbm, vmem = pl.BlockSpec(memory_space=pl.ANY), pl.BlockSpec(memory_space=pltpu.VMEM)
 
@@ -750,9 +895,10 @@
         out_shape=[
             shape(3, n_t, *a_own.shape), shape(rows, d), shape(n_t, rows, 3 * wide), shape(n_t, rows, wide),
             shape(rows, d, t=F32), shape(n_t, rows, i_own.shape[1]), shape(n_t, rows, i_own.shape[1]), shape(rows, d),
+            shape(3, n_t, n_dp, lent, d),
         ],
-        in_specs=[hbm] * 4 + [vmem] * 6,
-        out_specs=[hbm] * 8,
+        in_specs=[hbm] * 4 + [vmem] * 4 + [hbm] * 2,
+        out_specs=[hbm] * 9,
         scratch_shapes=[
             pltpu.VMEM((rows, d), BF16),
             pltpu.VMEM((rows, d), BF16),
@@ -764,13 +910,18 @@
             pltpu.VMEM((2, rows, d), BF16),
             pltpu.VMEM((2, rows, d), BF16),
             pltpu.VMEM((rows, d), BF16),
-            pltpu.VMEM((ROW, 2 * QB), F32),
+            pltpu.VMEM((2 * QB, ROW), F32),
             pltpu.VMEM((3,) + a_own.shape, BF16),
+            pltpu.VMEM(tables[0].shape, F32),
+            pltpu.VMEM(tables[1].shape, F32),
+            dma((2,)),
             dma((3,)), dma((6 + 2 * n_t,)), dma(()), dma(()), dma(()),
             dma((count,)), dma((count,)), dma((count, n_dp)), dma((count, n_dp)),
+            dma((3,)), dma((3,)), dma((3, n_t)), dma((3, n_t)),
+            dma((3, n_t, n_dp)), dma((3, n_t, n_dp)), dma((3, n_t, n_dp)), dma((3, n_t, n_dp)),
         ],
         compiler_params=pltpu.CompilerParams(collective_id=0, has_side_effects=True, vmem_limit_bytes=60 * 2**20),
-    )(a_own, i_own, d_own, x0, gains, seg[:, None], seg[None, :], obs[None, :], *tables)
+    )(a_own, i_own, d_own, x0, gains, seg[:, None], seg[None, :], obs[:, None], *tables)
 
 
 def attend_slot_back(qkv, do, dqk, dcat, mask):
@@ -780,11 +931,11 @@
         q, k, v = (slice((t * heads + h) * HEAD_SIZE, (t * heads + h + 1) * HEAD_SIZE) for t in range(3))
         qh, kh, vh, dh = qkv[:, q], qkv[:, k], qkv[:, v], do[:, q]
         p = probabilities(qh, kh, mask)
-        dcat[:, v] = by_window(p.astype(BF16), dh).astype(BF16)
-        dp = by_block(dot_nt, dh, vh)
-        ds = (p * (dp - jnp.sum(p * dp, axis=1, keepdims=True))).astype(BF16)
-        dqk[:, q] = by_block(dot_nn, ds, kh) * SCALE
-        dqk[:, k] = by_window(ds, qh) * SCALE
+        dcat[:, v] = to_keys(p.astype(BF16), dh).astype(BF16)
+        dp = by_window(vh, dh)
+        ds = (p * (dp - jnp.sum(p * dp, axis=0, keepdims=True))).astype(BF16)
+        dqk[:, q] = to_queries(ds, kh) * SCALE
+        dqk[:, k] = to_keys(ds, qh) * SCALE
 
 
 def outer_product(out, left, right):
@@ -798,7 +949,7 @@
     lax.fori_loop(0, 2, turn, 0)
 
 
-def norm_back_rows(g, dn, h, gain, gain_sum, write):
+def norm_back_rows(g, dn, h, gain, gain_sum, normed, write):
     gain_sum[...] = jnp.zeros_like(gain_sum)
     step = 32
 
@@ -806,6 +957,8 @@
         hr, dr = h[at, :].astype(F32), dn[at, :]
         r = lax.rsqrt(jnp.mean(hr * hr, axis=1, keepdims=True) + EPS)
         y = gain * dr
+        if normed is not None:
+            normed[at, :] = (hr * r * gain).astype(BF16)
         gain_sum[...] += jnp.sum((dr * hr * r).reshape(step // 8, 8, -1), axis=0)
         write(at, g[at, :].astype(F32) + r * y - hr * (r * r * r) * jnp.mean(hr * y, axis=1, keepdims=True))
 
@@ -814,10 +967,10 @@
 
 def backward_kernel(
     n_dp, n_t, a_own, i_own, d_own, full, cot, xs, qkv_in, o_in, h2_in, act_in, slope_in, out_in, gains,
-    seg_col, seg_row, obs_row, cos, sin,
+    seg_col, seg_row, obs_col, cos_in, sin_in,
     layer_acts, grad_acts, out_sums, out_gains, hbm_sums, hbm_got, hbm_ring, du_hbm,
-    gbuf, act, du, n, h2, x, dn, ga, proj, qkv, o, do, dcat, dhb, mask, wbuf, gain0, gain1, gain_buf,
-    w_sem, l_sem, o_sem, a_sem, u_sem, q_sem, st_sem, y_send, y_recv, s1_send, s1_recv, s2_send, s2_recv, t_send, t_recv,
+    gbuf, act, du, n, h2, x, dn, ga, proj, qkv, o, do, dcat, dhb, mask, wbuf, cos, sin, gain0, gain1, gain_buf,
+    c_sem, w_sem, l_sem, o_sem, a_sem, u_sem, q_sem, st_sem, y_send, y_recv, s1_send, s1_recv, s2_send, s2_recv, t_send, t_recv,
     *reduce_refs,
 ):
     section = lax.axis_index("section")
@@ -876,9 +1029,16 @@
 
     act_copy(0).start()
     slope_copy(0).start()
-    write_mask(mask, seg_col, seg_row, obs_row)
+    tables = [local(t, to, c_sem.at[i]) for i, (t, to) in enumerate(((cos_in, cos), (sin_in, sin)))]
+    for c in tables:
+        c.start()
+    write_mask(mask, seg_col, seg_row, obs_col)
     h2_copy.wait()
-    norm_rows(h2, gains[1:2, :], n)
+
+    @pl.when(first)
+    def _():
+        norm_rows(h2, gains[1:2, :], n)
+
     acts_in.wait()
     acts_out.start()
     arrival = pltpu.make_async_remote_copy(
@@ -955,8 +1115,8 @@
         h2[at, :] = value
         ga[at, :] = value.astype(BF16)
 
-    norm_back_rows(gbuf, dn, h2, gains[1:2, :], gain1, write_middle)
-    for c in o_copies:
+    norm_back_rows(gbuf, dn, h2, gains[1:2, :], gain1, n, write_middle)
+    for c in (*o_copies, *tables):
         c.wait()
 
     for j in range(n_t):
@@ -1000,7 +1160,7 @@
     def write_input(at, value):
         dhb[at, :] = value.astype(BF16)
 
-    norm_back_rows(h2, dn, x, gains[0:1, :], gain0, write_input)
+    norm_back_rows(h2, dn, x, gains[0:1, :], gain0, None, write_input)
     over = pltpu.make_async_remote_copy(
         src_ref=dhb, dst_ref=gbuf, send_sem=y_send, recv_sem=y_recv, device_id=other, device_id_type=MESH
     )
@@ -1115,19 +1275,20 @@
             shape(n_t, rows, d), shape(n_t, rows, d), shape(3, piece, d, t=F32), shape(8, d, t=F32),
             *reduce_hbm(n_dp, n_t, count, piece, d), shape(n_t, rows, d),
         ],
-        in_specs=[hbm] * 12 + [vmem] * 6,
+        in_specs=[hbm] * 12 + [vmem] * 4 + [hbm] * 2,
         out_specs=[hbm] * 3 + [vmem] + [hbm] * 4,
         scratch_shapes=[
             buf(rows, d), buf(2, rows, d), buf(2, rows, d), buf(rows, d), buf(rows, d, t=F32), buf(rows, d),
             buf(rows, d, t=F32), buf(rows, d), buf(rows, d, t=F32), buf(2, rows, 3 * wide), buf(n_t, rows, wide),
-            buf(rows, wide), buf(n_t, rows, 3 * wide), buf(rows, d), buf(ROW, 2 * QB, t=F32), buf(3, *a_own.shape),
+            buf(rows, wide), buf(n_t, rows, 3 * wide), buf(rows, d), buf(2 * QB, ROW, t=F32), buf(3, *a_own.shape),
+            buf(*tables[0].shape, t=F32), buf(*tables[1].shape, t=F32),
             buf(8, d, t=F32), buf(8, d, t=F32), buf(2 * steps, 8, d, t=F32),
-            dma((3,)), dma((5,)), dma((n_t,)), dma((2,)), dma((2,)), dma((2,)), dma((2,)), dma(()), dma(()),
+            dma((2,)), dma((3,)), dma((5,)), dma((n_t,)), dma((2,)), dma((2,)), dma((2,)), dma((2,)), dma(()), dma(()),
             dma((2, n_t)), dma((2, n_t)), dma((2, n_t)), dma((2, n_t)), dma((steps,)), dma((steps,)),
             *reduce_scratch(n_dp, n_t, count, piece, d),
         ],
         compiler_params=pltpu.CompilerParams(collective_id=1, has_side_effects=True, vmem_limit_bytes=62 * 2**20),
-    )(a_own, i_own, d_own, kept[0], cot, *kept[1:], gains, seg[:, None], seg[None, :], obs[None, :], *tables)
+    )(a_own, i_own, d_own, kept[0], cot, *kept[1:], gains, seg[:, None], seg[None, :], obs[:, None], *tables)
 
 
 def own_rows(x, count):
@@ -1143,11 +1304,9 @@
     count = micro * rows // n_t
     tables = rope_tables()
     stack = jnp.concatenate([jnp.swapaxes(w_qkv, 1, 2), w_out[None]], axis=0).reshape(4 * hd, d)
-    x0 = own_rows(tokens, count)
-    g1 = own_rows(cotangent, count)
     seg, obs = own_rows(seg_ids, count), own_rows(observed, count)
-    kept = run_forward(stack, w_in, w_down, x0, gains, seg, obs, tables)
-    layer_acts, grad_acts, sums, gain = run_backward(stack, w_in, w_down, kept, g1, gains, seg, obs, tables)[:4]
+    kept = run_forward(stack, w_in, w_down, own_rows(tokens, count), gains, seg, obs, tables)[:8]
+    layer_acts, grad_acts, sums, gain = run_backward(stack, w_in, w_down, kept, own_rows(cotangent, count), gains, seg, obs, tables)[:4]
     piece = d // n_dp
     gain = lax.dynamic_slice_in_dim(gain[:2], lax.axis_index("dp") * piece, piece, 1)
     r_attn, r_in, r_down = sums[0], sums[1], sums[2]

time: 713 us -> 680 us (0.954)
  Pallas kernels: 669 us -> 642 us
    pallas_call x1, Pallas kernels: 236 us -> 201 us  [run_forward(): pl.pallas_call(functools.partial(forward_kernel, n_dp, n_t), out_shape=[s...]
    pallas_call x1, Pallas kernels: 433 us -> 441 us  [run_backward(): pl.pallas_call(functools.partial(backward_kernel, n_dp, n_t), out_shape=[...]
where the time goes in v5:
time: 680 us; the launch traced here: 672 us
  Pallas kernels  642 us (94%)
  local copies, waits for them, and re-layouts  25.3 us (4%)
    pallas_call x1, Pallas kernels, run_backward(): pl.pallas_call(functools.partial(backward_kernel, n_dp, n_t), out_shape=[...  441 us
    pallas_call x1, Pallas kernels, run_forward(): pl.pallas_call(functools.partial(forward_kernel, n_dp, n_t), out_shape=[s...  201 us

profile of v5, /device:TPU:0, one launch (start us, length us, event | category | flops | bytes accessed | tf_op | source)
XLA Modules:
  0.0 671.9 jit_solution(3901957953753612484)
XLA Ops:
  0.7 0.7 copy.31
  1.4 0.1 dynamic_slice.16
  1.4 0.0 copy-start.2
  1.4 0.7 copy.30
  2.1 0.1 dynamic_slice.17
  2.2 0.4 fusion.2
  2.6 0.9 copy.18.obs_col
  3.5 0.9 copy.17.seg_col
  4.3 0.1 tile.8
  4.5 1.5 copy.19.cos_in
  6.0 0.0 copy-done.2
  6.0 0.1 tile.20
  6.1 1.5 copy.20.sin_in
  7.6 0.0 copy-start
  7.6 0.0 copy-start.1
  7.6 3.5 constant_dynamic-slice_fusion
  11.1 0.0 copy-done
  11.1 0.0 copy-done.1
  11.1 2.0 pad_maximum_fusion
  13.1 200.8 %shard_map.144 = (bf16[3,4,1280,1280]{3,2,1,0:T(8,128)(2,1)}, bf16[512,1280]{1,0:T(8,128)(2,1)}, bf16[4,512,960]{2,1,0:T(8,128)(2,1)}, bf16[4,512,320]{2,1,0:T(8...) custom-call(bf16[1280,1280]{1,0:T(8,128)(2,1)} %bitcast.46, ...), custom_call_target="tpu_custom_call" | custom-call | tf_op jit(solution)/shard_map/pallas_call | solution.py:893
  213.9 441.2 %shard_map.145 = (bf16[4,512,1280]{2,1,0:T(8,128)(2,1)}, bf16[4,512,1280]{2,1,0:T(8,128)(2,1)}, f32[3,320,1280]{2,1,0:T(8,128)}, f32[8,1280]{1,0:T(8,128)}, bf16...) custom-call(bf16[1280,1280]{1,0:T(8,128)(2,1)} %bitcast.47, ...), custom_call_target="tpu_custom_call" | custom-call | tf_op jit(solution)/shard_map/pallas_call | solution.py:1272
  655.1 0.8 slice.31
  655.9 0.7 dynamic-slice_bitcast_fusion
  656.5 4.4 slice_bitcast_fusion
  661.0 0.3 slice_bitcast_fusion.2
  661.3 1.0 copy.25
  662.3 0.0 slice-start
  662.3 1.2 maximum_bitcast_fusion
  663.5 5.8 copy.34
  669.3 0.0 slice-done
  669.3 0.0 slice-done.1
  669.3 2.4 copy.35
  (4 shorter events, 0.0 us)
Async XLA Ops:
  1.4 4.5 copy-start.2
  7.6 3.5 copy-start
  7.6 3.5 copy-start.1
  662.3 7.0 %slice-start = ((s8[5242880]{0:T(1024)(128)(4,1)}), s8[4194304]{0:T(1024)(128)(4,1)S(1)}, s32[]{:S(2)}) async-start(s8[5242880]{0:T(1024)(128)(4,1)} %bitcast.52), calls=%async_computation | async-start | bytes 8388608
  663.5 5.8 slice-start.1

commit v6 on v5

--- a/solution.py
+++ b/solution.py
@@ -216,28 +216,31 @@
         self.advance(i + 1)
         self.share(i, 0)
 
-    def relay(self, i):
+    def relay(self, i, bit):
         m, k, h = self.units[i]
         l = self.l
-        for j in sorted(range(1, l.n_dp), key=lambda j: (-low_bit(j), j)):
+        for j in range(bit, l.n_dp, 2 * bit):
             l.arrived(self.piece(m, k, l.mix(j), h), self.p_recv.at[i, j], self.p_send.at[i, j], {"dp": l.flip(low_bit(j))})
             self.share(i, j)
 
     def walk(self, lent=None, lag=2):
-        for i in range(len(self.units) + lag):
+        hops = self.l.bits[::-1]
+        for i in range(len(self.units) + lag + len(hops) - 1):
             if i < len(self.units):
                 m, k, h = self.units[i]
                 self.take(i)
                 if lent is not None and h == 0:
                     lent.take_back(m, k)
             done = None
-            if i >= lag:
-                self.relay(i - lag)
-                m, k, h = self.units[i - lag]
-                if h == len(self.parts) - 1:
-                    if lent is not None:
-                        lent.finish_back(m, k)
-                    done = (m, k)
+            for hop, bit in enumerate(hops):
+                at = i - lag - hop
+                if 0 <= at < len(self.units):
+                    self.relay(at, bit)
+                    m, k, h = self.units[at]
+                    if hop == len(hops) - 1 and h == len(self.parts) - 1:
+                        if lent is not None:
+                            lent.finish_back(m, k)
+                        done = (m, k)
             yield done
 
 
@@ -405,6 +408,12 @@
         self.above = (2 * n_t - 2 - links.z) // n_t
 
 
+def travel_order(order):
+    if len(order) != 12:
+        return list(range(len(order)))
+    return [0, 1, 2, 3, 4, 8, 5, 9, 6, 10, 7, 11]
+
+
 class Reduce:
     def __init__(self, links, places, order, out, hbm, scratch):
         self.l, self.places, self.order, self.out = links, places, order, out
@@ -413,6 +422,8 @@
          self.c_send, self.c_recv, self.z_send, self.z_recv,
          self.f_sem, self.s_sem, self.t_sem, self.o_sem) = scratch
         self.moves = []
+        self.queue = travel_order(order)
+        self.stored, self.gone = set(), 0
         self.levels = len(links.bits)
         self.rows = self.fetched.shape[2]
         self.storing = None
@@ -463,7 +474,11 @@
 
     def give_next(self, i):
         self.store_copy(i).wait()
-        self.give(i, 1, lambda piece: self.sums.at[i, piece // 2])
+        self.stored.add(i)
+        while self.gone < len(self.queue) and self.queue[self.gone] in self.stored:
+            at = self.queue[self.gone]
+            self.give(at, 1, lambda piece: self.sums.at[at, piece // 2])
+            self.gone += 1
 
     def push(self, i):
         self.give_block(i)
@@ -472,20 +487,19 @@
     def pump(self):
         for move in list(self.moves):
             i, stage = move
-            if stage == 1 and any(o[0] == i - 2 for o in self.moves):
+            if stage == 0 and any(o[0] == i - 2 for o in self.moves):
                 break
-            if stage > 0:
-                (self.fetch, self.add_first, self.give_next)[stage - 1](i)
+            (self.fetch, self.add_first, self.give_next)[stage](i)
             move[1] += 1
-            if move[1] == 4:
+            if move[1] == 3:
                 self.moves.remove(move)
 
     def flush(self, i=None):
-        while any(i is None or o[0] <= i for o in self.moves):
+        while any(i is None or o[0] == i for o in self.moves):
             self.pump()
 
     def clear(self, i):
-        while any(o[0] == i - 3 and o[1] < 3 for o in self.moves):
+        while any(o[0] == i - 3 and o[1] < 2 for o in self.moves):
             self.pump()
         self.l.finish((i - 3, 0))
 
@@ -531,13 +545,13 @@
         copy.start()
         copy.wait()
 
-    def pass_on(self, i):
+    def pass_on(self, i, turn):
         l, p = self.l, self.places
         m, j = self.order[i]
-        l.finish(("z", i - 3))
+        l.finish(("z", turn - 3))
         terms = [self.terms.at[t] for t in range(3)]
         if j < l.n_t - 1:
-            s, up, out = p.shard[j], p.up[j], self.moving.at[i % 3]
+            s, up, out = p.shard[j], p.up[j], self.moving.at[turn % 3]
             behind = up * p.below + (1 - up) * p.above
             for c in self.term_copies(i):
                 c.wait()
@@ -552,7 +566,7 @@
                 add_rows(out, *terms[:2])
 
             l.send(out, self.ring.at[m, s, 1 - up], self.z_send.at[i], self.z_recv.at[m, s, 1 - up], {"tensor": l.z + 2 * up - 1},
-                   ("z", i), again=lambda: (self.moving.at[i % 3], self.z_send.at[i]))
+                   ("z", turn), again=lambda: (self.moving.at[turn % 3], self.z_send.at[i]))
         else:
             if self.storing is not None:
                 self.out_copy(self.storing).wait()
@@ -567,12 +581,14 @@
             self.out_copy(m).start()
             self.storing = m
 
-    def last_step(self, i):
-        self.flush(i)
+    def last_step(self, turn):
+        i = self.queue[turn]
+        for before in self.queue[:turn + 1]:
+            self.flush(before)
         for level in range(1, self.levels - 1):
             self.middle(i, level)
         self.collect(i)
-        self.pass_on(i)
+        self.pass_on(i, turn)
 
     def close(self):
         self.out_copy(self.storing).wait()
@@ -649,6 +665,10 @@
     lax.fori_loop(0, rows // step, turn, 0)
 
 
+def column_steps(width):
+    return [slice(c, c + 256) for c in range(0, width, 256)]
+
+
 def norm_rows(source, gain, out):
     def body(at):
         h = source[at, :].astype(F32)
@@ -686,6 +706,18 @@
     def wait(self, j):
         self.copy(j).wait()
         return self.buf.at[j % self.buf.shape[0]]
+
+
+PARTS = 2
+
+
+def over_part(src, dst, send, recv, where, c):
+    size = src.shape[0] // PARTS
+    at = pl.ds(c * size, size)
+    return pltpu.make_async_remote_copy(
+        src_ref=src.at[at, :], dst_ref=dst.at[at, :], send_sem=send.at[c], recv_sem=recv.at[c],
+        device_id=where, device_id_type=MESH,
+    )
 
 
 def forward_kernel(
@@ -758,10 +790,9 @@
         until(1, 0, n_t - 1)
         load.start(0)
         load.start(1)
-        until(1, 2, n_t - 2)
-        pltpu.make_async_remote_copy(
-            src_ref=outb, dst_ref=x, send_sem=y_send, recv_sem=y_recv, device_id=other, device_id_type=MESH
-        ).wait_recv()
+        until(1, 1, n_t - 2)
+        for c in range(PARTS):
+            over_part(outb, x, y_send, y_recv, other, c).wait_recv()
 
     store(x, xs, s_sem.at[0])
     norm_rows(x, gains[0:1, :], n)
@@ -810,9 +841,10 @@
 
         @pl.when(first)
         def _():
-            until(0, 2, s)
+            until(0, 1 if s == n_t - 1 else 2, s)
             load.start(j)
-            load.start(j + 1)
+            if s < n_t - 1:
+                load.start(j + 1)
 
         @pl.when(second)
         def _():
@@ -825,20 +857,22 @@
                 load.start(j + 2)
 
         w = load.wait(j)
-        proj[...] = dot_nn(n[...], w[...])
         if s >= 2:
             for copy in stores[-4:-2]:
                 copy.wait()
             del stores[-4:-2]
-
-        def silu(at):
-            u = proj[at, :]
+        for c in column_steps(act.shape[2]):
+            u = dot_nn(n[...], w[:, c])
             sig = lax.logistic(u)
-            act[s % 2, at, :] = (u * sig).astype(BF16)
-            slope[s % 2, at, :] = (sig * (1.0 + u * (1.0 - sig))).astype(BF16)
-
-        row_loop(rows, 32, silu)
+            act[s % 2, :, c] = (u * sig).astype(BF16)
+            slope[s % 2, :, c] = (sig * (1.0 + u * (1.0 - sig))).astype(BF16)
         tick(*((1,) if s == 0 else (0, 1)))
+
+        @pl.when(first)
+        def _():
+            if s == n_t - 1:
+                until(0, 2, s)
+                load.start(j + 1)
 
         @pl.when(second)
         def _():
@@ -847,30 +881,29 @@
                 load.start(j + 3)
 
         w = load.wait(j + 1)
-        acc[...] = acc[...] + dot_nn(act[s % 2], w[...])
+        if s < n_t - 1:
+            acc[...] = acc[...] + dot_nn(act[s % 2], w[...])
+        else:
+            for c in range(PARTS):
+                at = slice(c * rows // PARTS, (c + 1) * rows // PARTS)
+                outb[at, :] = (acc[at, :] + dot_nn(act[s % 2, at, :], w[...])).astype(BF16)
+
+                @pl.when(first)
+                def _():
+                    over_part(outb, x, y_send, y_recv, other, c).start()
+
         store(act.at[s % 2], act_out.at[s], s_sem.at[spare + 2 * (s % 2)])
         store(slope.at[s % 2], slope_out.at[s], s_sem.at[spare + 2 * (s % 2) + 1])
 
-    def finish(at):
-        outb[at, :] = acc[at, :].astype(BF16)
-
-    row_loop(rows, 32, finish)
     assert all(len(h - {None}) == 3 * (n_t - 1) for h in here)
-    over = pltpu.make_async_remote_copy(
-        src_ref=outb, dst_ref=x, send_sem=y_send, recv_sem=y_recv, device_id=other, device_id_type=MESH
-    )
-
-    @pl.when(first)
-    def _():
-        over.start()
-
     store(outb, out, x_sem)
     for copy in stores:
         copy.wait()
 
     @pl.when(first)
     def _():
-        over.wait_send()
+        for c in range(PARTS):
+            over_part(outb, x, y_send, y_recv, other, c).wait_send()
         l.drain()
 
     @pl.when(second)
@@ -915,7 +948,7 @@
             pltpu.VMEM(tables[0].shape, F32),
             pltpu.VMEM(tables[1].shape, F32),
             dma((2,)),
-            dma((3,)), dma((6 + 2 * n_t,)), dma(()), dma(()), dma(()),
+            dma((3,)), dma((6 + 2 * n_t,)), dma((PARTS,)), dma((PARTS,)), dma(()),
             dma((count,)), dma((count,)), dma((count, n_dp)), dma((count, n_dp)),
             dma((3,)), dma((3,)), dma((3, n_t)), dma((3, n_t)),
             dma((3, n_t, n_dp)), dma((3, n_t, n_dp)), dma((3, n_t, n_dp)), dma((3, n_t, n_dp)),
@@ -949,9 +982,11 @@
     lax.fori_loop(0, 2, turn, 0)
 
 
-def norm_back_rows(g, dn, h, gain, gain_sum, normed, write):
-    gain_sum[...] = jnp.zeros_like(gain_sum)
+def norm_back_rows(g, dn, h, gain, gain_sum, normed, write, part=0, parts=1):
+    if part == 0:
+        gain_sum[...] = jnp.zeros_like(gain_sum)
     step = 32
+    count = h.shape[0] // step // parts
 
     def body(at):
         hr, dr = h[at, :].astype(F32), dn[at, :]
@@ -962,7 +997,11 @@
         gain_sum[...] += jnp.sum((dr * hr * r).reshape(step // 8, 8, -1), axis=0)
         write(at, g[at, :].astype(F32) + r * y - hr * (r * r * r) * jnp.mean(hr * y, axis=1, keepdims=True))
 
-    row_loop(h.shape[0], step, body)
+    def turn(r, _):
+        body(pl.ds(pl.multiple_of((part * count + r) * step, step), step))
+        return 0
+
+    lax.fori_loop(0, count, turn, 0)
 
 
 def backward_kernel(
@@ -997,20 +1036,24 @@
     load = Loader(wbuf, w_sem, [own[m] if j == n_t - 1 else full.at[m, slots[j]] for m, j in order])
 
     l.greet([{"tensor": l.up}, {"tensor": l.down}, other] + [{"dp": l.flip(b)} for b in l.bits])
-    spread1.start()
+    cot_copy = pltpu.make_async_copy(cot, gbuf, l_sem.at[4])
+
+    @pl.when(second)
+    def _():
+        cot_copy.start()
+
+    def local(src, dst, sem):
+        return pltpu.make_async_copy(src, dst, sem)
+
     load.start(0)
     load.start(1)
-
-    def local(src, dst, sem):
-        return pltpu.make_async_copy(src, dst, sem)
+    spread1.start()
 
     acts_in = local(out_in, dhb, l_sem.at[0])
     acts_out = local(dhb, layer_acts.at[l.z], l_sem.at[0])
     h2_copy = local(h2_in, h2, l_sem.at[1])
     x_copy = local(xs, x, l_sem.at[2])
     o_copies = [local(o_in.at[slots[j]], o.at[j], o_sem.at[j]) for j in range(n_t)]
-    for c in (acts_in, h2_copy, x_copy, *o_copies):
-        c.start()
 
     def act_copy(j):
         return local(act_in.at[slots[j]], act.at[j % 2], a_sem.at[j % 2])
@@ -1027,35 +1070,30 @@
     def qkv_copy(j):
         return local(qkv_in.at[slots[j]], qkv.at[j % 2], q_sem.at[j % 2])
 
+    slope_copy(0).start()
     act_copy(0).start()
-    slope_copy(0).start()
+    for c in (h2_copy, acts_in, x_copy, *o_copies):
+        c.start()
     tables = [local(t, to, c_sem.at[i]) for i, (t, to) in enumerate(((cos_in, cos), (sin_in, sin)))]
     for c in tables:
         c.start()
     write_mask(mask, seg_col, seg_row, obs_col)
-    h2_copy.wait()
 
     @pl.when(first)
     def _():
+        h2_copy.wait()
         norm_rows(h2, gains[1:2, :], n)
-
-    acts_in.wait()
-    acts_out.start()
-    arrival = pltpu.make_async_remote_copy(
-        src_ref=dhb, dst_ref=gbuf, send_sem=y_send, recv_sem=y_recv, device_id=other, device_id_type=MESH
-    )
-    cot_copy = local(cot, gbuf, l_sem.at[4])
 
     @pl.when(second)
     def _():
-        cot_copy.start()
         cot_copy.wait()
 
     @pl.when(first)
     def _():
         for k in range(1, n_t - 1):
             spread1.step(k)
-        arrival.wait_recv()
+        for c in range(PARTS):
+            over_part(dhb, gbuf, y_send, y_recv, other, c).wait_recv()
 
     def block_of(reducer, i):
         if i >= 3:
@@ -1068,24 +1106,24 @@
             if j + 1 >= 2:
                 du_out(j - 1).wait()
             slope_copy(j + 1).start()
+        act_copy(j).wait()
+
+        @pl.when(first)
+        def _():
+            outer_product(block_of(r, 2 * j), gbuf, act.at[j % 2])
+            r.pump()
+            r.push(2 * j)
+
         w = load.wait(2 * j)
-        proj[...] = dot_nt(gbuf[...], w[...])
+        slope_copy(j).wait()
+        for c in column_steps(act.shape[2]):
+            du[j % 2, :, c] = (dot_nt(gbuf[...], w[c, :]) * du[j % 2, :, c].astype(F32)).astype(BF16)
         load.start(2 * j + 2)
-        slope_copy(j).wait()
-
-        def scale(at):
-            du[j % 2, at, :] = (proj[at, :] * du[j % 2, at, :].astype(F32)).astype(BF16)
-
-        row_loop(rows, 32, scale)
         du_out(j).start()
-        act_copy(j).wait()
 
         @pl.when(first)
         def _():
             r.pump()
-            outer_product(block_of(r, 2 * j), gbuf, act.at[j % 2])
-            r.pump()
-            r.push(2 * j)
 
         w = load.wait(2 * j + 1)
         if j == 0:
@@ -1110,6 +1148,12 @@
         du_out(j).wait()
 
     qkv_copy(0).start()
+    acts_in.wait()
+    acts_out.start()
+
+    @pl.when(second)
+    def _():
+        h2_copy.wait()
 
     def write_middle(at, value):
         h2[at, :] = value
@@ -1145,10 +1189,10 @@
         def _():
             r.pump()
 
-        if j != 1:
+        if j in (0, 2):
             @pl.when(end_first)
             def _():
-                r.last_step((2, None, 3, 4)[j])
+                r.last_step(2 + j // 2)
 
         if j < 2:
             @pl.when(inner_first)
@@ -1160,14 +1204,12 @@
     def write_input(at, value):
         dhb[at, :] = value.astype(BF16)
 
-    norm_back_rows(h2, dn, x, gains[0:1, :], gain0, None, write_input)
-    over = pltpu.make_async_remote_copy(
-        src_ref=dhb, dst_ref=gbuf, send_sem=y_send, recv_sem=y_recv, device_id=other, device_id_type=MESH
-    )
-
-    @pl.when(second)
-    def _():
-        over.start()
+    for c in range(PARTS):
+        norm_back_rows(h2, dn, x, gains[0:1, :], gain0, None, write_input, c, PARTS)
+
+        @pl.when(second)
+        def _():
+            over_part(dhb, gbuf, y_send, y_recv, other, c).start()
 
     spread2.start()
     grads_out = local(dhb, grad_acts.at[l.z], l_sem.at[0])
@@ -1213,22 +1255,22 @@
 
     @pl.when(inner_first)
     def _():
-        for i in range(2, 5):
+        for i in range(2, 4):
             rm.last_step(i)
 
     @pl.when(second)
     def _():
-        for i in range(5):
+        for i in range(4):
             r2.last_step(i)
         for k in range(2, n_t - 1):
             spread1b.step(k)
 
-    for i in range(5, len(order)):
+    for i in range(4, len(order)):
         r.last_step(i)
-        if i == 5 or i == 7:
+        if i == 4 or i == 5:
             @pl.when(inner)
             def _():
-                spread2.step((i - 3) // 2)
+                spread2.step(i - 3)
         if i >= 6 and i - 6 < total.count:
             total.step(i - 6)
     for t in range(len(order) - 6, total.count):
@@ -1248,7 +1290,8 @@
 
     @pl.when(second)
     def _():
-        over.wait_send()
+        for c in range(PARTS):
+            over_part(dhb, gbuf, y_send, y_recv, other, c).wait_send()
 
     l.drain()
 
@@ -1283,7 +1326,7 @@
             buf(rows, wide), buf(n_t, rows, 3 * wide), buf(rows, d), buf(2 * QB, ROW, t=F32), buf(3, *a_own.shape),
             buf(*tables[0].shape, t=F32), buf(*tables[1].shape, t=F32),
             buf(8, d, t=F32), buf(8, d, t=F32), buf(2 * steps, 8, d, t=F32),
-            dma((2,)), dma((3,)), dma((5,)), dma((n_t,)), dma((2,)), dma((2,)), dma((2,)), dma((2,)), dma(()), dma(()),
+            dma((2,)), dma((3,)), dma((5,)), dma((n_t,)), dma((2,)), dma((2,)), dma((2,)), dma((2,)), dma((PARTS,)), dma((PARTS,)),
             dma((2, n_t)), dma((2, n_t)), dma((2, n_t)), dma((2, n_t)), dma((steps,)), dma((steps,)),
             *reduce_scratch(n_dp, n_t, count, piece, d),
         ],

time: 680 us -> 642 us (0.944)
  Pallas kernels: 642 us -> 602 us
    pallas_call x1, Pallas kernels: 441 us -> 421 us  [run_backward(): pl.pallas_call(functools.partial(backward_kernel, n_dp, n_t), out_shape=[...]
    pallas_call x1, Pallas kernels: 201 us -> 181 us  [run_forward(): pl.pallas_call(functools.partial(forward_kernel, n_dp, n_t), out_shape=[s...]
where the time goes in v6:
time: 642 us; the launch traced here: 632 us
  Pallas kernels  602 us (94%)
  local copies, waits for them, and re-layouts  25.3 us (4%)
    pallas_call x1, Pallas kernels, run_backward(): pl.pallas_call(functools.partial(backward_kernel, n_dp, n_t), out_shape=[...  421 us
    pallas_call x1, Pallas kernels, run_forward(): pl.pallas_call(functools.partial(forward_kernel, n_dp, n_t), out_shape=[s...  181 us

profile of v6, /device:TPU:0, one launch (start us, length us, event | category | flops | bytes accessed | tf_op | source)
XLA Modules:
  0.0 632.1 jit_solution(15131869460278418855)
XLA Ops:
  0.7 0.7 copy.31
  1.4 0.1 dynamic_slice.16
  1.4 0.0 copy-start.2
  1.4 0.7 copy.30
  2.1 0.1 dynamic_slice.17
  2.2 0.4 fusion.2
  2.6 0.9 copy.18.obs_col
  3.5 0.9 copy.17.seg_col
  4.3 0.1 tile.8
  4.5 1.5 copy.19.cos_in
  6.0 0.0 copy-done.2
  6.0 0.1 tile.20
  6.1 1.5 copy.20.sin_in
  7.6 0.0 copy-start
  7.6 0.0 copy-start.1
  7.6 3.5 constant_dynamic-slice_fusion
  11.1 0.0 copy-done
  11.1 0.0 copy-done.1
  11.1 2.0 pad_maximum_fusion
  13.1 180.8 %shard_map.144 = (bf16[3,4,1280,1280]{3,2,1,0:T(8,128)(2,1)}, bf16[512,1280]{1,0:T(8,128)(2,1)}, bf16[4,512,960]{2,1,0:T(8,128)(2,1)}, bf16[4,512,320]{2,1,0:T(8...) custom-call(bf16[1280,1280]{1,0:T(8,128)(2,1)} %bitcast.46, ...), custom_call_target="tpu_custom_call" | custom-call | tf_op jit(solution)/shard_map/pallas_call | solution.py:926
  194.0 421.1 %shard_map.145 = (bf16[4,512,1280]{2,1,0:T(8,128)(2,1)}, bf16[4,512,1280]{2,1,0:T(8,128)(2,1)}, f32[3,320,1280]{2,1,0:T(8,128)}, f32[8,1280]{1,0:T(8,128)}, bf16...) custom-call(bf16[1280,1280]{1,0:T(8,128)(2,1)} %bitcast.47, ...), custom_call_target="tpu_custom_call" | custom-call | tf_op jit(solution)/shard_map/pallas_call | solution.py:1315
  615.1 0.8 slice.31
  615.9 0.7 dynamic-slice_bitcast_fusion
  616.5 4.4 slice_bitcast_fusion
  620.9 0.3 slice_bitcast_fusion.2
  621.3 1.0 copy.25
  622.3 0.0 slice-start
  622.3 1.2 maximum_bitcast_fusion
  623.5 5.8 copy.34
  629.2 0.0 slice-done
  629.2 0.0 slice-done.1
  629.2 2.4 copy.35
  (4 shorter events, 0.0 us)
Async XLA Ops:
  1.4 4.5 copy-start.2
  7.6 3.5 copy-start
  7.6 3.5 copy-start.1
  622.3 7.0 %slice-start = ((s8[5242880]{0:T(1024)(128)(4,1)}), s8[4194304]{0:T(1024)(128)(4,1)S(1)}, s32[]{:S(2)}) async-start(s8[5242880]{0:T(1024)(128)(4,1)} %bitcast.52), calls=%async_computation | async-start | bytes 8388608
  623.5 5.8 slice-start.1

commit v7 on v6

--- a/solution.py
+++ b/solution.py
@@ -35,33 +35,47 @@
 
 
 def rope_tables():
-    freq = 10000.0 ** (-jnp.arange(HALF, dtype=F32) / HALF)
-    ang = jnp.arange(ROW, dtype=F32)[:, None] * freq[None, :]
-    cos, sin = jnp.cos(ang), jnp.sin(ang)
-    cos_full = jnp.tile(jnp.concatenate([cos, cos], axis=1), (1, GROUP))
-    sin_full = jnp.tile(jnp.concatenate([-sin, sin], axis=1), (1, GROUP))
-    return cos_full, sin_full
-
-
-def partner(x):
-    width = x.shape[1]
-    lane = lax.broadcasted_iota(jnp.int32, x.shape, 1)
-    first = lax.rem(lane, HEAD_SIZE) < HALF
-    return jnp.where(first, pltpu.roll(x, width - HALF, 1), pltpu.roll(x, HALF, 1))
+    freq = 10000.0 ** (-np.arange(HALF) / HALF)
+    ang = np.arange(ROW)[:, None] * freq[None, :]
+    cos, sin = np.cos(ang), np.sin(ang)
+    cos_full = np.tile(np.concatenate([cos, cos], axis=1), (1, GROUP))
+    sin_full = np.tile(np.concatenate([-sin, sin], axis=1), (1, GROUP))
+    return jnp.asarray(cos_full, F32), jnp.asarray(sin_full, F32)
+
+
+def write_halves(halves):
+    lane = lax.broadcasted_iota(jnp.int32, halves.shape, 1)
+    halves[...] = (lax.rem(lane, HEAD_SIZE) < HALF).astype(F32)
+
+
+def partner(x, halves):
+    return jnp.where(halves[0:1, :] > 0, pltpu.roll(x, x.shape[1] - HALF, 1), pltpu.roll(x, HALF, 1))
 
 
 def windows():
     return [max(i - 1, 0) * QB for i in range(ROW // QB)]
 
 
-def write_mask(mask, seg_col, seg_row, obs_col):
+def own_row(ref, z):
+    per = ref.shape[1] // ROW
+    at = pl.multiple_of(lax.rem(z, per) * ROW, ROW)
+    return ref[pl.ds(z // per, 1), pl.ds(at, ROW)].astype(F32)
+
+
+def column(row):
+    return jnp.transpose(jnp.broadcast_to(row, (128, ROW)))[:, 0:1]
+
+
+def write_mask(mask, seg_ids, observed, z):
+    seg_row = own_row(seg_ids, z)
+    seg_col, obs_col = column(seg_row), column(own_row(observed, z))
     for i, k0 in enumerate(windows()):
         keys, queries = slice(k0, k0 + 2 * QB), slice(i * QB, (i + 1) * QB)
         shape = (2 * QB, QB)
         kj = lax.broadcasted_iota(jnp.int32, shape, 0) + k0
         qi = lax.broadcasted_iota(jnp.int32, shape, 1) + i * QB
         same = seg_col[keys, :] == seg_row[:, queries]
-        seen = (obs_col[keys, :] == 1) | (kj == qi)
+        seen = (obs_col[keys, :] == 1.0) | (kj == qi)
         mask[:, queries] = (same & (kj <= qi) & seen).astype(F32)
 
 
@@ -695,16 +709,23 @@
     def __init__(self, buf, sem, blocks):
         self.buf, self.sem, self.blocks = buf, sem, blocks
 
-    def copy(self, j):
-        slot = j % self.buf.shape[0]
-        return pltpu.make_async_copy(self.blocks[j], self.buf.at[slot], self.sem.at[slot])
+    def copies(self, j):
+        slot, first, found = j % self.buf.shape[0], 0, []
+        block = self.blocks[j]
+        for n, ref in enumerate(block if isinstance(block, tuple) else (block,)):
+            to = self.buf.at[slot, pl.ds(first, ref.shape[0]), :]
+            found.append(pltpu.make_async_copy(ref, to, self.sem.at[n, slot]))
+            first += ref.shape[0]
+        return found
 
     def start(self, j):
         if j < len(self.blocks):
-            self.copy(j).start()
+            for c in self.copies(j):
+                c.start()
 
     def wait(self, j):
-        self.copy(j).wait()
+        for c in self.copies(j):
+            c.wait()
         return self.buf.at[j % self.buf.shape[0]]
 
 
@@ -721,17 +742,23 @@
 
 
 def forward_kernel(
-    n_dp, n_t, a_own, i_own, d_own, x0, gains, seg_col, seg_row, obs_col, cos_in, sin_in,
-    full, xs, qkv_out, o_out, h2_out, act_out, slope_out, out, held,
-    x, n, proj, qkv, o, h2, acc, act, slope, outb, mask, wbuf, cos, sin,
-    c_sem, w_sem, s_sem, y_send, y_recv, x_sem, z_send, z_recv, p_send, p_recv,
+    n_dp, n_t, q_own, o_own, i_own, d_own, x0, gains, seg_ids, observed, cos_in, sin_in,
+    full, xs, qkv_out, o_out, h2_out, act_out, slope_out, out, mask_out, held,
+    stack, x, n, proj, qkv, o, h2, acc, act, slope, outb, mask, wbuf, cos, sin, halves,
+    a_sem, c_sem, w_sem, s_sem, y_send, y_recv, x_sem, z_send, z_recv, p_send, p_recv,
     *lend_sems,
 ):
     l, l1 = Links(n_dp, n_t), Links(n_dp, n_t)
     section = lax.axis_index("section")
     first, second = section == 0, section != 0
-    own = (a_own, i_own, d_own)
-    _, parts0, parts1 = gather_parts(a_own.shape[0] // n_dp)
+    own = (stack, i_own, d_own)
+    _, parts0, parts1 = gather_parts(stack.shape[0] // n_dp)
+    stacked = [
+        pltpu.make_async_copy(ref, stack.at[pl.ds(at, ref.shape[0]), :], a_sem.at[n])
+        for n, (ref, at) in enumerate(((q_own, 0), (o_own, q_own.shape[0])))
+    ]
+    for c in stacked:
+        c.start()
     g0 = Gather(l, own, full, parts0, z_send, z_recv, p_send, p_recv)
     g1 = Gather(l1, own, full, parts1, z_send, z_recv, p_send, p_recv)
     lend0, lend1 = Lend(l, own, full, held, *lend_sems), Lend(l1, own, full, held, *lend_sems)
@@ -767,16 +794,20 @@
     tables = [pltpu.make_async_copy(t, to, c_sem.at[i]) for i, (t, to) in enumerate(((cos_in, cos), (sin_in, sin)))]
     for c in tables:
         c.start()
+    for c in stacked:
+        c.wait()
 
     @pl.when(first)
     def _():
         lend0.give()
         g0.start()
-        copy = pltpu.make_async_copy(x0, x, x_sem)
+        copy = pltpu.make_async_copy(own_block(x0, l.z, rows), x, x_sem)
         copy.start()
         copy.wait()
 
-    write_mask(mask, seg_col, seg_row, obs_col)
+    write_mask(mask, seg_ids, observed, l.z)
+    write_halves(halves)
+    store(mask, mask_out, c_sem.at[2])
     for c in tables:
         c.wait()
 
@@ -811,7 +842,7 @@
 
         def turn_rows(at):
             v = proj[at, 0:2 * wide]
-            qkv[s, at, 0:2 * wide] = (v * cos[at, :] + partner(v) * sin[at, :]).astype(BF16)
+            qkv[s, at, 0:2 * wide] = (v * cos[at, :] + partner(v, halves) * sin[at, :]).astype(BF16)
             qkv[s, at, 2 * wide:3 * wide] = proj[at, 2 * wide:3 * wide].astype(BF16)
 
         row_loop(rows, 32, turn_rows)
@@ -911,11 +942,12 @@
         l1.drain()
 
 
-def run_forward(a_own, i_own, d_own, x0, gains, seg, obs, tables):
+def run_forward(q_own, o_own, i_own, d_own, x0, gains, seg, obs, tables):
     n_dp, n_t = lax.axis_size("dp"), lax.axis_size("tensor")
-    rows, d = x0.shape
-    wide = a_own.shape[0] // 4
-    lent, parts, _ = gather_parts(a_own.shape[0] // n_dp)
+    wide, d = o_own.shape
+    rows = x0.shape[0] * x0.shape[1] // n_t
+    whole = (4 * wide, d)
+    lent, parts, _ = gather_parts(whole[0] // n_dp)
     count = 3 * (n_t - 1) * len(parts)
     dma = pltpu.SemaphoreType.DMA
     hbm, vmem = pl.BlockSpec(memory_space=pl.ANY), pl.BlockSpec(memory_space=pltpu.VMEM)
@@ -926,13 +958,14 @@
     return pl.pallas_call(
         functools.partial(forward_kernel, n_dp, n_t),
         out_shape=[
-            shape(3, n_t, *a_own.shape), shape(rows, d), shape(n_t, rows, 3 * wide), shape(n_t, rows, wide),
+            shape(3, n_t, *whole), shape(rows, d), shape(n_t, rows, 3 * wide), shape(n_t, rows, wide),
             shape(rows, d, t=F32), shape(n_t, rows, i_own.shape[1]), shape(n_t, rows, i_own.shape[1]), shape(rows, d),
-            shape(3, n_t, n_dp, lent, d),
+            shape(2 * QB, ROW, t=F32), shape(3, n_t, n_dp, lent, d),
         ],
-        in_specs=[hbm] * 4 + [vmem] * 4 + [hbm] * 2,
-        out_specs=[hbm] * 9,
+        in_specs=[hbm] * 5 + [vmem] * 3 + [hbm] * 2,
+        out_specs=[hbm] * 10,
         scratch_shapes=[
+            pltpu.VMEM(whole, BF16),
             pltpu.VMEM((rows, d), BF16),
             pltpu.VMEM((rows, d), BF16),
             pltpu.VMEM((rows, d), F32),
@@ -944,17 +977,17 @@
             pltpu.VMEM((2, rows, d), BF16),
             pltpu.VMEM((rows, d), BF16),
             pltpu.VMEM((2 * QB, ROW), F32),
-            pltpu.VMEM((3,) + a_own.shape, BF16),
+            pltpu.VMEM((3,) + whole, BF16),
             pltpu.VMEM(tables[0].shape, F32),
             pltpu.VMEM(tables[1].shape, F32),
-            dma((2,)),
-            dma((3,)), dma((6 + 2 * n_t,)), dma((PARTS,)), dma((PARTS,)), dma(()),
+            pltpu.VMEM((8, tables[0].shape[1]), F32),
+            dma((2,)), dma((3,)), dma((2, 3)), dma((6 + 2 * n_t,)), dma((PARTS,)), dma((PARTS,)), dma(()),
             dma((count,)), dma((count,)), dma((count, n_dp)), dma((count, n_dp)),
             dma((3,)), dma((3,)), dma((3, n_t)), dma((3, n_t)),
             dma((3, n_t, n_dp)), dma((3, n_t, n_dp)), dma((3, n_t, n_dp)), dma((3, n_t, n_dp)),
         ],
         compiler_params=pltpu.CompilerParams(collective_id=0, has_side_effects=True, vmem_limit_bytes=60 * 2**20),
-    )(a_own, i_own, d_own, x0, gains, seg[:, None], seg[None, :], obs[:, None], *tables)
+    )(q_own, o_own, i_own, d_own, x0, gains, seg, obs, *tables)
 
 
 def attend_slot_back(qkv, do, dqk, dcat, mask):
@@ -1005,10 +1038,10 @@
 
 
 def backward_kernel(
-    n_dp, n_t, a_own, i_own, d_own, full, cot, xs, qkv_in, o_in, h2_in, act_in, slope_in, out_in, gains,
-    seg_col, seg_row, obs_col, cos_in, sin_in,
+    n_dp, n_t, q_own, o_own, i_own, d_own, full, cot, xs, qkv_in, o_in, h2_in, act_in, slope_in, out_in, mask_in, gains,
+    cos_in, sin_in,
     layer_acts, grad_acts, out_sums, out_gains, hbm_sums, hbm_got, hbm_ring, du_hbm,
-    gbuf, act, du, n, h2, x, dn, ga, proj, qkv, o, do, dcat, dhb, mask, wbuf, cos, sin, gain0, gain1, gain_buf,
+    gbuf, act, du, n, h2, x, dn, ga, proj, qkv, o, do, dcat, dhb, mask, wbuf, cos, sin, halves, gain0, gain1, gain_buf,
     c_sem, w_sem, l_sem, o_sem, a_sem, u_sem, q_sem, st_sem, y_send, y_recv, s1_send, s1_recv, s2_send, s2_recv, t_send, t_recv,
     *reduce_refs,
 ):
@@ -1016,7 +1049,7 @@
     first, second = section == 0, section != 0
     other = {"section": 1 - section}
     l, l2, l3 = (Links(n_dp, n_t) for _ in range(3))
-    own = (a_own, i_own, d_own)
+    own = ((q_own, o_own), i_own, d_own)
     rows, d = h2.shape
     wide = do.shape[1]
     places = Places(l)
@@ -1036,7 +1069,7 @@
     load = Loader(wbuf, w_sem, [own[m] if j == n_t - 1 else full.at[m, slots[j]] for m, j in order])
 
     l.greet([{"tensor": l.up}, {"tensor": l.down}, other] + [{"dp": l.flip(b)} for b in l.bits])
-    cot_copy = pltpu.make_async_copy(cot, gbuf, l_sem.at[4])
+    cot_copy = pltpu.make_async_copy(own_block(cot, l.z, rows), gbuf, l_sem.at[4])
 
     @pl.when(second)
     def _():
@@ -1074,10 +1107,10 @@
     act_copy(0).start()
     for c in (h2_copy, acts_in, x_copy, *o_copies):
         c.start()
-    tables = [local(t, to, c_sem.at[i]) for i, (t, to) in enumerate(((cos_in, cos), (sin_in, sin)))]
+    tables = [local(t, to, c_sem.at[i]) for i, (t, to) in enumerate(((cos_in, cos), (sin_in, sin), (mask_in, mask)))]
     for c in tables:
         c.start()
-    write_mask(mask, seg_col, seg_row, obs_col)
+    write_halves(halves)
 
     @pl.when(first)
     def _():
@@ -1178,7 +1211,7 @@
 
         def turn_back(at):
             v = proj[at, 0:2 * wide]
-            dcat[j, at, 0:2 * wide] = (v * cos[at, :] - partner(v) * sin[at, :]).astype(BF16)
+            dcat[j, at, 0:2 * wide] = (v * cos[at, :] - partner(v, halves) * sin[at, :]).astype(BF16)
 
         row_loop(rows, 32, turn_back)
         if j == 0:
@@ -1296,10 +1329,10 @@
     l.drain()
 
 
-def run_backward(a_own, i_own, d_own, kept, cot, gains, seg, obs, tables):
+def run_backward(q_own, o_own, i_own, d_own, kept, cot, gains, tables):
     n_dp, n_t = lax.axis_size("dp"), lax.axis_size("tensor")
-    rows, d = cot.shape
-    wide = a_own.shape[0] // 4
+    wide, d = o_own.shape
+    rows = cot.shape[0] * cot.shape[1] // n_t
     piece = d // n_dp
     count = 3 * n_t
     steps = len(ring_bits(n_dp)) + n_t
@@ -1318,25 +1351,84 @@
             shape(n_t, rows, d), shape(n_t, rows, d), shape(3, piece, d, t=F32), shape(8, d, t=F32),
             *reduce_hbm(n_dp, n_t, count, piece, d), shape(n_t, rows, d),
         ],
-        in_specs=[hbm] * 12 + [vmem] * 4 + [hbm] * 2,
+        in_specs=[hbm] * 14 + [vmem] + [hbm] * 2,
         out_specs=[hbm] * 3 + [vmem] + [hbm] * 4,
         scratch_shapes=[
             buf(rows, d), buf(2, rows, d), buf(2, rows, d), buf(rows, d), buf(rows, d, t=F32), buf(rows, d),
             buf(rows, d, t=F32), buf(rows, d), buf(rows, d, t=F32), buf(2, rows, 3 * wide), buf(n_t, rows, wide),
-            buf(rows, wide), buf(n_t, rows, 3 * wide), buf(rows, d), buf(2 * QB, ROW, t=F32), buf(3, *a_own.shape),
-            buf(*tables[0].shape, t=F32), buf(*tables[1].shape, t=F32),
+            buf(rows, wide), buf(n_t, rows, 3 * wide), buf(rows, d), buf(2 * QB, ROW, t=F32), buf(3, 4 * wide, d),
+            buf(*tables[0].shape, t=F32), buf(*tables[1].shape, t=F32), buf(8, tables[0].shape[1], t=F32),
             buf(8, d, t=F32), buf(8, d, t=F32), buf(2 * steps, 8, d, t=F32),
-            dma((2,)), dma((3,)), dma((5,)), dma((n_t,)), dma((2,)), dma((2,)), dma((2,)), dma((2,)), dma((PARTS,)), dma((PARTS,)),
+            dma((3,)), dma((2, 3)), dma((5,)), dma((n_t,)), dma((2,)), dma((2,)), dma((2,)), dma((2,)), dma((PARTS,)), dma((PARTS,)),
             dma((2, n_t)), dma((2, n_t)), dma((2, n_t)), dma((2, n_t)), dma((steps,)), dma((steps,)),
             *reduce_scratch(n_dp, n_t, count, piece, d),
         ],
         compiler_params=pltpu.CompilerParams(collective_id=1, has_side_effects=True, vmem_limit_bytes=62 * 2**20),
-    )(a_own, i_own, d_own, kept[0], cot, *kept[1:], gains, seg[:, None], seg[None, :], obs[:, None], *tables)
-
-
-def own_rows(x, count):
-    flat = x.reshape((-1,) + x.shape[2:])
-    return lax.dynamic_slice_in_dim(flat, lax.axis_index("tensor") * count, count, 0)
+    )(q_own, o_own, i_own, d_own, kept[0], cot, *kept[1:], gains, *tables)
+
+
+def finish_kernel(n_dp, layer_in, grad_in, sums, gain, layer_out, grad_out, qkv, out, w_in, down, gain_out, rows, heads, wide, sem, heads_sem, wide_sem):
+    arrays = ((layer_in, layer_out), (grad_in, grad_out))
+    n = layer_in.shape[0]
+
+    def load(i):
+        return pltpu.make_async_copy(arrays[i // n][0].at[i % n], rows.at[i], sem.at[0, i])
+
+    def store(i):
+        return pltpu.make_async_copy(rows.at[i], arrays[i // n][1].at[i % n], sem.at[1, i])
+
+    heads_in = pltpu.make_async_copy(sums.at[0], heads, heads_sem)
+    wide_in = [pltpu.make_async_copy(sums.at[1 + m], wide.at[m], wide_sem.at[0, m]) for m in range(2)]
+    wide_out = [pltpu.make_async_copy(wide.at[m], to, wide_sem.at[1, m]) for m, to in enumerate((w_in, down))]
+    heads_in.start()
+    for c in wide_in:
+        c.start()
+    for i in range(2 * n):
+        load(i).start()
+    hd = out.shape[0]
+    me = lax.axis_index("dp")
+    for k in range(n_dp):
+        @pl.when(me == k)
+        def _():
+            gain_out[...] = gain[0:2, k * gain_out.shape[1]:(k + 1) * gain_out.shape[1]]
+
+    for c, o in zip(wide_in, wide_out):
+        c.wait()
+        o.start()
+    for i in range(2 * n):
+        load(i).wait()
+        store(i).start()
+    heads_in.wait()
+    for t in range(3):
+        qkv[t] = heads[:, t * hd:(t + 1) * hd]
+    out[...] = jnp.transpose(heads[:, 3 * hd:])
+    for o in wide_out:
+        o.wait()
+    for i in range(2 * n):
+        store(i).wait()
+
+
+def lay_out(layer_acts, grad_acts, sums, gain, n_dp):
+    n, rows, d = layer_acts.shape
+    piece, hd = sums.shape[1], sums.shape[2] // 4
+    hbm, vmem = pl.BlockSpec(memory_space=pl.ANY), pl.BlockSpec(memory_space=pltpu.VMEM)
+    dma = pltpu.SemaphoreType.DMA
+    acts = jax.ShapeDtypeStruct(layer_acts.shape, BF16)
+
+    def shape(*s):
+        return jax.ShapeDtypeStruct(s, F32)
+
+    return pl.pallas_call(
+        functools.partial(finish_kernel, n_dp),
+        out_shape=[acts, acts, shape(3, piece, hd), shape(hd, piece), shape(piece, d), shape(piece, d), shape(2, d // n_dp)],
+        in_specs=[hbm, hbm, hbm, vmem],
+        out_specs=[hbm, hbm, vmem, vmem, hbm, hbm, vmem],
+        scratch_shapes=[
+            pltpu.VMEM((2 * n, rows, d), BF16), pltpu.VMEM((piece, d), F32), pltpu.VMEM((2, piece, d), F32),
+            dma((2, 2 * n)), dma(()), dma((2, 2)),
+        ],
+        compiler_params=pltpu.CompilerParams(vmem_limit_bytes=62 * 2**20),
+    )(layer_acts, grad_acts, sums, gain)
 
 
 def on_device(tokens, cotangent, seg_ids, observed, w_qkv, w_out, w_in, w_down, norm_gains):
@@ -1344,21 +1436,16 @@
     w_qkv, w_out, w_in, w_down, gains = w_qkv[0], w_out[0], w_in[0], w_down[0], norm_gains[0]
     micro, rows, d = tokens.shape
     hd = w_out.shape[0]
-    count = micro * rows // n_t
     tables = rope_tables()
-    stack = jnp.concatenate([jnp.swapaxes(w_qkv, 1, 2), w_out[None]], axis=0).reshape(4 * hd, d)
-    seg, obs = own_rows(seg_ids, count), own_rows(observed, count)
-    kept = run_forward(stack, w_in, w_down, own_rows(tokens, count), gains, seg, obs, tables)[:8]
-    layer_acts, grad_acts, sums, gain = run_backward(stack, w_in, w_down, kept, own_rows(cotangent, count), gains, seg, obs, tables)[:4]
-    piece = d // n_dp
-    gain = lax.dynamic_slice_in_dim(gain[:2], lax.axis_index("dp") * piece, piece, 1)
-    r_attn, r_in, r_down = sums[0], sums[1], sums[2]
-    r_qkv = jnp.stack([r_attn[:, i * hd:(i + 1) * hd] for i in range(3)])
+    heads = jnp.swapaxes(w_qkv, 1, 2).reshape(3 * hd, d)
+    kept = run_forward(heads, w_out, w_in, w_down, tokens, gains, seg_ids, observed, tables)[:9]
+    layer_acts, grad_acts, sums, gain = run_backward(heads, w_out, w_in, w_down, kept, cotangent, gains, tables)[:4]
+    layer_acts, grad_acts, r_qkv, r_out, r_in, r_down, gain = lay_out(layer_acts, grad_acts, sums, gain, n_dp)
     return (
         layer_acts.reshape(1, micro, rows, d),
         grad_acts.reshape(1, micro, rows, d),
         r_qkv[None],
-        r_attn[:, 3 * hd:].T[None],
+        r_out[None],
         r_in[None],
         r_down.T[None],
         gain[None],

time: 642 us -> 624 us (0.972)
  local copies, waits for them, and re-layouts: 25.3 us -> 0 us
  Pallas kernels: 602 us -> 614 us
    pallas_call x0 -> x1, Pallas kernels: none -> 12.3 us  [lay_out(): pl.pallas_call(functools.partial(finish_kernel, n_dp), out_shape=[acts, a...]
    unnamed x15 -> x0, local copies, waits for them, and re-layouts: 10.5 us -> none
    broadcast_in_dim x5 -> x0, local copies, waits for them, and re-layouts: 7.13 us -> none  [the longest x1 4.44 us: on_device(): r_down.T[None]]
where the time goes in v7:
time: 624 us; the launch traced here: 615 us
  Pallas kernels  614 us (98%)
    pallas_call x1, Pallas kernels, run_backward(): pl.pallas_call(functools.partial(backward_kernel, n_dp, n_t), out_shape=[...  422 us
    pallas_call x1, Pallas kernels, run_forward(): pl.pallas_call(functools.partial(forward_kernel, n_dp, n_t), out_shape=[s...  180 us

profile of v7, /device:TPU:0, one launch (start us, length us, event | category | flops | bytes accessed | tf_op | source)
XLA Modules:
  0.0 615.2 jit_solution(17698166475749756460)
XLA Ops:
  0.6 180.0 %shard_map.162 = (bf16[3,4,1280,1280]{3,2,1,0:T(8,128)(2,1)}, bf16[512,1280]{1,0:T(8,128)(2,1)}, bf16[4,512,960]{2,1,0:T(8,128)(2,1)}, bf16[4,512,320]{2,1,0:T(8...) custom-call(bf16[960,1280]{1,0:T(8,128)(2,1)} %bitcast.22, ...), custom_call_target="tpu_custom_call" | custom-call | tf_op jit(solution)/shard_map/pallas_call | solution.py:958
  180.7 421.8 %shard_map.163 = (bf16[4,512,1280]{2,1,0:T(8,128)(2,1)}, bf16[4,512,1280]{2,1,0:T(8,128)(2,1)}, f32[3,320,1280]{2,1,0:T(8,128)}, f32[8,1280]{1,0:T(8,128)}, bf16...) custom-call(bf16[960,1280]{1,0:T(8,128)(2,1)} %bitcast.23, ...), custom_call_target="tpu_custom_call" | custom-call | tf_op jit(solution)/shard_map/pallas_call | solution.py:1348
  602.4 12.3 %shard_map.164 = (bf16[4,512,1280]{2,1,0:T(8,128)(2,1)}, bf16[4,512,1280]{2,1,0:T(8,128)(2,1)}, f32[3,320,320]{2,1,0:T(8,128)}, f32[320,320]{1,0:T(8,128)}, f32[...) custom-call(bf16[4,512,1280]{2,1,0:T(8,128)(2,1)} %get-tuple-element.36.layer_in, ...), custom_call_target="tpu_custom_call" | custom-call | tf_op jit(solution)/shard_map/pallas_call | solution.py:1421

commit v8 on v7

--- a/solution.py
+++ b/solution.py
@@ -367,16 +367,17 @@
 
 def add_rows(out, *terms):
     rows = out.shape[0]
+    step = 64 if rows % 64 == 0 else 16
 
     def body(r, _):
-        at = pl.ds(pl.multiple_of(r * 16, 16), 16)
+        at = pl.ds(pl.multiple_of(r * step, step), step)
         total = terms[0][at, :].astype(F32)
         for t in terms[1:]:
             total = total + t[at, :].astype(F32)
         out[at, :] = total.astype(out.dtype)
         return 0
 
-    lax.fori_loop(0, rows // 16, body, 0)
+    lax.fori_loop(0, rows // step, body, 0)
 
 
 def reduce_scratch(n_dp, n_t, count, rows, c):
@@ -689,7 +690,7 @@
         r = lax.rsqrt(jnp.mean(h * h, axis=1, keepdims=True) + EPS)
         out[at, :] = (h * r * gain).astype(BF16)
 
-    row_loop(source.shape[0], 32, body)
+    row_loop(source.shape[0], 64, body)
 
 
 def own_block(ref, z, rows):
@@ -845,7 +846,7 @@
             qkv[s, at, 0:2 * wide] = (v * cos[at, :] + partner(v, halves) * sin[at, :]).astype(BF16)
             qkv[s, at, 2 * wide:3 * wide] = proj[at, 2 * wide:3 * wide].astype(BF16)
 
-        row_loop(rows, 32, turn_rows)
+        row_loop(rows, 128, turn_rows)
         tick(0)
         attend_slot(qkv.at[s], o.at[s], mask)
         tick(0, 1)
@@ -864,7 +865,7 @@
         r = lax.rsqrt(jnp.mean(h * h, axis=1, keepdims=True) + EPS)
         n[at, :] = (h * r * gains[1:2, :]).astype(BF16)
 
-    row_loop(rows, 32, middle)
+    row_loop(rows, 64, middle)
     store(h2, h2_out, s_sem.at[1 + 2 * n_t])
     spare = 2 + 2 * n_t
     for s in range(n_t):
@@ -1018,7 +1019,7 @@
 def norm_back_rows(g, dn, h, gain, gain_sum, normed, write, part=0, parts=1):
     if part == 0:
         gain_sum[...] = jnp.zeros_like(gain_sum)
-    step = 32
+    step = 64
     count = h.shape[0] // step // parts
 
     def body(at):
@@ -1213,7 +1214,7 @@
             v = proj[at, 0:2 * wide]
             dcat[j, at, 0:2 * wide] = (v * cos[at, :] - partner(v, halves) * sin[at, :]).astype(BF16)
 
-        row_loop(rows, 32, turn_back)
+        row_loop(rows, 128, turn_back)
         if j == 0:
             dn[...] = dot_nn(dcat[j], w[0:3 * wide, :])
         else:

time: 624 us -> 621 us (level)
  no operation moved by 1% of the time
where the time goes in v8:
time: 621 us; the launch traced here: 611 us
  Pallas kernels  610 us (98%)
    pallas_call x1, Pallas kernels, run_backward(): pl.pallas_call(functools.partial(backward_kernel, n_dp, n_t), out_shape=[...  419 us
    pallas_call x1, Pallas kernels, run_forward(): pl.pallas_call(functools.partial(forward_kernel, n_dp, n_t), out_shape=[s...  179 us

profile of v8, /device:TPU:0, one launch (start us, length us, event | category | flops | bytes accessed | tf_op | source)
XLA Modules:
  0.0 611.0 jit_solution(3986173222757307320)
XLA Ops:
  0.6 178.9 %shard_map.162 = (bf16[3,4,1280,1280]{3,2,1,0:T(8,128)(2,1)}, bf16[512,1280]{1,0:T(8,128)(2,1)}, bf16[4,512,960]{2,1,0:T(8,128)(2,1)}, bf16[4,512,320]{2,1,0:T(8...) custom-call(bf16[960,1280]{1,0:T(8,128)(2,1)} %bitcast.22, ...), custom_call_target="tpu_custom_call" | custom-call | tf_op jit(solution)/shard_map/pallas_call | solution.py:959
  179.6 418.9 %shard_map.163 = (bf16[4,512,1280]{2,1,0:T(8,128)(2,1)}, bf16[4,512,1280]{2,1,0:T(8,128)(2,1)}, f32[3,320,1280]{2,1,0:T(8,128)}, f32[8,1280]{1,0:T(8,128)}, bf16...) custom-call(bf16[960,1280]{1,0:T(8,128)(2,1)} %bitcast.23, ...), custom_call_target="tpu_custom_call" | custom-call | tf_op jit(solution)/shard_map/pallas_call | solution.py:1349
  598.4 12.3 %shard_map.164 = (bf16[4,512,1280]{2,1,0:T(8,128)(2,1)}, bf16[4,512,1280]{2,1,0:T(8,128)(2,1)}, f32[3,320,320]{2,1,0:T(8,128)}, f32[320,320]{1,0:T(8,128)}, f32[...) custom-call(bf16[4,512,1280]{2,1,0:T(8,128)(2,1)} %get-tuple-element.36.layer_in, ...), custom_call_target="tpu_custom_call" | custom-call | tf_op jit(solution)/shard_map/pallas_call | solution.py:1422
